TPU v7x, 32 devices: a whole 2x2x4 slice. The times are simulated.
32 devices in a mesh: seq: 4 (over y, core), fsdp: 8 (over z, x).
Axes of the slice: x: 2, y: 2, z: 4, core: 2. Of those that a mesh axis runs over, the one named last changes fastest.
Arguments:
- tokens: bfloat16 [8, 1024, 1024], P('fsdp', 'seq'), may hold values from -6 to 6
- cotangent: bfloat16 [8, 1024, 1024], P('fsdp', 'seq'), may hold values from -6 to 6
- scene_lengths: int32 [8, 3], P('fsdp'), may hold values from 1 to 1022, as said below
- key_mask: int32 [8, 1024], P('fsdp'), may hold values 0 or 1
- project_in: bfloat16 [1024, 3072], P('fsdp'), may hold values from -0.1875 to 0.1875
- project_out: bfloat16 [1024, 1024], P('fsdp'), may hold values from -1.5 to 1.5
- up_weight: bfloat16 [1024, 4096], P('fsdp'), may hold values from -0.1875 to 0.1875
- down_weight: bfloat16 [4096, 1024], P('fsdp'), may hold values from -0.09375 to 0.09375
- in_gain: bfloat16 [1024], P('fsdp'), may hold values from 0.5 to 1.5
- in_shift: bfloat16 [1024], P('fsdp'), may hold values from -2 to 2
- out_shift: bfloat16 [1024], P('fsdp'), may hold values from -2 to 2
- mid_gain: bfloat16 [1024], P('fsdp'), may hold values from 0.5 to 1.5
- mid_shift: bfloat16 [1024], P('fsdp'), may hold values from -2 to 2
- up_shift: bfloat16 [4096], P('fsdp'), may hold values from -3 to 3
- down_shift: bfloat16 [1024], P('fsdp'), may hold values from -2 to 2
Outputs:
- result: bfloat16 [8, 1024, 1024], P('fsdp', 'seq')
- grad_tokens: bfloat16 [8, 1024, 1024], P('fsdp', 'seq')
- grad_project_in: float32 [1024, 3072], P('fsdp')
- grad_project_out: float32 [1024, 1024], P('fsdp')
- grad_up_weight: float32 [1024, 4096], P('fsdp')
- grad_down_weight: float32 [4096, 1024], P('fsdp')
- grad_in_gain: float32 [1024], P('fsdp')
- grad_in_shift: float32 [1024], P('fsdp')
- grad_out_shift: float32 [1024], P('fsdp')
- grad_mid_gain: float32 [1024], P('fsdp')
- grad_mid_shift: float32 [1024], P('fsdp')
- grad_up_shift: float32 [4096], P('fsdp')
- grad_down_shift: float32 [1024], P('fsdp')
Inputs may be any that keep to these rules, and one draw needn't show every extreme that they name: `scene_lengths`: A row sums to 1024; its second entry is the longest, the first and the third are at most 64 (the pieces of scenes cut at the group's ends), and in some row the first entry is 64.
All inputs are finite; a program needn't handle non-finite values. No bound on the sum of `key_mask` on one device may be relied on, other than what follows from the above.
Results may differ from a plain program's by a relative error of at most 0.03.
Values may be sent and summed in bfloat16 or wider, within the bound.
No kernel may reach another device: no remote copies, remote signals or barrier semaphores. Data moves between devices by JAX's collectives and lax.ppermute only.
A program may use at most 192 MiB of HBM per device.

v0:
```python
import functools
import math

import jax
import jax.numpy as jnp
from jax import lax
from jax.experimental import pallas as pl
from jax.experimental.pallas import tpu as pltpu
from jax.sharding import PartitionSpec as P


HEADS = 16
HEAD_DIM = 64
EPSILON = 1e-05
MASKED = -1e30
MIB = 1 << 20
F32 = jnp.float32
BF16 = jnp.bfloat16
LOG2E = math.log2(math.e)
HBM = pl.BlockSpec(memory_space=pl.ANY)
STEP = 1024


def ring_order(count):
    wide = max(count // 4, 1)
    tall = count // wide
    path = [(row, 0) for row in range(tall)]
    for row in reversed(range(tall)):
        columns = list(range(1, wide))
        if (tall - 1 - row) % 2:
            columns.reverse()
        path += [(row, column) for column in columns]
    return [row * wide + column for row, column in path]


def order_table(order):
    count = len(order)
    rows = []
    for device in range(count):
        spot = order.index(device)
        rows.append(
            [order[(spot + i) % count] for i in range(count)]
            + [(order.index(i) - spot) % count for i in range(count)]
            + [device]
        )
    return rows


def ring_steps(order):
    onward = list(zip(order, order[1:] + order[:1]))
    return onward, [(target, source) for source, target in onward]


def after(value, *others):
    return lax.optimization_barrier((value, *others))[0] if others else value


def ring_gather(block, order, cut, waits=()):
    onward, backward = ring_steps(order)
    count = len(order)
    half = count // 2
    parts = [(0, 0, block)]
    left = right = block
    waits = dict(enumerate(waits, 2))
    for step in range(1, half):
        if step in waits:
            left, right = lax.optimization_barrier((left, right, *waits[step]))[:2]
        left = lax.ppermute(left, "fsdp", onward)
        right = lax.ppermute(right, "fsdp", backward)
        parts += [(count - step, 0, left), (step, 0, right)]
    if half in waits:
        left, right = lax.optimization_barrier((left, right, *waits[half]))[:2]
    parts.append((half, 0, lax.ppermute(left[:cut], "fsdp", onward)))
    if cut < block.shape[0]:
        parts.append((half, cut, lax.ppermute(right[cut:], "fsdp", backward)))
    return parts


class RingSum:
    def __init__(self, scalars, pieces, order, cut):
        self.scalars, self.pieces = scalars, pieces
        self.onward, self.backward = ring_steps(order)
        self.count, self.step = len(order), 1
        far = [part[self.count // 2] for part in pieces]
        if len(far) == 2 and far[0].shape[0] == cut:
            self.left, self.right = far
        else:
            far = jnp.concatenate(far)
            self.left, self.right = far[:cut], far[cut:]
        self.send()

    def send(self):
        self.left = lax.ppermute(self.left, "fsdp", self.onward)
        if self.right is not None and self.right.shape[0]:
            self.right = lax.ppermute(self.right, "fsdp", self.backward)
        else:
            self.right = None

    def advance(self, *waits):
        if self.step == self.count // 2:
            return []
        left = after(self.left, *waits)
        near, far = self.count // 2 - self.step, self.count // 2 + self.step
        self.left, self.right = merge(self.scalars, self.pieces, near, far, left, self.right)
        sent = [self.left, self.right]
        self.send()
        self.step += 1
        return sent

    def finish(self):
        while self.step < self.count // 2:
            self.advance()
        return merge(self.scalars, self.pieces, 0, None, self.left, self.right)


def swap(value, axis, count, bit):
    return lax.ppermute(value, axis, [(i, i ^ bit) for i in range(count)])


def spread(block, count):
    parts = {0: block}
    bit = count // 2
    while bit:
        parts.update({place | bit: swap(part, "seq", count, bit) for place, part in parts.items()})
        bit //= 2
    return [parts[place] for place in range(count)]


def fold(kept, sent, count):
    addends, sends = [kept], [sent]
    bit = 1
    while True:
        addends.append(swap(sends[-1], "seq", count, bit))
        bit *= 2
        if bit == count:
            return addends, sends
        sends.append(sum(part[1::2].astype(F32) for part in addends).astype(BF16))
        addends = [part[0::2] for part in addends]


def run(kernel, outs, *, grid, scalars, specs, arrays, out_specs, scratch=(), flops=0, vmem=20, kept=None):
    return pl.pallas_call(
        kernel,
        out_shape=[jax.ShapeDtypeStruct(o.shape, o.dtype) for o in outs],
        grid_spec=pltpu.PrefetchScalarGridSpec(
            num_scalar_prefetch=1,
            grid=grid,
            in_specs=specs,
            out_specs=out_specs,
            scratch_shapes=list(scratch),
        ),
        input_output_aliases=kept or {},
        compiler_params=pltpu.CompilerParams(vmem_limit_bytes=vmem * MIB),
        cost_estimate=pl.CostEstimate(flops=0, bytes_accessed=1024, transcendentals=0),
    )(scalars, *arrays)


def shape(dims, dtype=BF16):
    return jax.ShapeDtypeStruct(dims, dtype)


def whole(dims):
    return pl.BlockSpec(dims, lambda *_: (0,) * len(dims))


def dot(left, right):
    return jnp.dot(left, right, preferred_element_type=F32)


def dot_nt(left, right):
    return lax.dot_general(left, right, (((1,), (1,)), ((), ())), preferred_element_type=F32)


def dot_tn(left, right):
    return lax.dot_general(left, right, (((0,), (0,)), ((), ())), preferred_element_type=F32)


def each(count, body):
    if count == 1:
        body(0)
    else:
        lax.fori_loop(0, count, lambda number, carry: (body(number), carry)[1], 0)


def blocks_of(total, rows):
    return min(total, 1024) // rows


def standard(values):
    center = values - jnp.mean(values, axis=-1, keepdims=True)
    spread_of = jnp.mean(center * center, axis=-1, keepdims=True)
    inverse = lax.rsqrt(spread_of + EPSILON)
    return center * inverse, inverse


def norm_pull(grad, gain, unit, inverse):
    slope = grad * gain
    first = jnp.mean(slope, axis=-1, keepdims=True)
    second = jnp.mean(slope * unit, axis=-1, keepdims=True)
    return inverse * (slope - first - unit * second)


def column_sum(values):
    return jnp.sum(values, axis=0, keepdims=True)


def landing(parts, refs, fields, places, sems):
    height = sum(part.shape[0] for distance, _, part in parts if distance == 0)
    copies = []
    for (distance, start, part), ref in zip(parts, refs):
        for (low, high), columns, target in fields:
            high = high or height
            begin, end = max(low, start), min(high, start + part.shape[0])
            if begin >= end:
                continue
            offset = places[distance] * (high - low) + (begin - low)
            source = ref.at[pl.ds(begin - start, end - begin)]
            if columns is not None:
                source = ref.at[pl.ds(begin - start, end - begin), pl.ds(*columns)]
            target = target.at[pl.ds(pl.multiple_of(offset, 16), end - begin)]
            copies.append(pltpu.make_async_copy(source, target, sems.at[len(copies)]))
    return copies


def landings(parts, fields):
    return len(parts) * fields


def wait_all(copies):
    for copy in copies:
        copy.start()
    for copy in copies:
        copy.wait()


def merge(scalars, pieces, near, far, left, right):
    heights = [part.shape[1] for part in pieces]
    height, width = sum(heights), pieces[0].shape[2]
    arrays, specs = [], []
    for distance in (near,) if far is None else (near, far):
        for part, rows in zip(pieces, heights):
            arrays.append(part)
            specs.append(pl.BlockSpec((1, rows, width), lambda i, _, d=distance: (d, 0, 0)))
    sums = [part for part in (left, right) if part is not None]

    def kernel(_, *refs):
        held = refs[: len(arrays)]
        sums_refs = list(refs[len(arrays) : len(arrays) + len(sums)])
        outs = refs[len(arrays) + len(sums) :]
        first = left.shape[0]
        for side, out in enumerate(outs):
            start = 0
            for ref, rows in zip(held[side * len(pieces) :], heights):
                own = ref[0].astype(F32)
                span = slice(start, start + rows)
                if far is None:
                    for part in sums_refs:
                        own = own + part[span, :].astype(F32)
                    out[span, :] = own.astype(BF16)
                elif side < len(sums) and sums[side].shape[0] == height:
                    out[span, :] = (own + sums_refs[side][span, :].astype(F32)).astype(BF16)
                else:
                    out[span, :] = own.astype(BF16)
                start += rows
            if far is not None and side < len(sums) and sums[side].shape[0] < height:
                base = 0 if side == 0 else first
                rows = sums[side].shape[0]
                span = slice(base, base + rows)
                total = out[span, :].astype(F32) + sums_refs[side][...].astype(F32)
                out[span, :] = total.astype(BF16)

    whole_out = whole((height, width))
    count = 1 if far is None else 2
    outs = run(
        kernel,
        [shape((height, width))] * count,
        grid=(1,),
        scalars=scalars,
        specs=specs + [whole(part.shape) for part in sums],
        arrays=arrays + sums,
        out_specs=[whole_out] * count,
    )
    return outs[0] if far is None else outs


def select(scalars, arrays, starts, columns, fields=()):
    rows = arrays[0].shape[0]
    own = scalars.shape[0] - 1
    width = len(starts) * columns
    height = rows + (16 if fields else 0)
    if columns % 128:
        pick = lambda array, start, size: lax.dynamic_slice_in_dim(
            array, (start + scalars[own]) * size, size, 1
        )
        parts = [pick(array, start, columns) for array, start in zip(arrays, starts)]
        parts = jnp.concatenate(parts, axis=1)
        if not fields:
            return parts
        line = lax.dynamic_slice_in_dim(fields[-1], scalars[own], 1, 0)
        below = jnp.concatenate([*fields[:-1], line], axis=1)
        below = jnp.pad(below, ((0, 0), (0, 16 * width - below.shape[1])))
        return jnp.concatenate([parts, below.reshape(16, width)])

    def kernel(_, *refs):
        held = refs[: len(arrays) + len(fields)]
        out, sems, *lines = refs[len(held) :]
        mine = lax.axis_index("seq")
        copies = []
        for number, (ref, start) in enumerate(zip(held, starts)):
            begin = pl.multiple_of((start + mine) * columns, 128)
            target = out.at[pl.ds(0, rows), pl.ds(number * columns, columns)]
            copies.append((ref.at[:, pl.ds(begin, columns)], target))
        for number, ref in enumerate(held[len(arrays) :]):
            copies.append((ref, lines[number]))
        wait_all(
            [
                pltpu.make_async_copy(source, target, sems.at[number])
                for number, (source, target) in enumerate(copies)
            ]
        )
        if not fields:
            return
        size = lines[0].shape[1]
        per = width // size
        row = lax.broadcasted_iota(jnp.int32, (16, size), 0)
        values = [line[...].astype(F32) for line in lines]
        chosen = lax.broadcasted_iota(jnp.int32, values[-1].shape, 0) == mine
        values[-1] = column_sum(jnp.where(chosen, values[-1], 0.0))
        for start in range(per):
            value = jnp.zeros(row.shape, F32)
            for number in range(start, len(lines), per):
                value = jnp.where(row == number // per, values[number], value)
            out[rows:, start * size : (start + 1) * size] = value.astype(BF16)

    return run(
        kernel,
        [shape((height, width))],
        grid=(1,),
        scalars=jnp.zeros((1,), jnp.int32),
        specs=[pl.BlockSpec(memory_space=pltpu.HBM)] * (len(arrays) + len(fields)),
        arrays=[*arrays, *fields],
        out_specs=[whole((height, width))],
        scratch=[pltpu.SemaphoreType.DMA((len(arrays) + len(fields),))]
        + [pltpu.VMEM(field.shape, BF16) for field in fields],
        vmem=60 if fields else 20,
    )[0]


def tables(scalars, lengths, key_mask, along):
    total = key_mask.shape[1]
    rows = total // along
    scenes = lengths.shape[1]
    own = scalars.shape[0] - 1

    def kernel(places, lengths_ref, mask_ref, query_table, key_table):
        row = lax.broadcasted_iota(jnp.int32, (HEAD_DIM, rows), 0)
        for number in range(along):
            start = pl.multiple_of((places[own] ^ number) * rows, 128)
            spot = start + lax.broadcasted_iota(jnp.int32, (1, rows), 1)
            keep = mask_ref[:, pl.ds(start, rows)] == 1
            keep = jnp.where(keep, 1.0, 0.0)
            scene = jnp.zeros((1, rows), jnp.int32)
            edge = 0
            for part in range(scenes):
                keep = jnp.where(spot == edge, 1.0, keep)
                edge = edge + lengths_ref[0, part]
                scene = scene + jnp.where(spot >= edge, 1, 0)
            same = jnp.where(row == scene, 1.0, 0.0)
            keys = jnp.where(same * keep > 0.5, 0.0, MASKED)
            keys = jnp.where(row < scenes, keys, jnp.where(row < scenes + 3, -1.0, 0.0))
            span = slice(number * rows, (number + 1) * rows)
            query_table[span, :] = same.T.astype(BF16)
            key_table[span, :] = keys.T.astype(BF16)

    return run(
        kernel,
        [shape((total, HEAD_DIM))] * 2,
        grid=(1,),
        scalars=scalars,
        specs=[pl.BlockSpec(memory_space=pltpu.SMEM), whole(key_mask.shape)],
        arrays=[lengths, key_mask],
        out_specs=[whole((total, HEAD_DIM))] * 2,
    )


def standardize(scalars, tokens):
    rows, width = tokens[0].shape
    total = rows * len(tokens)

    def kernel(_, *refs):
        parts, (unit, joined) = refs[: len(tokens)], refs[len(tokens) :]
        for number, part in enumerate(parts):
            span = slice(number * rows, (number + 1) * rows)
            joined[span, :] = part[...]
            unit[span, :], _ = standard(part[...].astype(F32))

    return run(
        kernel,
        [shape((total, width), F32), shape((total, width))],
        grid=(1,),
        scalars=scalars,
        specs=[whole((rows, width))] * len(tokens),
        arrays=tokens,
        out_specs=[whole((total, width))] * 2,
    )


def field_at(number, strip, columns):
    per = columns // strip
    return number // per, number % per * strip


def project(scalars, unit, parts, rows, strip, unit_strip):
    total, width = unit.shape
    columns = parts[0][2].shape[1]
    share = columns // 4
    groups = width // strip
    count = landings(parts, 3)
    blocks = blocks_of(total, rows)

    def kernel(places, unit_ref, *refs):
        held = refs[: len(parts)]
        normed, query, keys, values, weight, out_weight, vectors, tail, extra, sems, *joint = refs[
            len(parts) :
        ]

        @pl.when(pl.program_id(0) == 0)
        def _():
            fields = [((strip, strip + 16), None, extra)]
            if joint:
                fields.append(((0, strip), None, joint[0]))
            else:
                fields.append(((0, strip), (0, 3 * share), weight))
                fields.append(((0, strip), (3 * share, share), out_weight))
            wait_all(landing(parts, held, fields, places, sems))
            if joint:
                weight[...] = joint[0][:, : 3 * share]
                out_weight[...] = joint[0][:, 3 * share :]
            for number in range(groups):
                block = extra[number * 16 : (number + 1) * 16, :].astype(F32)
                for field in range(7):
                    row, start = field_at(field, strip, columns)
                    part = block[row : row + 1, start : start + strip]
                    vectors[field : field + 1, number * strip : (number + 1) * strip] = part
                tail[:, number * unit_strip : (number + 1) * unit_strip] = part[:, :unit_strip]

        def block(number):
            span = pl.ds(pl.multiple_of(number * rows, rows), rows)
            part = (unit_ref[span, :] * vectors[0:1, :] + vectors[1:2, :]).astype(BF16)
            normed[span, :] = part
            mixed = dot(part, weight[...]).astype(BF16)
            query[span, :] = mixed[:, :share]
            keys[span, :] = mixed[:, share : 2 * share]
            values[span, :] = mixed[:, 2 * share :]

        each(blocks, block)

    by_rows = lambda w: pl.BlockSpec((rows * blocks, w), lambda i, _: (i, 0))
    return run(
        kernel,
        [shape((total, width))]
        + [shape((total, share))] * 3
        + [shape((width, 3 * share)), shape((width, share))]
        + [shape((8, width), F32), shape((1, groups * unit_strip), F32)],
        grid=(total // rows // blocks,),
        scalars=scalars,
        specs=[by_rows(width)] + [HBM] * len(parts),
        arrays=[unit] + [part for _, _, part in parts],
        out_specs=[by_rows(width)]
        + [by_rows(share)] * 3
        + [whole((width, 3 * share)), whole((width, share))]
        + [whole((8, width)), whole((1, groups * unit_strip))],
        scratch=[pltpu.VMEM((groups * 16, columns), BF16), pltpu.SemaphoreType.DMA((count,))]
        + [pltpu.VMEM((width, columns), BF16)] * (share % 128 > 0),
        flops=2 * total * width * 3 * share,
    )


def split_three(values):
    high = values.astype(BF16)
    rest = values - high.astype(F32)
    middle = rest.astype(BF16)
    return high, middle, (rest - middle.astype(F32)).astype(BF16)


def head_pairs(share):
    wide = min(share, 2 * HEAD_DIM)
    return share // wide, wide


def attend(scalars, query, keys, values, query_mask, key_mask, pair, before=()):
    total, share = query.shape
    wide = head_pairs(share)[1]
    rows = min(total, 256 * STEP // total)
    heads = wide // HEAD_DIM
    scale = HEAD_DIM**-0.5

    def kernel(_, q_ref, k_ref, v_ref, qm_ref, km_ref, *refs):
        attended, extra, k_held, v_held = refs[len(before) :]
        ones = jnp.ones((total, HEAD_DIM), BF16)
        place = lax.broadcasted_iota(jnp.int32, (rows, HEAD_DIM), 1)
        for head in range(heads):
            lanes = slice(head * HEAD_DIM, (head + 1) * HEAD_DIM)
            k_held[head] = jnp.concatenate([k_ref[:, lanes], km_ref[...]], axis=1)
            v_held[head] = jnp.concatenate([v_ref[:, lanes], ones], axis=1)

        def block(number):
            span = pl.ds(pl.multiple_of(number * rows, rows), rows)
            mask = qm_ref[span, :]
            outs, extras = [], []
            for head in range(heads):
                lanes = slice(head * HEAD_DIM, (head + 1) * HEAD_DIM)
                q = jnp.concatenate([q_ref[span, lanes], mask], axis=1)
                scores = dot_nt(q, k_held[head])
                top = jnp.max(scores, axis=1, keepdims=True)
                weights = jnp.exp2((scores - top) * (LOG2E * scale)).astype(BF16)
                summed = dot(weights, v_held[head])
                amount = summed[:, HEAD_DIM : HEAD_DIM + 1]
                outs.append(summed[:, :HEAD_DIM] / amount)
                high, middle, low = split_three(top + jnp.log(amount) / scale)
                tail = jnp.where(place == 4, middle, jnp.where(place == 5, low, mask))
                extras.append(jnp.where(place == 3, high, tail))
            attended[span, :] = jnp.concatenate(outs, axis=1).astype(BF16)
            extra[span, :] = jnp.concatenate(extras, axis=1)

        each(total // rows, block)

    fixed = pl.BlockSpec((total, wide), lambda i, _: (0, pair))
    table = whole((total, HEAD_DIM))
    return run(
        kernel,
        [shape((total, share))] * 2,
        grid=(1,),
        scalars=scalars,
        specs=[fixed, fixed, fixed, table, table] + [HBM] * len(before),
        arrays=[query, keys, values, query_mask, key_mask, *before],
        out_specs=[fixed, fixed],
        scratch=[pltpu.VMEM((heads, total, 2 * HEAD_DIM), BF16)] * 2,
        kept={6 + number: number for number in range(len(before))},
        flops=4 * 4 * total * total * wide,
    )


def column_copies(places, refs, target, sems, rows):
    own = places.shape[0] - 1
    if len(refs) == 1:
        return [pltpu.make_async_copy(refs[0].at[rows], target, sems.at[0])]
    columns = refs[0].shape[1]
    return [
        pltpu.make_async_copy(
            ref.at[rows],
            target.at[:, pl.ds(pl.multiple_of((places[own] ^ place) * columns, 128), columns)],
            sems.at[place],
        )
        for place, ref in enumerate(refs)
    ]


def attend_out(scalars, attended, tokens, vectors, outs, rows):
    places_along = len(attended)
    total, width = tokens.shape
    share = attended[0].shape[1]
    own = scalars.shape[0] - 1

    def kernel(places, *refs):
        attended_refs, refs = refs[:places_along], refs[places_along:]
        tokens_ref, vectors_ref = refs[:2]
        held, (gathered, normed, middle_own, out_ref, sems) = (
            refs[2 : 2 + len(outs)],
            refs[2 + len(outs) :],
        )
        step = pl.program_id(0)

        @pl.when(step == 0)
        def _():
            wait_all(column_copies(places, held, out_ref, sems, pl.ds(0, width)))

        for place, ref in enumerate(attended_refs):
            gathered[:, place * share : (place + 1) * share] = ref[...]
        branch = vectors_ref[2:3, :]
        for place in range(places_along):
            start = pl.multiple_of((places[own] ^ place) * share, share)
            branch = branch + dot(attended_refs[place][...], out_ref[pl.ds(start, share), :])
        middle = tokens_ref[...].astype(F32) + branch

        @pl.when(step == 0)
        def _():
            middle_own[...] = middle

        unit, _ = standard(middle)
        normed[...] = (unit * vectors_ref[3:4, :] + vectors_ref[4:5, :]).astype(BF16)

    by_rows = pl.BlockSpec((rows, width), lambda i, _: (i, 0))
    part_of = lambda x: pl.BlockSpec((rows, share), lambda i, _: (i ^ x, 0))
    return run(
        kernel,
        [shape((total, width)), shape((total, width)), shape((rows, width), F32)],
        grid=(places_along,),
        scalars=scalars,
        specs=[part_of(x) for x in range(places_along)]
        + [by_rows, whole(vectors.shape)]
        + [HBM] * len(outs),
        arrays=[*attended, tokens, vectors, *outs],
        out_specs=[by_rows, by_rows, whole((rows, width))],
        scratch=[pltpu.VMEM((width, width), BF16), pltpu.SemaphoreType.DMA((len(outs),))],
        flops=2 * total * width * width,
    )


def feed(scalars, normed, cotangent, up_shift, rings, rows, strip):
    total, width = normed.shape
    units = up_shift.shape[1]
    steps, blocks = total // rows, blocks_of(total, rows)
    parts = [part for ring in rings for part in ring]
    signals = 2 * len(parts)

    def kernel(places, *refs):
        normed_ref, cot_ref, shift_ref = refs[:3]
        held = refs[3 : 3 + len(parts)]
        active, grad_hidden, kept, sent, grad_shift, down, up, sems = refs[3 + len(parts) :]
        step = pl.program_id(0)

        @pl.when(step == 0)
        def _():
            if len(rings) == 1:
                fields = [((0, strip), None, up), ((strip, None), None, down)]
                copies = landing(rings[0], held, fields, places, sems)
            else:
                first, second = held[: len(rings[0])], held[len(rings[0]) :]
                copies = landing(rings[0], first, [((0, None), None, up)], places, sems)
                left = sems.at[pl.ds(len(copies), signals - len(copies))]
                copies += landing(rings[1], second, [((0, None), None, down)], places, left)
            wait_all(copies)
            grad_shift[...] = jnp.zeros_like(grad_shift)

        def pair(number):
            for half, out in enumerate((kept, sent)):
                span = pl.ds(pl.multiple_of((2 * number + half) * rows, rows), rows)
                hidden = dot(normed_ref[span, :], up[...]) + shift_ref[...]
                share_of = 0.5 + 0.5 * lax.erf(hidden * (0.5**0.5))
                active[span, :] = (hidden * share_of).astype(BF16)
                slope = share_of + hidden * (
                    jnp.exp2(hidden * hidden * (-0.5 * LOG2E)) * ((2 * math.pi) ** -0.5)
                )
                grad = (slope * dot_nt(cot_ref[span, :], down[...])).astype(BF16)
                grad_hidden[span, :] = grad
                grad_shift[...] += column_sum(grad.astype(F32))
                out[step * (blocks // 2) + number] = dot_nt(grad, up[...]).astype(BF16)

        each(blocks // 2, pair)

    by_rows = lambda w: pl.BlockSpec((rows * blocks, w), lambda i, _: (i, 0))
    halves = (steps // 2, rows, width)
    return run(
        kernel,
        [
            shape((total, units)),
            shape((total, units)),
            shape(halves),
            shape(halves),
            shape((1, units), F32),
            shape((units, width)),
        ],
        grid=(steps // blocks,),
        scalars=scalars,
        specs=[by_rows(width), by_rows(width), whole(up_shift.shape)] + [HBM] * len(parts),
        arrays=[normed, cotangent, up_shift] + [part for _, _, part in parts],
        out_specs=[
            by_rows(units),
            by_rows(units),
            whole(halves),
            whole(halves),
            whole((1, units)),
            whole((units, width)),
        ],
        scratch=[pltpu.VMEM((width, units), BF16), pltpu.SemaphoreType.DMA((signals,))],
        flops=6 * total * width * units,
        vmem=32,
    )


def descend(scalars, active, down, rows):
    total, units = active.shape
    width = down.shape[1]

    blocks = blocks_of(total, rows)

    def kernel(_, active_ref, down_ref, kept, sent):
        def pair(number):
            for half, out in enumerate((kept, sent)):
                span = pl.ds(pl.multiple_of((2 * number + half) * rows, rows), rows)
                part = dot(active_ref[span, :], down_ref[...]).astype(BF16)
                out[pl.program_id(0) * (blocks // 2) + number] = part

        each(blocks // 2, pair)

    halves = (total // rows // 2, rows, width)
    return run(
        kernel,
        [shape(halves)] * 2,
        grid=(total // rows // blocks,),
        scalars=scalars,
        specs=[pl.BlockSpec((rows * blocks, units), lambda i, _: (i, 0)), whole(down.shape)],
        arrays=[active, down],
        out_specs=[whole(halves)] * 2,
        flops=2 * total * units * width,
    )


def outer(scalars, left, right, count):
    total, height = left.shape
    width = right.shape[1]
    rows = min(height, 256)
    piece = height // count

    def kernel(places, left_ref, right_ref, out):
        def block(number):
            start = pl.multiple_of(number * rows, rows)
            product = dot_tn(left_ref[:, pl.ds(start, rows)], right_ref[...]).astype(BF16)
            for part in range(rows // piece):
                target = places[count + number * (rows // piece) + part]
                out[target] = product[part * piece : (part + 1) * piece]

        each(height // rows, block)

    return run(
        kernel,
        [shape((count, piece, width))],
        grid=(1,),
        scalars=scalars,
        specs=[whole(left.shape), whole(right.shape)],
        arrays=[left, right],
        out_specs=[whole((count, piece, width))],
        flops=2 * total * height * width,
    )[0]


def middle_back(scalars, addends, middle, cotangent, vectors):
    rows, width = middle.shape
    block = min(rows, 128)

    def kernel(_, *refs):
        parts = refs[: len(addends)]
        middle_ref, cot_ref, vectors_ref, grad_middle, grad_branch, sums = refs[len(addends) :]
        grad = sum(part[0].astype(F32) for part in parts)
        cot = cot_ref[...].astype(F32)
        unit, inverse = standard(middle_ref[...])
        total = cot + norm_pull(grad, vectors_ref[3:4, :], unit, inverse)
        grad_middle[...] = total
        branch = total.astype(BF16)
        grad_branch[...] = branch

        @pl.when(pl.program_id(0) == 0)
        def _():
            sums[...] = jnp.zeros_like(sums)

        sums[0:1, :] += column_sum(branch.astype(F32))
        sums[1:2, :] += column_sum(grad * unit)
        sums[2:3, :] += column_sum(grad)
        sums[3:4, :] += column_sum(cot)

    by_rows = pl.BlockSpec((block, width), lambda i, _: (i, 0))
    return run(
        kernel,
        [shape((rows, width), F32), shape((rows, width)), shape((8, width), F32)],
        grid=(rows // block,),
        scalars=scalars,
        specs=[pl.BlockSpec((1, block, width), lambda i, _: (0, i, 0))] * len(addends)
        + [by_rows, by_rows, whole(vectors.shape)],
        arrays=[*addends, middle, cotangent, vectors],
        out_specs=[by_rows, by_rows, whole((8, width))],
    )


def attended_back(scalars, branches, outs, attended):
    count = len(branches)
    total, share = attended.shape
    rows, width = branches[0].shape
    own = scalars.shape[0] - 1

    def kernel(places, *refs):
        parts, held = refs[:count], refs[count : count + len(outs)]
        attended_ref, grads, extras, out_ref, sems = refs[count + len(outs) :]
        start = pl.multiple_of(places[own] * share, 16)
        wait_all(column_copies(places, held, out_ref, sems, pl.ds(start, share)))
        line = lax.broadcasted_iota(jnp.int32, (share, share), 0) // HEAD_DIM
        lane = lax.broadcasted_iota(jnp.int32, (share, share), 1) // HEAD_DIM
        over_head = jnp.where(line == lane, 1.0, 0.0).astype(BF16)
        place = lax.broadcasted_iota(jnp.int32, (rows, share), 1) % HEAD_DIM
        for number, part in enumerate(parts):
            span = slice(number * rows, (number + 1) * rows)
            grad = dot_nt(part[...], out_ref[...]).astype(BF16)
            grads[span, :] = grad
            product = grad.astype(F32) * attended_ref[span, :].astype(F32)
            delta = sum(dot(piece, over_head) for piece in split_three(product))
            high, middle, low = (piece.astype(F32) for piece in split_three(delta))
            extra = jnp.where(place == 4, middle, jnp.where(place == 5, low, 0.0))
            extras[span, :] = jnp.where(place == 3, high, extra).astype(BF16)

    return run(
        kernel,
        [shape((total, share))] * 2,
        grid=(1,),
        scalars=scalars,
        specs=[whole((rows, width))] * count
        + [HBM] * len(outs)
        + [whole((total, share))],
        arrays=[*branches, *outs, attended],
        out_specs=[whole((total, share))] * 2,
        scratch=[pltpu.VMEM((share, width), BF16), pltpu.SemaphoreType.DMA((len(outs),))],
        flops=2 * total * width * share,
    )


def attend_back(scalars, query, extra, keys, key_mask, values, grads, grad_extra, pair, before=()):
    total, share = query.shape
    wide = head_pairs(share)[1]
    rows = min(total, 256 * STEP // total)
    heads = wide // HEAD_DIM
    scale = HEAD_DIM**-0.5

    def kernel(_, q_ref, qx_ref, k_ref, km_ref, v_ref, g_ref, gx_ref, *refs):
        dq_ref, dk_ref, dv_ref, held, q_held, g_held = refs[len(before) :]
        held[...] = jnp.zeros_like(held)
        for head in range(heads):
            lanes = slice(head * HEAD_DIM, (head + 1) * HEAD_DIM)
            q_held[head] = jnp.concatenate([q_ref[:, lanes], qx_ref[:, lanes]], axis=1)
            g_held[head] = jnp.concatenate([g_ref[:, lanes], gx_ref[:, lanes]], axis=1)

        def block(number):
            span = pl.ds(pl.multiple_of(number * rows, rows), rows)
            mask = km_ref[span, :]
            grad_keys, grad_values = [], []
            for head in range(heads):
                lanes = slice(head * HEAD_DIM, (head + 1) * HEAD_DIM)
                key_part = k_ref[span, lanes]
                k = jnp.concatenate([key_part, mask], axis=1)
                v = jnp.concatenate([v_ref[span, lanes], jnp.maximum(mask, -1.0)], axis=1)
                shares = jnp.exp2(dot_nt(k, q_held[head]) * (LOG2E * scale))
                grad_scores = (shares * dot_nt(v, g_held[head])).astype(BF16)
                grad_values.append(dot(shares.astype(BF16), g_ref[:, lanes]))
                grad_keys.append(dot(grad_scores, q_ref[:, lanes]) * scale)
                held[lanes, :] += dot_tn(key_part, grad_scores) * scale
            dk_ref[span, :] = jnp.concatenate(grad_keys, axis=1).astype(BF16)
            dv_ref[span, :] = jnp.concatenate(grad_values, axis=1).astype(BF16)

        each(total // rows, block)
        dq_ref[...] = held[...].T.astype(BF16)

    fixed = pl.BlockSpec((total, wide), lambda i, _: (0, pair))
    return run(
        kernel,
        [shape((total, share))] * 3,
        grid=(1,),
        scalars=scalars,
        specs=[fixed, fixed, fixed, whole((total, HEAD_DIM)), fixed, fixed, fixed]
        + [HBM] * len(before),
        arrays=[query, extra, keys, key_mask, values, grads, grad_extra, *before],
        out_specs=[fixed, fixed, fixed],
        scratch=[pltpu.VMEM((wide, total), F32)]
        + [pltpu.VMEM((heads, total, 2 * HEAD_DIM), BF16)] * 2,
        kept={8 + number: number for number in range(len(before))},
        flops=10 * 4 * total * total * wide,
    )


def projection_grads(
    scalars, normed, mixed, gathered, branches, weight, vectors, middle_sums, up_sums, count
):
    total, width = normed.shape
    share = mixed[0].shape[1]
    rows = max(min(width, 256 * STEP // total), 128)
    piece = width // count
    units = up_sums.shape[1] // count
    block_rows = branches[0].shape[0]
    own = scalars.shape[0] - 1
    per = share // piece
    column = pl.BlockSpec((block_rows, share), lambda i, w: (0, w[own]))
    if share % 128:
        column = whole((block_rows, share))
        branches = [
            lax.dynamic_slice_in_dim(part, scalars[own] * share, share, 1) for part in branches
        ]

    def to_row(values):
        if values.shape[1] % 128 == 0:
            values = sum(
                values[:, start : start + 128] for start in range(0, values.shape[1], 128)
            )
        return jnp.sum(values.T, axis=0, keepdims=True)

    def kernel(places, normed_ref, gathered_ref, weight_ref, vectors_ref, sums_ref, up_ref, *refs):
        mixed_refs, parts = refs[:3], refs[3 : 3 + len(branches)]
        out, totals, fields = refs[3 + len(branches) :]
        for place, ref in enumerate(mixed_refs):
            totals[place : place + 1, :] = column_sum(ref[...].astype(F32))
        for number in range(count):
            span = slice(number * piece, (number + 1) * piece)
            fields[number, 2:6, :] = sums_ref[0:4, span]
            fields[number, 6:7, :units] = up_ref[:, number * units : (number + 1) * units]

        def block(step):
            begin = pl.ds(pl.multiple_of(step * rows, 128), rows)
            left = normed_ref[:, begin]
            products, gain, shift = [], 0.0, 0.0
            for place, ref in enumerate(mixed_refs):
                product = dot_tn(left, ref[...])
                products.append(product.astype(BF16))
                part = weight_ref[begin, place * share : (place + 1) * share].astype(F32)
                gain = gain + to_row(product * part)
                shift = shift + to_row(part * totals[place : place + 1, :])
            gain = (gain - vectors_ref[1:2, begin] * shift) / vectors_ref[0:1, begin]
            branch = 0.0
            for number, part in enumerate(parts):
                held = gathered_ref[number * block_rows : (number + 1) * block_rows, begin]
                branch = branch + dot_tn(held, part[...])
            branch = branch.astype(BF16)
            for part in range(rows // piece):
                span = slice(part * piece, (part + 1) * piece)
                number = step * (rows // piece) + part
                target = places[count + number]
                for place, product in enumerate(products):
                    out[target, :piece, place * share : (place + 1) * share] = product[span]
                held = fields[number]
                entries = [gain[:, span], shift[:, span]] + [held[i : i + 1] for i in range(2, 7)]
                row = lax.broadcasted_iota(jnp.int32, (16, piece), 0)
                spots = [field_at(number, piece, 4 * share) for number in range(7)]
                for start in range(0, 4 * share, piece):
                    value = jnp.zeros((16, piece), F32)
                    for entry, (line, first) in zip(entries, spots):
                        if first == start:
                            value = jnp.where(row == line, entry, value)
                    out[target, piece:, start : start + piece] = value.astype(BF16)
                natural = ((number // per) ^ places[own]) * per + number % per
                out[places[count + natural], :piece, 3 * share :] = branch[span]

        each(width // rows, block)

    return run(
        kernel,
        [shape((count, piece + 16, 4 * share))],
        grid=(1,),
        scalars=scalars,
        specs=[whole((total, width))] * 2
        + [whole(weight.shape), whole(vectors.shape)]
        + [whole(middle_sums.shape), whole(up_sums.shape)]
        + [whole((total, share))] * 3
        + [column] * len(branches),
        arrays=[normed, gathered, weight, vectors, middle_sums, up_sums, *mixed, *branches],
        out_specs=[whole((count, piece + 16, 4 * share))],
        scratch=[pltpu.VMEM((8, share), F32), pltpu.VMEM((count, 8, piece), F32)],
        flops=2 * total * width * 4 * share,
        vmem=40 if total > STEP else 24,
    )[0]


def normed_back(scalars, mixed, weight, rows):
    total, share = mixed[0].shape
    width = weight.shape[0]

    blocks = blocks_of(total, rows)

    def kernel(_, q_ref, k_ref, v_ref, weight_ref, kept, sent):
        def pair(number):
            for half, out in enumerate((kept, sent)):
                span = pl.ds(pl.multiple_of((2 * number + half) * rows, rows), rows)
                grad = 0.0
                for place, ref in enumerate((q_ref, k_ref, v_ref)):
                    lanes = slice(place * share, (place + 1) * share)
                    grad = grad + dot_nt(ref[span, :], weight_ref[:, lanes])
                out[pl.program_id(0) * (blocks // 2) + number] = grad.astype(BF16)

        each(blocks // 2, pair)

    by_rows = pl.BlockSpec((rows * blocks, share), lambda i, _: (i, 0))
    halves = (total // rows // 2, rows, width)
    return run(
        kernel,
        [shape(halves), shape(halves)],
        grid=(total // rows // blocks,),
        scalars=scalars,
        specs=[by_rows] * 3 + [whole(weight.shape)],
        arrays=[*mixed, weight],
        out_specs=[whole(halves), whole(halves)],
        flops=2 * total * width * 3 * share,
    )


def tokens_back(scalars, addends, tokens, grad_middle, vectors):
    rows, width = tokens.shape
    block = min(rows, 128)

    def kernel(_, *refs):
        parts = refs[: len(addends)]
        tokens_ref, middle_ref, vectors_ref, out = refs[len(addends) :]
        grad = sum(part[0].astype(F32) for part in parts)
        unit, inverse = standard(tokens_ref[...].astype(F32))
        pulled = norm_pull(grad, vectors_ref[0:1, :], unit, inverse)
        out[...] = (middle_ref[...] + pulled).astype(BF16)

    by_rows = pl.BlockSpec((block, width), lambda i, _: (i, 0))
    return run(
        kernel,
        [shape((rows, width))],
        grid=(rows // block,),
        scalars=scalars,
        specs=[pl.BlockSpec((1, block, width), lambda i, _: (0, i, 0))] * len(addends)
        + [by_rows, by_rows, whole(vectors.shape)],
        arrays=[*addends, tokens, grad_middle, vectors],
        out_specs=[by_rows],
    )[0]


def place_attention(scalars, parts, strip, unit_strip):
    columns = parts[0].shape[1]
    share = columns // 4
    along = len(parts)
    own = scalars.shape[0] - 1

    def kernel(places, *refs):
        held, grad_in, grad_out, small, tail = refs[:along], *refs[along : along + 2], *refs[-2:]
        total = 0.0
        for number, ref in enumerate(held):
            spot = places[own] ^ number
            for place in range(4):
                part = ref[:strip, place * share : (place + 1) * share].astype(F32)
                target = grad_out if place == 3 else grad_in
                start = pl.multiple_of((place % 3 * along + spot) * share, 128)
                target[:, pl.ds(start, share)] = part
            extra = ref[strip:, :].astype(F32)
            total = total + extra
            row, start = field_at(6, strip, columns)
            target = pl.multiple_of(spot * unit_strip, 128)
            tail[:, pl.ds(target, unit_strip)] = extra[row : row + 1, start : start + unit_strip]
        for field in range(6):
            row, start = field_at(field, strip, columns)
            small[field : field + 1, :] = total[row : row + 1, start : start + strip]

    outs = [(strip, 3 * share * along), (strip, share * along), (8, strip), (1, along * unit_strip)]
    return run(
        kernel,
        [shape(out, F32) for out in outs],
        grid=(1,),
        scalars=scalars,
        specs=[whole(part.shape) for part in parts],
        arrays=parts,
        out_specs=[whole(out) for out in outs],
    )


def place_feed(scalars, parts, strip, unit_strip, groups):
    width = parts[0].shape[1]
    along = len(parts)
    own = scalars.shape[0] - 1

    def kernel(places, *refs):
        held, (grad_up, grad_down) = refs[:along], refs[along:]
        for number, ref in enumerate(held):
            spot = places[own] ^ number
            for group in range(groups):
                start = pl.multiple_of((group * along + spot) * unit_strip, 128)
                lanes = slice(group * unit_strip, (group + 1) * unit_strip)
                grad_up[:, pl.ds(start, unit_strip)] = ref[:strip, lanes].astype(F32)
            start = pl.multiple_of(spot * unit_strip, 16)
            grad_down[pl.ds(start, unit_strip), :] = ref[strip:, :].astype(F32)

    outs = [(strip, groups * along * unit_strip), (along * unit_strip, width)]
    return run(
        kernel,
        [shape(out, F32) for out in outs],
        grid=(1,),
        scalars=scalars,
        specs=[whole(part.shape) for part in parts],
        arrays=parts,
        out_specs=[whole(out) for out in outs],
    )


def natural(parts, mine):
    return jnp.take(jnp.stack(parts), mine ^ jnp.arange(len(parts)), axis=0)


def local(
    groups,
    along,
    tokens,
    cotangent,
    scene_lengths,
    key_mask,
    project_in,
    project_out,
    up_weight,
    down_weight,
    in_gain,
    in_shift,
    out_shift,
    mid_gain,
    mid_shift,
    up_shift,
    down_shift,
):
    rows, width = tokens.shape[1:]
    total = rows * along
    hidden_units = up_weight.shape[1]
    strip = width // groups
    share = width // along
    unit_strip = hidden_units // groups // along
    units = unit_strip * groups
    mine, group = lax.axis_index("seq"), lax.axis_index("fsdp")
    order = ring_order(groups)
    rings = []
    for device in order_table(order):
        rings += [[*device, place] for place in range(along)]
    scalars = lax.dynamic_index_in_dim(
        jnp.array(rings, jnp.int32), group * along + mine, 0, keepdims=False
    )
    cut = max(unit_strip // 2 // 16, 1) * 16
    own_tokens = tokens[0]
    own_cot = cotangent[0]

    fields = [in_gain, in_shift, out_shift, mid_gain, mid_shift, down_shift]
    in_part = select(
        scalars,
        [project_in] * 3 + [project_out],
        [0, along, 2 * along, 0],
        share,
        [field.reshape(1, strip) for field in fields] + [up_shift.reshape(along, -1)],
    )
    token_parts = spread(after(own_tokens, in_part), along)
    unit, all_tokens = standardize(scalars, token_parts)
    in_parts = ring_gather(in_part, order, strip // 2, [[], [*token_parts[1 : along - 1]]])
    hops = [[part for d, _, part in in_parts if d in (i, groups - i)] for i in range(1, groups // 2 + 1)]

    cot_parts = spread(after(own_cot, token_parts[-2], *hops[2]), along)
    up_weight, down_weight, key_mask = lax.optimization_barrier(
        (up_weight, down_weight, key_mask, *hops[0])
    )[:3]
    up_part = select(scalars, [up_weight] * groups, [along * i for i in range(groups)], unit_strip)
    down_part = lax.dynamic_slice_in_dim(down_weight, mine * unit_strip, unit_strip, 0)
    query_mask, key_table = tables(scalars, scene_lengths, key_mask, along)
    up_part = after(up_part, key_table)
    all_cot = jnp.concatenate(cot_parts)
    joined = up_part.shape[1] == down_part.shape[1]
    normed, query, keys, values, in_weight, out_columns, vectors, up_shift_all = project(
        scalars, unit, in_parts, rows, strip, unit_strip
    )
    outs = spread(out_columns, along)
    pairs = head_pairs(share)[0]
    attended = attend(scalars, query, keys, values, query_mask, key_table, 0)
    if joined:
        feed_part = after(jnp.concatenate([up_part, down_part]), *hops[-1])
        rings = [ring_gather(feed_part, order, strip, [[attended[0]]])]
    else:
        rings = [ring_gather(up_part, order, strip // 2), ring_gather(down_part, order, cut)]
    first_hop = [part for d, _, part in rings[0] if d in (1, groups - 1)]
    for pair in range(1, pairs):
        query = after(query, outs[1], attended[0], all_cot, *first_hop)
        attended = attend(scalars, query, keys, values, query_mask, key_table, pair, attended)
    attended, extra = attended
    all_attended = spread(attended, along)
    if share % 128:
        outs = [jnp.transpose(natural(outs, mine), (1, 0, 2)).reshape(width, width)]

    gathered, normed_mid, middle = attend_out(
        scalars, all_attended, all_tokens, vectors, outs, rows
    )
    active, grad_hidden, kept, sent, grad_up_shift, down_all = feed(
        scalars, normed_mid, all_cot, up_shift_all, rings, rows, strip
    )
    addends, sends = fold(kept, sent, along)
    active, normed_mid = lax.optimization_barrier((active, normed_mid, sends[-1]))[:2]
    up_pieces = outer(scalars, normed_mid, grad_hidden, groups)
    down_pieces = outer(scalars, active, all_cot, groups)
    if joined:
        sums = [RingSum(scalars, [up_pieces, down_pieces], order, strip)]
    else:
        sums = [
            RingSum(scalars, [up_pieces], order, strip // 2),
            RingSum(scalars, [down_pieces], order, cut),
        ]
    feed_sum = sums[0]
    grad_middle, grad_branch, middle_sums = middle_back(
        scalars, addends, middle, own_cot, vectors
    )
    branches = spread(grad_branch, along)
    active = after(active, *feed_sum.advance(grad_branch))
    result_addends, result_sends = fold(*descend(scalars, active, down_all, rows), along)
    ready = after(attended, *feed_sum.advance())
    grads, grad_extra = attended_back(scalars, branches, outs, ready)
    mixed = ()
    for pair in range(pairs):
        mixed = attend_back(
            scalars, query, extra, keys, key_table, values, grads, grad_extra, pair, mixed
        )
        if pair == 0:
            grads = after(grads, result_sends[-1], *feed_sum.advance(mixed[0]))
    pieces = projection_grads(
        scalars,
        after(normed, result_addends[-1]),
        mixed,
        gathered,
        branches,
        in_weight,
        vectors,
        middle_sums,
        grad_up_shift,
        groups,
    )
    feed_grads = [ring.finish() for ring in sums]
    pieces = after(pieces, feed_grads[0])
    attention_sum = RingSum(scalars, [pieces], order, strip // 2)
    feed_parts = spread(feed_grads[0], along)
    mixed = lax.optimization_barrier((*mixed, *attention_sum.advance(feed_parts[-2])))[:3]
    addends, sends = fold(*normed_back(scalars, mixed, in_weight, rows), along)
    fits = joined and not (share % 128 or unit_strip % 128)
    result = middle + vectors[5:6] + sum(part[0].astype(F32) for part in result_addends)
    result = result.astype(BF16)
    done = [result]
    if fits:
        grad_up, grad_down = place_feed(scalars, feed_parts, strip, unit_strip, groups)
        done += [grad_up, grad_down]
    attention_sum.advance(sends[-1], *done)
    grad_tokens = tokens_back(scalars, addends, own_tokens, grad_middle, vectors)
    attention_grads = after(attention_sum.finish(), grad_tokens)

    parts = spread(attention_grads, along)
    if fits:
        grad_in, grad_out, small, tail = place_attention(scalars, parts, strip, unit_strip)
    else:
        both = natural(parts, mine).astype(F32)
        grad_in = jnp.transpose(
            both[:, :strip, : 3 * share].reshape(along, strip, 3, share), (1, 2, 0, 3)
        ).reshape(strip, 3 * width)
        grad_out = jnp.transpose(both[:, :strip, 3 * share :], (1, 0, 2)).reshape(strip, width)
        small = jnp.sum(both[:, strip:], axis=0).reshape(-1, strip)
        tail = both[:, strip:].reshape(along, -1, strip)[:, 6, :unit_strip]
        ups = natural(feed_parts, mine).astype(F32)
        ups = ups.reshape(along, strip, groups, unit_strip)
        grad_up = jnp.transpose(ups, (1, 2, 0, 3)).reshape(strip, hidden_units)
        grad_down = natural(spread(feed_grads[1], along), mine).astype(F32)
        grad_down = grad_down.reshape(along * unit_strip, width)
    small = [small[i] for i in range(6)]
    return (
        result[None],
        grad_tokens[None],
        grad_in,
        grad_out,
        grad_up,
        grad_down,
        small[0],
        small[1],
        small[2],
        small[3],
        small[4],
        tail.reshape(-1),
        small[5],
    )


def solution(mesh):
    by_token = P("fsdp", "seq", None)
    by_row, by_part = P("fsdp", None), P("fsdp")
    return jax.shard_map(
        functools.partial(local, mesh.shape["fsdp"], mesh.shape["seq"]),
        mesh=mesh,
        in_specs=(by_token,) * 2 + (by_row,) * 6 + (by_part,) * 7,
        out_specs=(by_token,) * 2 + (by_row,) * 4 + (by_part,) * 7,
        check_vma=False,
    )
```

profile of v0, /device:TPU:0, one launch (start us, length us, event | category | flops | bytes accessed | tf_op | source)
XLA Modules:
  0.0 220.0 jit_solution(14945179254906476301)
XLA Ops:
  0.7 1.9 shard_map.255.refs_0_
  2.6 3.1 %collective-permute-start.3 = (bf16[144,1024]{1,0:T(8,128)(2,1)}, bf16[144,1024]{1,0:T(8,128)(2,1)S(1)}, u32[]{:S(2)}, u32[]{:S(2)}) collective-permute-start(bf16[144,1024]{1,0:T(8,128)(2,1)} %shard_map.255.refs_0_), channel_id=1, source_target_pairs={{0,2},{2,4},{4,6},{6,7},{7,5},{5,3},{3,1},{1,0},{8,10},{10,12},{12... | collective-permute-start | bytes 884744 | tf_op jit(solution)/shard_map/ppermute | solution.py:68
  5.7 2.0 collective-permute-start.1
  7.7 5.2 %collective-permute-done.3.refs_1_ = bf16[144,1024]{1,0:T(8,128)(2,1)S(1)} collective-permute-done((bf16[144,1024]{1,0:T(8,128)(2,1)}, bf16[144,1024]{1,0:T(8,128)(2,1)S(1)}, u32[]{:S(2)}, u32[]{:S(2)}) %collective-permute-start.3) | collective-permute-done | bytes 294944 | tf_op jit(solution)/shard_map/ppermute | solution.py:68
  12.9 1.5 collective-permute-done.4.refs_2_
  14.4 1.6 collective-permute-start.5
  17.9 1.3 collective-permute-done.1.refs_2_
  19.9 2.1 collective-permute-done.5.refs_3_
  22.1 2.0 collective-permute-done.6.refs_4_
  24.1 1.6 collective-permute-start.7
  26.1 5.0 %collective-permute-done.7.refs_5_ = bf16[144,1024]{1,0:T(8,128)(2,1)} collective-permute-done((bf16[144,1024]{1,0:T(8,128)(2,1)}, bf16[144,1024]{1,0:T(8,128)(2,1)}, u32[]{:S(2)}, u32[]{:S(2)}) %collective-permute-start.7) | collective-permute-done | bytes 294944 | tf_op jit(solution)/shard_map/ppermute | solution.py:68
  31.1 1.5 collective-permute-done.8.refs_6_
  32.6 1.5 collective-permute-start.13
  36.2 1.6 collective-permute-start.9
  38.6 1.3 shard_map.258
  40.0 2.0 collective-permute-done.9.refs_7_
  41.9 1.6 collective-permute-start.15
  44.5 1.9 shard_map.256
  46.4 4.7 %shard_map.257 = (bf16[1024,1024]{1,0:T(8,128)(2,1)S(1)}, bf16[1024,256]{1,0:T(8,128)(2,1)S(1)}, bf16[1024,256]{1,0:T(8,128)(2,1)S(1)}, bf16[1024,256]{1,0:T(8,1...) custom-call(s32[18]{0:T(128)S(1)} %dynamic-slice_bitcast_fusion._.pl, ...), custom_call_target="tpu_custom_call" | custom-call | bytes 1024 | tf_op jit(solution)/shard_map/pallas_call | solution.py:142
  51.2 6.1 %shard_map.259 = (bf16[1024,256]{1,0:T(8,128)(2,1)S(1)}, bf16[1024,256]{1,0:T(8,128)(2,1)S(1)}) custom-call(s32[18]{0:T(128)S(1)} %dynamic-slice_bitcast_fusion._.places, bf16[1024,256]{1,0:T(8,128)(2,1)S(1)} %get-tuple-element.119.q_ref, bf16[1024,256]{1,0:T(8,128)(2,1)S(1)} %get-tuple-element.108.k_ref, bf16[1024,256]{1,0:T(8,128)(2,1)S(1)} %get-tuple-element.109.v_ref, ...), custom_call_target="tpu_custom_call" | custom-call | bytes 1024 | tf_op jit(solution)/shard_map/pallas_call | solution.py:142
  57.9 1.6 collective-permute-start.22
  61.1 6.1 %shard_map.261 = (bf16[1024,256]{1,0:T(8,128)(2,1)S(1)}, bf16[1024,256]{1,0:T(8,128)(2,1)S(1)}) custom-call(s32[18]{0:T(128)S(1)} %dynamic-slice_bitcast_fusion._.places, bf16[1024,256]{1,0:T(8,128)(2,1)S(1)} %get-tuple-element.119.q_ref, bf16[1024,256]{1,0:T(8,128)(2,1)S(1)} %get-tuple-element.108.k_ref, ...), custom_call_target="tpu_custom_call", output_to_operand_aliasing={{0}: (6, {}), {1}: (7, {})} | custom-call | bytes 1024 | tf_op jit(solution)/shard_map/pallas_call | solution.py:142
  67.2 1.6 collective-permute-start.18
  68.8 3.1 %collective-permute-done.22.refs_6_ = bf16[256,1024]{1,0:T(8,128)(2,1)S(1)} collective-permute-done((bf16[256,1024]{1,0:T(8,128)(2,1)S(1)}, bf16[256,1024]{1,0:T(8,128)(2,1)S(1)}, u32[]{:S(2)}, u32[]{:S(2)}) %collective-permute-start.22) | collective-permute-done | bytes 524320 | tf_op jit(solution)/shard_map/ppermute | solution.py:68
  71.9 1.6 collective-permute-start.24
  74.5 8.5 %collective-permute-done.18.refs_2_ = bf16[1024,256]{1,0:T(8,128)(2,1)S(1)} collective-permute-done((bf16[1024,256]{1,0:T(8,128)(2,1)S(1)}, bf16[1024,256]{1,0:T(8,128)(2,1)S(1)}, u32[]{:S(2)}, u32[]{:S(2)}) %collective-permute-start.18) | collective-permute-done | bytes 524320 | tf_op jit(solution)/shard_map/ppermute | solution.py:117
  82.9 2.2 %collective-permute-done.24.refs_8_ = bf16[256,1024]{1,0:T(8,128)(2,1)S(1)} collective-permute-done((bf16[256,1024]{1,0:T(8,128)(2,1)S(1)}, bf16[256,1024]{1,0:T(8,128)(2,1)S(1)}, u32[]{:S(2)}, u32[]{:S(2)}) %collective-permute-start.24) | collective-permute-done | bytes 524320 | tf_op jit(solution)/shard_map/ppermute | solution.py:68
  85.2 1.6 collective-permute-start.26
  87.5 5.6 %shard_map.262 = (bf16[1024,1024]{1,0:T(8,128)(2,1)S(1)}, bf16[1024,1024]{1,0:T(8,128)(2,1)S(1)}, f32[256,1024]{1,0:T(8,128)S(1)}) custom-call(s32[18]{0:T(128)S(1)} %dynamic-slice_bitcast_fusion._.places, bf16[1024,256]{1,0:T(8,128)(2,1)S(1)} %get-tuple-element.146.refs_0_.refs_8_, bf16[1024,256]{1,0:T(8,128)(2,1)S(1)} %collective-permute-done.17.refs_1_, ...), custom_call_target="tpu_custom_call" | custom-call | bytes 1024 | tf_op jit(solution)/shard_map/pallas_call | solution.py:142
  93.5 8.3 %shard_map.263 = (bf16[1024,1024]{1,0:T(8,128)(2,1)S(1)}, bf16[1024,1024]{1,0:T(8,128)(2,1)S(1)}, bf16[2,256,1024]{2,1,0:T(8,128)(2,1)S(1)}, bf16[2,256,1024]{2,...) custom-call(s32[18]{0:T(128)S(1)} %dynamic-slice_bitcast_fusion._.places, ...), custom_call_target="tpu_custom_call" | custom-call | bytes 1024 | tf_op jit(solution)/shard_map/pallas_call | solution.py:142
  101.9 2.6 %collective-permute-done.28 = bf16[2,256,1024]{2,1,0:T(8,128)(2,1)S(1)} collective-permute-done((bf16[2,256,1024]{2,1,0:T(8,128)(2,1)S(1)}, bf16[2,256,1024]{2,1,0:T(8,128)(2,1)S(1)}, u32[]{:S(2)}, u32[]{:S(2)}) %collective-permute-start.28) | collective-permute-done | bytes 1048608 | tf_op jit(solution)/shard_map/ppermute | solution.py:117
  104.8 1.6 collective-permute-start.30
  106.3 3.6 %shard_map.264.refs_0_.refs_2_ = bf16[8,128,1024]{2,1,0:T(8,128)(2,1)S(1)} custom-call(s32[18]{0:T(128)S(1)} %dynamic-slice_bitcast_fusion._.places, bf16[1024,1024]{1,0:T(8,128)(2,1)S(1)} %get-tuple-element.133.refs_0_.left_ref, bf16[1024,1024]{1,0:T(8,128)(2,1)S(1)} %get-tuple-element.134.right_ref), custom_call_target="tpu_custom_call" | custom-call | bytes 1024 | tf_op jit(solution)/shard_map/pallas_call | solution.py:142
  109.9 1.5 collective-permute-start.29
  111.5 3.6 %shard_map.265.refs_1_.refs_3_ = bf16[8,128,1024]{2,1,0:T(8,128)(2,1)S(1)} custom-call(s32[18]{0:T(128)S(1)} %dynamic-slice_bitcast_fusion._.places, bf16[1024,1024]{1,0:T(8,128)(2,1)S(1)} %get-tuple-element.139.left_ref.active_ref, bf16[1024,1024]{1,0:T(8,128)(2,1)S(1)} %constant_dynamic-update-slice_fusion.refs_1_.right_ref), custom_call_target="tpu_custom_call" | custom-call | bytes 1024 | tf_op jit(solution)/shard_map/pallas_call | solution.py:142
  115.8 3.0 %collective-permute-done.30.refs_2_ = bf16[1,256,1024]{2,1,0:T(8,128)(2,1)S(1)} collective-permute-done((bf16[1,256,1024]{2,1,0:T(8,128)(2,1)S(1)}, bf16[1,256,1024]{2,1,0:T(8,128)(2,1)S(1)}, u32[]{:S(2)}, u32[]{:S(2)}) %collective-permute-start.30) | collective-permute-done | bytes 524320 | tf_op jit(solution)/shard_map/ppermute | solution.py:117
  118.8 1.9 shard_map.266
  120.7 1.6 collective-permute-start.35
  123.8 1.3 collective-permute-start.37
  125.8 3.0 %shard_map.268 = (bf16[2,256,1024]{2,1,0:T(8,128)(2,1)S(1)}, bf16[2,256,1024]{2,1,0:T(8,128)(2,1)S(1)}) custom-call(s32[18]{0:T(128)S(1)} %dynamic-slice_bitcast_fusion._.places, bf16[1024,1024]{1,0:T(8,128)(2,1)S(1)} %get-tuple-element.139.left_ref.active_ref, bf16[1024,1024]{1,0:T(8,128)(2,1)S(1)} %get-tuple-element.140.down_ref), custom_call_target="tpu_custom_call" | custom-call | bytes 1024 | tf_op jit(solution)/shard_map/pallas_call | solution.py:142
  129.5 4.5 %collective-permute-done.35.refs_2_.refs_5_ = bf16[256,1024]{1,0:T(8,128)(2,1)S(1)} collective-permute-done((bf16[256,1024]{1,0:T(8,128)(2,1)S(1)}, bf16[256,1024]{1,0:T(8,128)(2,1)S(1)}, u32[]{:S(2)}, u32[]{:S(2)}) %collective-permute-start.35) | collective-permute-done | bytes 524320 | tf_op jit(solution)/shard_map/ppermute | solution.py:117
  133.9 2.4 %collective-permute-done.37.refs_4_ = bf16[256,1024]{1,0:T(8,128)(2,1)S(1)} collective-permute-done((bf16[256,1024]{1,0:T(8,128)(2,1)S(1)}, bf16[256,1024]{1,0:T(8,128)(2,1)S(1)}, u32[]{:S(2)}, u32[]{:S(2)}) %collective-permute-start.37) | collective-permute-done | bytes 524320 | tf_op jit(solution)/shard_map/ppermute | solution.py:93
  138.1 1.3 collective-permute-start.39
  140.1 2.9 %shard_map.270 = (bf16[1024,256]{1,0:T(8,128)(2,1)S(1)}, bf16[1024,256]{1,0:T(8,128)(2,1)S(1)}) custom-call(s32[18]{0:T(128)S(1)} %dynamic-slice_bitcast_fusion._.places, bf16[256,1024]{1,0:T(8,128)(2,1)S(1)} %get-tuple-element.135.refs_0_.refs_3_, bf16[256,1024]{1,0:T(8,128)(2,1)S(1)} %collective-permute-done.34.refs_1_.refs_4_, ...), custom_call_target="tpu_custom_call" | custom-call | bytes 1024 | tf_op jit(solution)/shard_map/pallas_call | solution.py:142
  143.0 7.2 %shard_map.271 = (bf16[1024,256]{1,0:T(8,128)(2,1)S(1)}, bf16[1024,256]{1,0:T(8,128)(2,1)S(1)}, bf16[1024,256]{1,0:T(8,128)(2,1)S(1)}) custom-call(s32[18]{0:T(128)S(1)} %dynamic-slice_bitcast_fusion._.places, bf16[1024,256]{1,0:T(8,128)(2,1)S(1)} %get-tuple-element.119.q_ref, bf16[1024,256]{1,0:T(8,128)(2,1)S(1)} %get-tuple-element.143.qx_ref, ...), custom_call_target="tpu_custom_call" | custom-call | bytes 1024 | tf_op jit(solution)/shard_map/pallas_call | solution.py:142
  155.0 7.2 %shard_map.273 = (bf16[1024,256]{1,0:T(8,128)(2,1)S(1)}, bf16[1024,256]{1,0:T(8,128)(2,1)S(1)}, bf16[1024,256]{1,0:T(8,128)(2,1)S(1)}) custom-call(s32[18]{0:T(128)S(1)} %dynamic-slice_bitcast_fusion._.places, bf16[1024,256]{1,0:T(8,128)(2,1)S(1)} %get-tuple-element.119.q_ref, ...), custom_call_target="tpu_custom_call", output_to_operand_aliasing={{0}: (8, {}), {1}: (9, {}), {2}: (10, {})} | custom-call | bytes 1024 | tf_op jit(solution)/shard_map/pallas_call | solution.py:142
  163.9 2.3 %collective-permute-start.44 = (bf16[256,1024]{1,0:T(8,128)(2,1)S(1)}, bf16[256,1024]{1,0:T(8,128)(2,1)S(1)}, u32[]{:S(2)}, u32[]{:S(2)}) collective-permute-start(bf16[256,1024]{1,0:T(8,128)(2,1)S(1)} %shard_map.275.refs_0_), channel_id=1, source_target_pairs={{0,16},{8,24},{16,0},{24,8},{1,17},{9,25},{17,1},{25,9},{2,18},{10... | collective-permute-start | bytes 1572872 | tf_op jit(solution)/shard_map/ppermute | solution.py:117
  166.2 4.4 %shard_map.274.refs_0_.refs_1_ = bf16[8,144,1024]{2,1,0:T(8,128)(2,1)S(1)} custom-call(s32[18]{0:T(128)S(1)} %dynamic-slice_bitcast_fusion._.places, bf16[1024,1024]{1,0:T(8,128)(2,1)S(1)} %get-tuple-element.160.normed_ref, bf16[1024,1024]{1,0:T(8,128)(2,1)S(1)} %get-tuple-element.161.gathered_ref, bf16[1024,768]{1,0:T(8,128)(2,1)S(1)} %get-tuple-element.162.weight_ref, ...), custom_call_target="tpu_custom_call" | custom-call | bytes 1024 | tf_op jit(solution)/shard_map/pallas_call | solution.py:142
  171.0 1.8 collective-permute-start.43
  172.8 3.2 %collective-permute-done.43.refs_2_ = bf16[64,1024]{1,0:T(8,128)(2,1)S(1)} collective-permute-done((bf16[64,1024]{1,0:T(8,128)(2,1)S(1)}, bf16[64,1024]{1,0:T(8,128)(2,1)S(1)}, u32[]{:S(2)}, u32[]{:S(2)}) %collective-permute-start.43) | collective-permute-done | bytes 131104 | tf_op jit(solution)/shard_map/ppermute | solution.py:93
  176.7 2.6 %shard_map.277 = (bf16[2,256,1024]{2,1,0:T(8,128)(2,1)S(1)}, bf16[2,256,1024]{2,1,0:T(8,128)(2,1)S(1)}) custom-call(s32[18]{0:T(128)S(1)} %dynamic-slice_bitcast_fusion._.places, bf16[1024,256]{1,0:T(8,128)(2,1)S(1)} %get-tuple-element.169.refs_0_.q_ref, bf16[1024,256]{1,0:T(8,128)(2,1)S(1)} %get-tuple-element.170.refs_1_.k_ref, ...), custom_call_target="tpu_custom_call" | custom-call | bytes 1024 | tf_op jit(solution)/shard_map/pallas_call | solution.py:142
  179.9 1.7 collective-permute-start.48
  183.5 2.9 %shard_map.279 = (f32[128,4096]{1,0:T(8,128)}, f32[512,1024]{1,0:T(8,128)}) custom-call(s32[18]{0:T(128)S(1)} %dynamic-slice_bitcast_fusion._.places, bf16[256,1024]{1,0:T(8,128)(2,1)S(1)} %shard_map.275.refs_0_, bf16[256,1024]{1,0:T(8,128)(2,1)S(1)} %collective-permute-done.49.refs_1_, bf16[256,1024]{1,0:T(8,128)(2,1)S(1)} %collective-permute-done.44.refs_2_, ...), custom_call_target="tpu_custom_call" | custom-call | bytes 1024 | tf_op jit(solution)/shard_map/pallas_call | solution.py:142
  186.6 2.7 %collective-permute-done.48.refs_2_ = bf16[144,1024]{1,0:T(8,128)(2,1)S(1)} collective-permute-done((bf16[144,1024]{1,0:T(8,128)(2,1)S(1)}, bf16[144,1024]{1,0:T(8,128)(2,1)S(1)}, u32[]{:S(2)}, u32[]{:S(2)}) %collective-permute-start.48) | collective-permute-done | bytes 294944 | tf_op jit(solution)/shard_map/ppermute | solution.py:93
  189.3 1.5 collective-permute-done.51.refs_3_
  192.3 1.3 collective-permute-start.53
  194.4 5.4 %collective-permute-done.52.refs_2_ = bf16[144,1024]{1,0:T(8,128)(2,1)S(1)} collective-permute-done((bf16[144,1024]{1,0:T(8,128)(2,1)S(1)}, bf16[144,1024]{1,0:T(8,128)(2,1)S(1)}, u32[]{:S(2)}, u32[]{:S(2)}) %collective-permute-start.52) | collective-permute-done | bytes 294944 | tf_op jit(solution)/shard_map/ppermute | solution.py:93
  201.7 1.3 collective-permute-start.55
  203.1 3.0 %collective-permute-done.47.refs_2_ = bf16[1,256,1024]{2,1,0:T(8,128)(2,1)S(1)} collective-permute-done((bf16[1,256,1024]{2,1,0:T(8,128)(2,1)S(1)}, bf16[1,256,1024]{2,1,0:T(8,128)(2,1)S(1)}, u32[]{:S(2)}, u32[]{:S(2)}) %collective-permute-start.47) | collective-permute-done | bytes 524320 | tf_op jit(solution)/shard_map/ppermute | solution.py:117
  206.1 2.2 shard_map.278
  209.1 1.5 collective-permute-start.57
  210.6 5.3 %collective-permute-done.57.refs_2_ = bf16[144,1024]{1,0:T(8,128)(2,1)S(1)} collective-permute-done((bf16[144,1024]{1,0:T(8,128)(2,1)S(1)}, bf16[144,1024]{1,0:T(8,128)(2,1)S(1)}, u32[]{:S(2)}, u32[]{:S(2)}) %collective-permute-start.57) | collective-permute-done | bytes 294944 | tf_op jit(solution)/shard_map/ppermute | solution.py:117
  215.9 1.6 collective-permute-done.58.refs_3_
  217.5 2.0 shard_map.283
  (140 shorter events, 33.3 us)
Async XLA Ops:
  0.6 37.2 %copy-start = (bf16[512,1024]{1,0:T(8,128)(2,1)S(1)}, bf16[512,1024]{1,0:T(8,128)(2,1)}, u32[]{:S(2)}) copy-start(bf16[512,1024]{1,0:T(8,128)(2,1)} %param.23) | copy-start | bytes 3145732
  0.7 31.9 %copy-start.4 = (bf16[1,256,1024]{2,1,0:T(8,128)(2,1)S(1)}, bf16[1,256,1024]{2,1,0:T(8,128)(2,1)}, u32[]{:S(2)}) copy-start(bf16[1,256,1024]{2,1,0:T(8,128)(2,1)} %param.17) | copy-start | bytes 1572868
  0.7 37.2 %copy-start.2 = (bf16[128,4096]{1,0:T(8,128)(2,1)S(1)}, bf16[128,4096]{1,0:T(8,128)(2,1)}, u32[]{:S(2)}) copy-start(bf16[128,4096]{1,0:T(8,128)(2,1)} %refs_7_) | copy-start | bytes 3145732
  2.6 10.2 %collective-permute-start.3 = (bf16[144,1024]{1,0:T(8,128)(2,1)}, bf16[144,1024]{1,0:T(8,128)(2,1)S(1)}, u32[]{:S(2)}, u32[]{:S(2)}) collective-permute-start(bf16[144,1024]{1,0:T(8,128)(2,1)} %shard_map.255.refs_0_), channel_id=1, source_target_pairs={{0,2},{2,4},{4,6},{6,7},{7,5},{5,3},{3,1},{1,0},{8,10},{10,12},{12... | collective-permute-start | bytes 884744 | tf_op jit(solution)/shard_map/ppermute | solution.py:68
  5.7 8.7 %collective-permute-start.4 = (bf16[144,1024]{1,0:T(8,128)(2,1)}, bf16[144,1024]{1,0:T(8,128)(2,1)S(1)}, u32[]{:S(2)}, u32[]{:S(2)}) collective-permute-start(bf16[144,1024]{1,0:T(8,128)(2,1)} %shard_map.255.refs_0_), channel_id=1, source_target_pairs={{2,0},{4,2},{6,4},{7,6},{5,7},{3,5},{1,3},{0,1},{10,8},{12,10},{14... | collective-permute-start | bytes 884744 | tf_op jit(solution)/shard_map/ppermute | solution.py:69
  5.7 13.4 %collective-permute-start.1 = (bf16[256,1024]{1,0:T(8,128)(2,1)S(1)}, bf16[256,1024]{1,0:T(8,128)(2,1)S(1)}, u32[]{:S(2)}, u32[]{:S(2)}) collective-permute-start(bf16[256,1024]{1,0:T(8,128)(2,1)S(1)} %bitcast.39), channel_id=1, source_target_pairs={{0,16},{8,24},{16,0},{24,8},{1,17},{9,25},{17,1},{25,9},{2,18},{10... | collective-permute-start | bytes 1572872 | tf_op jit(solution)/shard_map/ppermute | solution.py:117
  7.7 11.4 %collective-permute-start = (bf16[256,1024]{1,0:T(8,128)(2,1)S(1)}, bf16[256,1024]{1,0:T(8,128)(2,1)S(1)}, u32[]{:S(2)}, u32[]{:S(2)}) collective-permute-start(bf16[256,1024]{1,0:T(8,128)(2,1)S(1)} %bitcast.40), channel_id=1, source_target_pairs={{0,8},{8,0},{16,24},{24,16},{1,9},{9,1},{17,25},{25,17},{2,10},{10... | collective-permute-start | bytes 1572872 | tf_op jit(solution)/shard_map/ppermute | solution.py:117
  14.4 7.7 %collective-permute-start.5 = (bf16[144,1024]{1,0:T(8,128)(2,1)S(1)}, bf16[144,1024]{1,0:T(8,128)(2,1)}, u32[]{:S(2)}, u32[]{:S(2)}) collective-permute-start(bf16[144,1024]{1,0:T(8,128)(2,1)S(1)} %collective-permute-done.3.refs_1_), channel_id=1, source_target_pairs={{0,2},{2,4},{4,6},{6,7},{7,5},{5,3},{3,1},{1,0},{8,10},{10,12},{12... | collective-permute-start | bytes 884744 | tf_op jit(solution)/shard_map/ppermute | solution.py:68
  16.7 7.4 %collective-permute-start.6 = (bf16[144,1024]{1,0:T(8,128)(2,1)S(1)}, bf16[144,1024]{1,0:T(8,128)(2,1)}, u32[]{:S(2)}, u32[]{:S(2)}) collective-permute-start(bf16[144,1024]{1,0:T(8,128)(2,1)S(1)} %collective-permute-done.4.refs_2_), channel_id=1, source_target_pairs={{2,0},{4,2},{6,4},{7,6},{5,7},{3,5},{1,3},{0,1},{10,8},{12,10},{14... | collective-permute-start | bytes 884744 | tf_op jit(solution)/shard_map/ppermute | solution.py:69
  24.1 7.0 %collective-permute-start.7 = (bf16[144,1024]{1,0:T(8,128)(2,1)}, bf16[144,1024]{1,0:T(8,128)(2,1)}, u32[]{:S(2)}, u32[]{:S(2)}) collective-permute-start(bf16[144,1024]{1,0:T(8,128)(2,1)} %collective-permute-done.5.refs_3_), channel_id=1, source_target_pairs={{0,2},{2,4},{4,6},{6,7},{7,5},{5,3},{3,1},{1,0},{8,10},{10,12},{12... | collective-permute-start | bytes 884744 | tf_op jit(solution)/shard_map/ppermute | solution.py:68
  25.7 6.9 %collective-permute-start.8 = (bf16[144,1024]{1,0:T(8,128)(2,1)}, bf16[144,1024]{1,0:T(8,128)(2,1)S(1)}, u32[]{:S(2)}, u32[]{:S(2)}) collective-permute-start(bf16[144,1024]{1,0:T(8,128)(2,1)} %collective-permute-done.6.refs_4_), channel_id=1, source_target_pairs={{2,0},{4,2},{6,4},{7,6},{5,7},{3,5},{1,3},{0,1},{10,8},{12,10},{14... | collective-permute-start | bytes 884744 | tf_op jit(solution)/shard_map/ppermute | solution.py:69
  32.6 11.4 %collective-permute-start.13 = (bf16[256,1024]{1,0:T(8,128)(2,1)S(1)}, bf16[256,1024]{1,0:T(8,128)(2,1)}, u32[]{:S(2)}, u32[]{:S(2)}) collective-permute-start(bf16[256,1024]{1,0:T(8,128)(2,1)S(1)} %bitcast.43), channel_id=1, source_target_pairs={{0,16},{8,24},{16,0},{24,8},{1,17},{9,25},{17,1},{25,9},{2,18},{10... | collective-permute-start | bytes 1572872 | tf_op jit(solution)/shard_map/ppermute | solution.py:117
  34.8 9.7 %collective-permute-start.2 = (bf16[256,1024]{1,0:T(8,128)(2,1)}, bf16[256,1024]{1,0:T(8,128)(2,1)S(1)}, u32[]{:S(2)}, u32[]{:S(2)}) collective-permute-start(bf16[256,1024]{1,0:T(8,128)(2,1)} %copy-done.6), channel_id=1, source_target_pairs={{0,8},{8,0},{16,24},{24,16},{1,9},{9,1},{17,25},{25,17},{2,10},{10... | collective-permute-start | bytes 1572872 | tf_op jit(solution)/shard_map/ppermute | solution.py:117
  34.8 7.1 %collective-permute-start.10 = (bf16[80,1024]{1,0:T(8,128)(2,1)S(1)}, bf16[80,1024]{1,0:T(8,128)(2,1)S(1)}, u32[]{:S(2)}, u32[]{:S(2)}) collective-permute-start(bf16[80,1024]{1,0:T(8,128)(2,1)S(1)} %slice.132), channel_id=1, source_target_pairs={{2,0},{4,2},{6,4},{7,6},{5,7},{3,5},{1,3},{0,1},{10,8},{12,10},{14... | collective-permute-start | bytes 491528 | tf_op jit(solution)/shard_map/ppermute | solution.py:75
  36.2 5.7 %collective-permute-start.9 = (bf16[64,1024]{1,0:T(8,128)(2,1)S(1)}, bf16[64,1024]{1,0:T(8,128)(2,1)S(1)}, u32[]{:S(2)}, u32[]{:S(2)}) collective-permute-start(bf16[64,1024]{1,0:T(8,128)(2,1)S(1)} %slice.131), channel_id=1, source_target_pairs={{0,2},{2,4},{4,6},{6,7},{7,5},{5,3},{3,1},{1,0},{8,10},{10,12},{12... | collective-permute-start | bytes 393224 | tf_op jit(solution)/shard_map/ppermute | solution.py:73
  38.6 7.8 %copy-start.13 = (bf16[144,1024]{1,0:T(8,128)(2,1)S(1)}, bf16[144,1024]{1,0:T(8,128)(2,1)}, u32[]{:S(2)}) copy-start(bf16[144,1024]{1,0:T(8,128)(2,1)} %copy-done.12) | copy-start | bytes 884740
  41.9 15.4 %collective-permute-start.15 = (bf16[256,1024]{1,0:T(8,128)(2,1)S(1)}, bf16[256,1024]{1,0:T(8,128)(2,1)S(1)}, u32[]{:S(2)}, u32[]{:S(2)}) collective-permute-start(bf16[256,1024]{1,0:T(8,128)(2,1)S(1)} %pad_maximum_fusion.refs_3_), channel_id=1, source_target_pairs={{0,2},{2,4},{4,6},{6,7},{7,5},{5,3},{3,1},{1,0},{8,10},{10,12},{12... | collective-permute-start | bytes 1572872 | tf_op jit(solution)/shard_map/ppermute | solution.py:68
  43.5 14.4 %collective-permute-start.16 = (bf16[256,1024]{1,0:T(8,128)(2,1)S(1)}, bf16[256,1024]{1,0:T(8,128)(2,1)S(1)}, u32[]{:S(2)}, u32[]{:S(2)}) collective-permute-start(bf16[256,1024]{1,0:T(8,128)(2,1)S(1)} %pad_maximum_fusion.refs_3_), channel_id=1, source_target_pairs={{2,0},{4,2},{6,4},{7,6},{5,7},{3,5},{1,3},{0,1},{10,8},{12,10},{14... | collective-permute-start | bytes 1572872 | tf_op jit(solution)/shard_map/ppermute | solution.py:69
  44.0 15.5 %collective-permute-start.12 = (bf16[256,1024]{1,0:T(8,128)(2,1)S(1)}, bf16[256,1024]{1,0:T(8,128)(2,1)S(1)}, u32[]{:S(2)}, u32[]{:S(2)}) collective-permute-start(bf16[256,1024]{1,0:T(8,128)(2,1)S(1)} %bitcast.44), channel_id=1, source_target_pairs={{0,8},{8,0},{16,24},{24,16},{1,9},{9,1},{17,25},{25,17},{2,10},{10... | collective-permute-start | bytes 1572872 | tf_op jit(solution)/shard_map/ppermute | solution.py:117
  44.0 17.1 %collective-permute-start.14 = (bf16[256,1024]{1,0:T(8,128)(2,1)}, bf16[256,1024]{1,0:T(8,128)(2,1)S(1)}, u32[]{:S(2)}, u32[]{:S(2)}) collective-permute-start(bf16[256,1024]{1,0:T(8,128)(2,1)} %collective-permute-done.13), channel_id=1, source_target_pairs={{0,8},{8,0},{16,24},{24,16},{1,9},{9,1},{17,25},{25,17},{2,10},{10... | collective-permute-start | bytes 1572872 | tf_op jit(solution)/shard_map/ppermute | solution.py:117
  51.1 10.0 %collective-permute-start.11 = (bf16[1024,256]{1,0:T(8,128)(2,1)S(1)}, bf16[1024,256]{1,0:T(8,128)(2,1)S(1)}, u32[]{:S(2)}, u32[]{:S(2)}) collective-permute-start(bf16[1024,256]{1,0:T(8,128)(2,1)S(1)} %get-tuple-element.107.refs_6_.refs_4_), channel_id=1, source_target_pairs={{0,8},{8,0},{16,24},{24,16},{1,9},{9,1},{17,25},{25,17},{2,10},{10... | collective-permute-start | bytes 1572872 | tf_op jit(solution)/shard_map/ppermute | solution.py:117
  57.3 16.7 %collective-permute-start.20 = (bf16[1024,256]{1,0:T(8,128)(2,1)S(1)}, bf16[1024,256]{1,0:T(8,128)(2,1)S(1)}, u32[]{:S(2)}, u32[]{:S(2)}) collective-permute-start(bf16[1024,256]{1,0:T(8,128)(2,1)S(1)} %get-tuple-element.107.refs_6_.refs_4_), channel_id=1, source_target_pairs={{0,16},{8,24},{16,0},{24,8},{1,17},{9,25},{17,1},{25,9},{2,18},{10... | collective-permute-start | bytes 1572872 | tf_op jit(solution)/shard_map/ppermute | solution.py:117
  57.9 14.0 %collective-permute-start.22 = (bf16[256,1024]{1,0:T(8,128)(2,1)S(1)}, bf16[256,1024]{1,0:T(8,128)(2,1)S(1)}, u32[]{:S(2)}, u32[]{:S(2)}) collective-permute-start(bf16[256,1024]{1,0:T(8,128)(2,1)S(1)} %collective-permute-done.15.refs_4_), channel_id=1, source_target_pairs={{0,2},{2,4},{4,6},{6,7},{7,5},{5,3},{3,1},{1,0},{8,10},{10,12},{12... | collective-permute-start | bytes 1572872 | tf_op jit(solution)/shard_map/ppermute | solution.py:68
  59.5 14.0 %collective-permute-start.23 = (bf16[256,1024]{1,0:T(8,128)(2,1)S(1)}, bf16[256,1024]{1,0:T(8,128)(2,1)S(1)}, u32[]{:S(2)}, u32[]{:S(2)}) collective-permute-start(bf16[256,1024]{1,0:T(8,128)(2,1)S(1)} %collective-permute-done.16.refs_5_), channel_id=1, source_target_pairs={{2,0},{4,2},{6,4},{7,6},{5,7},{3,5},{1,3},{0,1},{10,8},{12,10},{14... | collective-permute-start | bytes 1572872 | tf_op jit(solution)/shard_map/ppermute | solution.py:69
  67.2 15.7 %collective-permute-start.18 = (bf16[1024,256]{1,0:T(8,128)(2,1)S(1)}, bf16[1024,256]{1,0:T(8,128)(2,1)S(1)}, u32[]{:S(2)}, u32[]{:S(2)}) collective-permute-start(bf16[1024,256]{1,0:T(8,128)(2,1)S(1)} %get-tuple-element.146.refs_0_.refs_8_), channel_id=1, source_target_pairs={{0,16},{8,24},{16,0},{24,8},{1,17},{9,25},{17,1},{25,9},{2,18},{10... | collective-permute-start | bytes 1572872 | tf_op jit(solution)/shard_map/ppermute | solution.py:117
  71.9 13.2 %collective-permute-start.24 = (bf16[256,1024]{1,0:T(8,128)(2,1)S(1)}, bf16[256,1024]{1,0:T(8,128)(2,1)S(1)}, u32[]{:S(2)}, u32[]{:S(2)}) collective-permute-start(bf16[256,1024]{1,0:T(8,128)(2,1)S(1)} %collective-permute-done.22.refs_6_), channel_id=1, source_target_pairs={{0,2},{2,4},{4,6},{6,7},{7,5},{5,3},{3,1},{1,0},{8,10},{10,12},{12... | collective-permute-start | bytes 1572872 | tf_op jit(solution)/shard_map/ppermute | solution.py:68
  73.5 13.3 %collective-permute-start.25 = (bf16[256,1024]{1,0:T(8,128)(2,1)S(1)}, bf16[256,1024]{1,0:T(8,128)(2,1)S(1)}, u32[]{:S(2)}, u32[]{:S(2)}) collective-permute-start(bf16[256,1024]{1,0:T(8,128)(2,1)S(1)} %collective-permute-done.23.refs_7_), channel_id=1, source_target_pairs={{2,0},{4,2},{6,4},{7,6},{5,7},{3,5},{1,3},{0,1},{10,8},{12,10},{14... | collective-permute-start | bytes 1572872 | tf_op jit(solution)/shard_map/ppermute | solution.py:69
  74.0 13.6 %collective-permute-start.21 = (bf16[1024,256]{1,0:T(8,128)(2,1)S(1)}, bf16[1024,256]{1,0:T(8,128)(2,1)S(1)}, u32[]{:S(2)}, u32[]{:S(2)}) collective-permute-start(bf16[1024,256]{1,0:T(8,128)(2,1)S(1)} %collective-permute-done.20.refs_8_.refs_6_), channel_id=1, source_target_pairs={{0,8},{8,0},{16,24},{24,16},{1,9},{9,1},{17,25},{25,17},{2,10},{10... | collective-permute-start | bytes 1572872 | tf_op jit(solution)/shard_map/ppermute | solution.py:117
  74.0 13.6 %collective-permute-start.17 = (bf16[1024,256]{1,0:T(8,128)(2,1)S(1)}, bf16[1024,256]{1,0:T(8,128)(2,1)S(1)}, u32[]{:S(2)}, u32[]{:S(2)}) collective-permute-start(bf16[1024,256]{1,0:T(8,128)(2,1)S(1)} %get-tuple-element.146.refs_0_.refs_8_), channel_id=1, source_target_pairs={{0,8},{8,0},{16,24},{24,16},{1,9},{9,1},{17,25},{25,17},{2,10},{10... | collective-permute-start | bytes 1572872 | tf_op jit(solution)/shard_map/ppermute | solution.py:117
  82.9 4.6 %collective-permute-start.19 = (bf16[1024,256]{1,0:T(8,128)(2,1)S(1)}, bf16[1024,256]{1,0:T(8,128)(2,1)S(1)}, u32[]{:S(2)}, u32[]{:S(2)}) collective-permute-start(bf16[1024,256]{1,0:T(8,128)(2,1)S(1)} %collective-permute-done.18.refs_2_), channel_id=1, source_target_pairs={{0,8},{8,0},{16,24},{24,16},{1,9},{9,1},{17,25},{25,17},{2,10},{10... | collective-permute-start | bytes 1572872 | tf_op jit(solution)/shard_map/ppermute | solution.py:117
  85.2 7.9 %collective-permute-start.26 = (bf16[128,1024]{1,0:T(8,128)(2,1)S(1)}, bf16[128,1024]{1,0:T(8,128)(2,1)S(1)}, u32[]{:S(2)}, u32[]{:S(2)}) collective-permute-start(bf16[128,1024]{1,0:T(8,128)(2,1)S(1)} %slice.133), channel_id=1, source_target_pairs={{0,2},{2,4},{4,6},{6,7},{7,5},{5,3},{3,1},{1,0},{8,10},{10,12},{12... | collective-permute-start | bytes 786440 | tf_op jit(solution)/shard_map/ppermute | solution.py:73
  86.8 6.6 %collective-permute-start.27 = (bf16[128,1024]{1,0:T(8,128)(2,1)S(1)}, bf16[128,1024]{1,0:T(8,128)(2,1)S(1)}, u32[]{:S(2)}, u32[]{:S(2)}) collective-permute-start(bf16[128,1024]{1,0:T(8,128)(2,1)S(1)} %slice.134), channel_id=1, source_target_pairs={{2,0},{4,2},{6,4},{7,6},{5,7},{3,5},{1,3},{0,1},{10,8},{12,10},{14... | collective-permute-start | bytes 786440 | tf_op jit(solution)/shard_map/ppermute | solution.py:75
  101.8 2.7 %collective-permute-start.28 = (bf16[2,256,1024]{2,1,0:T(8,128)(2,1)S(1)}, bf16[2,256,1024]{2,1,0:T(8,128)(2,1)S(1)}, u32[]{:S(2)}, u32[]{:S(2)}) collective-permute-start(bf16[2,256,1024]{2,1,0:T(8,128)(2,1)S(1)} %get-tuple-element.131), channel_id=1, source_target_pairs={{0,8},{8,0},{16,24},{24,16},{1,9},{9,1},{17,25},{25,17},{2,10},{10... | collective-permute-start | bytes 3145736 | tf_op jit(solution)/shard_map/ppermute | solution.py:117
  104.8 14.0 %collective-permute-start.30 = (bf16[1,256,1024]{2,1,0:T(8,128)(2,1)S(1)}, bf16[1,256,1024]{2,1,0:T(8,128)(2,1)S(1)}, u32[]{:S(2)}, u32[]{:S(2)}) collective-permute-start(bf16[1,256,1024]{2,1,0:T(8,128)(2,1)S(1)} %add_convert_fusion.2), channel_id=1, source_target_pairs={{0,16},{8,24},{16,0},{24,8},{1,17},{9,25},{17,1},{25,9},{2,18},{10... | collective-permute-start | bytes 1572872 | tf_op jit(solution)/shard_map/ppermute | solution.py:117
  109.9 12.4 %collective-permute-start.29 = (bf16[128,1024]{1,0:T(8,128)(2,1)S(1)}, bf16[128,1024]{1,0:T(8,128)(2,1)S(1)}, u32[]{:S(2)}, u32[]{:S(2)}) collective-permute-start(bf16[128,1024]{1,0:T(8,128)(2,1)S(1)} %slice_bitcast_fusion.1), channel_id=1, source_target_pairs={{0,2},{2,4},{4,6},{6,7},{7,5},{5,3},{3,1},{1,0},{8,10},{10,12},{12... | collective-permute-start | bytes 786440 | tf_op jit(solution)/shard_map/ppermute | solution.py:93
  115.1 7.8 %collective-permute-start.31 = (bf16[128,1024]{1,0:T(8,128)(2,1)S(1)}, bf16[128,1024]{1,0:T(8,128)(2,1)S(1)}, u32[]{:S(2)}, u32[]{:S(2)}) collective-permute-start(bf16[128,1024]{1,0:T(8,128)(2,1)S(1)} %slice_bitcast_fusion), channel_id=1, source_target_pairs={{2,0},{4,2},{6,4},{7,6},{5,7},{3,5},{1,3},{0,1},{10,8},{12,10},{14... | collective-permute-start | bytes 786440 | tf_op jit(solution)/shard_map/ppermute | solution.py:95
  120.7 13.2 %collective-permute-start.35 = (bf16[256,1024]{1,0:T(8,128)(2,1)S(1)}, bf16[256,1024]{1,0:T(8,128)(2,1)S(1)}, u32[]{:S(2)}, u32[]{:S(2)}) collective-permute-start(bf16[256,1024]{1,0:T(8,128)(2,1)S(1)} %get-tuple-element.135.refs_0_.refs_3_), channel_id=1, source_target_pairs={{0,16},{8,24},{16,0},{24,8},{1,17},{9,25},{17,1},{25,9},{2,18},{10... | collective-permute-start | bytes 1572872 | tf_op jit(solution)/shard_map/ppermute | solution.py:117
  123.8 12.6 %collective-permute-start.37 = (bf16[256,1024]{1,0:T(8,128)(2,1)S(1)}, bf16[256,1024]{1,0:T(8,128)(2,1)S(1)}, u32[]{:S(2)}, u32[]{:S(2)}) collective-permute-start(bf16[256,1024]{1,0:T(8,128)(2,1)S(1)} %get-tuple-element.137), channel_id=1, source_target_pairs={{0,2},{2,4},{4,6},{6,7},{7,5},{5,3},{3,1},{1,0},{8,10},{10,12},{12... | collective-permute-start | bytes 1572872 | tf_op jit(solution)/shard_map/ppermute | solution.py:93
  125.1 12.2 %collective-permute-start.38 = (bf16[256,1024]{1,0:T(8,128)(2,1)S(1)}, bf16[256,1024]{1,0:T(8,128)(2,1)S(1)}, u32[]{:S(2)}, u32[]{:S(2)}) collective-permute-start(bf16[256,1024]{1,0:T(8,128)(2,1)S(1)} %get-tuple-element.138), channel_id=1, source_target_pairs={{2,0},{4,2},{6,4},{7,6},{5,7},{3,5},{1,3},{0,1},{10,8},{12,10},{14... | collective-permute-start | bytes 1572872 | tf_op jit(solution)/shard_map/ppermute | solution.py:95
  128.9 24.7 %collective-permute-start.32 = (bf16[2,256,1024]{2,1,0:T(8,128)(2,1)S(1)}, bf16[2,256,1024]{2,1,0:T(8,128)(2,1)S(1)}, u32[]{:S(2)}, u32[]{:S(2)}) collective-permute-start(bf16[2,256,1024]{2,1,0:T(8,128)(2,1)S(1)} %get-tuple-element.142), channel_id=1, source_target_pairs={{0,8},{8,0},{16,24},{24,16},{1,9},{9,1},{17,25},{25,17},{2,10},{10... | collective-permute-start | bytes 3145736 | tf_op jit(solution)/shard_map/ppermute | solution.py:117
  129.0 11.2 %collective-permute-start.34 = (bf16[256,1024]{1,0:T(8,128)(2,1)S(1)}, bf16[256,1024]{1,0:T(8,128)(2,1)S(1)}, u32[]{:S(2)}, u32[]{:S(2)}) collective-permute-start(bf16[256,1024]{1,0:T(8,128)(2,1)S(1)} %get-tuple-element.135.refs_0_.refs_3_), channel_id=1, source_target_pairs={{0,8},{8,0},{16,24},{24,16},{1,9},{9,1},{17,25},{25,17},{2,10},{10... | collective-permute-start | bytes 1572872 | tf_op jit(solution)/shard_map/ppermute | solution.py:117
  133.9 6.2 %collective-permute-start.36 = (bf16[256,1024]{1,0:T(8,128)(2,1)S(1)}, bf16[256,1024]{1,0:T(8,128)(2,1)S(1)}, u32[]{:S(2)}, u32[]{:S(2)}) collective-permute-start(bf16[256,1024]{1,0:T(8,128)(2,1)S(1)} %collective-permute-done.35.refs_2_.refs_5_), channel_id=1, source_target_pairs={{0,8},{8,0},{16,24},{24,16},{1,9},{9,1},{17,25},{25,17},{2,10},{10... | collective-permute-start | bytes 1572872 | tf_op jit(solution)/shard_map/ppermute | solution.py:117
  138.1 12.2 %collective-permute-start.39 = (bf16[256,1024]{1,0:T(8,128)(2,1)S(1)}, bf16[256,1024]{1,0:T(8,128)(2,1)S(1)}, u32[]{:S(2)}, u32[]{:S(2)}) collective-permute-start(bf16[256,1024]{1,0:T(8,128)(2,1)S(1)} %get-tuple-element.144), channel_id=1, source_target_pairs={{0,2},{2,4},{4,6},{6,7},{7,5},{5,3},{3,1},{1,0},{8,10},{10,12},{12... | collective-permute-start | bytes 1572872 | tf_op jit(solution)/shard_map/ppermute | solution.py:93
  139.3 11.4 %collective-permute-start.40 = (bf16[256,1024]{1,0:T(8,128)(2,1)S(1)}, bf16[256,1024]{1,0:T(8,128)(2,1)S(1)}, u32[]{:S(2)}, u32[]{:S(2)}) collective-permute-start(bf16[256,1024]{1,0:T(8,128)(2,1)S(1)} %get-tuple-element.145), channel_id=1, source_target_pairs={{2,0},{4,2},{6,4},{7,6},{5,7},{3,5},{1,3},{0,1},{10,8},{12,10},{14... | collective-permute-start | bytes 1572872 | tf_op jit(solution)/shard_map/ppermute | solution.py:95
  151.5 10.7 %collective-permute-start.41 = (bf16[256,1024]{1,0:T(8,128)(2,1)S(1)}, bf16[256,1024]{1,0:T(8,128)(2,1)S(1)}, u32[]{:S(2)}, u32[]{:S(2)}) collective-permute-start(bf16[256,1024]{1,0:T(8,128)(2,1)S(1)} %get-tuple-element.151), channel_id=1, source_target_pairs={{0,2},{2,4},{4,6},{6,7},{7,5},{5,3},{3,1},{1,0},{8,10},{10,12},{12... | collective-permute-start | bytes 1572872 | tf_op jit(solution)/shard_map/ppermute | solution.py:93
  152.4 10.7 %collective-permute-start.42 = (bf16[256,1024]{1,0:T(8,128)(2,1)S(1)}, bf16[256,1024]{1,0:T(8,128)(2,1)S(1)}, u32[]{:S(2)}, u32[]{:S(2)}) collective-permute-start(bf16[256,1024]{1,0:T(8,128)(2,1)S(1)} %get-tuple-element.152), channel_id=1, source_target_pairs={{2,0},{4,2},{6,4},{7,6},{5,7},{3,5},{1,3},{0,1},{10,8},{12,10},{14... | collective-permute-start | bytes 1572872 | tf_op jit(solution)/shard_map/ppermute | solution.py:95
  153.8 12.4 %collective-permute-start.33 = (bf16[1,256,1024]{2,1,0:T(8,128)(2,1)S(1)}, bf16[1,256,1024]{2,1,0:T(8,128)(2,1)S(1)}, u32[]{:S(2)}, u32[]{:S(2)}) collective-permute-start(bf16[1,256,1024]{2,1,0:T(8,128)(2,1)S(1)} %add_convert_fusion.1), channel_id=1, source_target_pairs={{0,16},{8,24},{16,0},{24,8},{1,17},{9,25},{17,1},{25,9},{2,18},{10... | collective-permute-start | bytes 1572872 | tf_op jit(solution)/shard_map/ppermute | solution.py:117
  163.9 12.2 %collective-permute-start.44 = (bf16[256,1024]{1,0:T(8,128)(2,1)S(1)}, bf16[256,1024]{1,0:T(8,128)(2,1)S(1)}, u32[]{:S(2)}, u32[]{:S(2)}) collective-permute-start(bf16[256,1024]{1,0:T(8,128)(2,1)S(1)} %shard_map.275.refs_0_), channel_id=1, source_target_pairs={{0,16},{8,24},{16,0},{24,8},{1,17},{9,25},{17,1},{25,9},{2,18},{10... | collective-permute-start | bytes 1572872 | tf_op jit(solution)/shard_map/ppermute | solution.py:117
  170.7 5.4 %collective-permute-start.45 = (bf16[80,1024]{1,0:T(8,128)(2,1)S(1)}, bf16[80,1024]{1,0:T(8,128)(2,1)S(1)}, u32[]{:S(2)}, u32[]{:S(2)}) collective-permute-start(bf16[80,1024]{1,0:T(8,128)(2,1)S(1)} %slice_bitcast_fusion.2), channel_id=1, source_target_pairs={{2,0},{4,2},{6,4},{7,6},{5,7},{3,5},{1,3},{0,1},{10,8},{12,10},{14... | collective-permute-start | bytes 491528 | tf_op jit(solution)/shard_map/ppermute | solution.py:95
  171.0 5.0 %collective-permute-start.43 = (bf16[64,1024]{1,0:T(8,128)(2,1)S(1)}, bf16[64,1024]{1,0:T(8,128)(2,1)S(1)}, u32[]{:S(2)}, u32[]{:S(2)}) collective-permute-start(bf16[64,1024]{1,0:T(8,128)(2,1)S(1)} %slice_bitcast_fusion.3), channel_id=1, source_target_pairs={{0,2},{2,4},{4,6},{6,7},{7,5},{5,3},{3,1},{1,0},{8,10},{10,12},{12... | collective-permute-start | bytes 393224 | tf_op jit(solution)/shard_map/ppermute | solution.py:93
  179.3 7.2 %collective-permute-start.46 = (bf16[2,256,1024]{2,1,0:T(8,128)(2,1)S(1)}, bf16[2,256,1024]{2,1,0:T(8,128)(2,1)S(1)}, u32[]{:S(2)}, u32[]{:S(2)}) collective-permute-start(bf16[2,256,1024]{2,1,0:T(8,128)(2,1)S(1)} %get-tuple-element.173), channel_id=1, source_target_pairs={{0,8},{8,0},{16,24},{24,16},{1,9},{9,1},{17,25},{25,17},{2,10},{10... | collective-permute-start | bytes 3145736 | tf_op jit(solution)/shard_map/ppermute | solution.py:117
  179.4 3.7 %collective-permute-start.49 = (bf16[256,1024]{1,0:T(8,128)(2,1)S(1)}, bf16[256,1024]{1,0:T(8,128)(2,1)S(1)}, u32[]{:S(2)}, u32[]{:S(2)}) collective-permute-start(bf16[256,1024]{1,0:T(8,128)(2,1)S(1)} %shard_map.275.refs_0_), channel_id=1, source_target_pairs={{0,8},{8,0},{16,24},{24,16},{1,9},{9,1},{17,25},{25,17},{2,10},{10... | collective-permute-start | bytes 1572872 | tf_op jit(solution)/shard_map/ppermute | solution.py:117
  179.9 3.6 %collective-permute-start.50 = (bf16[256,1024]{1,0:T(8,128)(2,1)S(1)}, bf16[256,1024]{1,0:T(8,128)(2,1)S(1)}, u32[]{:S(2)}, u32[]{:S(2)}) collective-permute-start(bf16[256,1024]{1,0:T(8,128)(2,1)S(1)} %collective-permute-done.44.refs_2_), channel_id=1, source_target_pairs={{0,8},{8,0},{16,24},{24,16},{1,9},{9,1},{17,25},{25,17},{2,10},{10... | collective-permute-start | bytes 1572872 | tf_op jit(solution)/shard_map/ppermute | solution.py:117
  179.9 9.4 %collective-permute-start.48 = (bf16[144,1024]{1,0:T(8,128)(2,1)S(1)}, bf16[144,1024]{1,0:T(8,128)(2,1)S(1)}, u32[]{:S(2)}, u32[]{:S(2)}) collective-permute-start(bf16[144,1024]{1,0:T(8,128)(2,1)S(1)} %get-tuple-element.167), channel_id=1, source_target_pairs={{0,2},{2,4},{4,6},{6,7},{7,5},{5,3},{3,1},{1,0},{8,10},{10,12},{12... | collective-permute-start | bytes 884744 | tf_op jit(solution)/shard_map/ppermute | solution.py:93
  181.7 9.1 %collective-permute-start.51 = (bf16[144,1024]{1,0:T(8,128)(2,1)S(1)}, bf16[144,1024]{1,0:T(8,128)(2,1)S(1)}, u32[]{:S(2)}, u32[]{:S(2)}) collective-permute-start(bf16[144,1024]{1,0:T(8,128)(2,1)S(1)} %get-tuple-element.168), channel_id=1, source_target_pairs={{2,0},{4,2},{6,4},{7,6},{5,7},{3,5},{1,3},{0,1},{10,8},{12,10},{14... | collective-permute-start | bytes 884744 | tf_op jit(solution)/shard_map/ppermute | solution.py:95
  191.5 8.3 %collective-permute-start.52 = (bf16[144,1024]{1,0:T(8,128)(2,1)S(1)}, bf16[144,1024]{1,0:T(8,128)(2,1)S(1)}, u32[]{:S(2)}, u32[]{:S(2)}) collective-permute-start(bf16[144,1024]{1,0:T(8,128)(2,1)S(1)} %get-tuple-element.178), channel_id=1, source_target_pairs={{0,2},{2,4},{4,6},{6,7},{7,5},{5,3},{3,1},{1,0},{8,10},{10,12},{12... | collective-permute-start | bytes 884744 | tf_op jit(solution)/shard_map/ppermute | solution.py:93
  192.3 8.0 %collective-permute-start.53 = (bf16[144,1024]{1,0:T(8,128)(2,1)S(1)}, bf16[144,1024]{1,0:T(8,128)(2,1)S(1)}, u32[]{:S(2)}, u32[]{:S(2)}) collective-permute-start(bf16[144,1024]{1,0:T(8,128)(2,1)S(1)} %get-tuple-element.179), channel_id=1, source_target_pairs={{2,0},{4,2},{6,4},{7,6},{5,7},{3,5},{1,3},{0,1},{10,8},{12,10},{14... | collective-permute-start | bytes 884744 | tf_op jit(solution)/shard_map/ppermute | solution.py:95
  193.5 12.6 %collective-permute-start.47 = (bf16[1,256,1024]{2,1,0:T(8,128)(2,1)S(1)}, bf16[1,256,1024]{2,1,0:T(8,128)(2,1)S(1)}, u32[]{:S(2)}, u32[]{:S(2)}) collective-permute-start(bf16[1,256,1024]{2,1,0:T(8,128)(2,1)S(1)} %add_convert_fusion), channel_id=1, source_target_pairs={{0,16},{8,24},{16,0},{24,8},{1,17},{9,25},{17,1},{25,9},{2,18},{10... | collective-permute-start | bytes 1572872 | tf_op jit(solution)/shard_map/ppermute | solution.py:117
  200.9 7.4 %collective-permute-start.54 = (bf16[144,1024]{1,0:T(8,128)(2,1)S(1)}, bf16[144,1024]{1,0:T(8,128)(2,1)S(1)}, u32[]{:S(2)}, u32[]{:S(2)}) collective-permute-start(bf16[144,1024]{1,0:T(8,128)(2,1)S(1)} %get-tuple-element.180), channel_id=1, source_target_pairs={{0,2},{2,4},{4,6},{6,7},{7,5},{5,3},{3,1},{1,0},{8,10},{10,12},{12... | collective-permute-start | bytes 884744 | tf_op jit(solution)/shard_map/ppermute | solution.py:93
  201.7 6.8 %collective-permute-start.55 = (bf16[144,1024]{1,0:T(8,128)(2,1)S(1)}, bf16[144,1024]{1,0:T(8,128)(2,1)S(1)}, u32[]{:S(2)}, u32[]{:S(2)}) collective-permute-start(bf16[144,1024]{1,0:T(8,128)(2,1)S(1)} %get-tuple-element.181), channel_id=1, source_target_pairs={{2,0},{4,2},{6,4},{7,6},{5,7},{3,5},{1,3},{0,1},{10,8},{12,10},{14... | collective-permute-start | bytes 884744 | tf_op jit(solution)/shard_map/ppermute | solution.py:95
  206.1 13.9 %copy-start.1 = (bf16[512,1024]{1,0:T(8,128)(2,1)S(1)}, bf16[512,1024]{1,0:T(8,128)(2,1)}, u32[]{:S(2)}) copy-start(bf16[512,1024]{1,0:T(8,128)(2,1)} %param.23) | copy-start | bytes 3145732
  209.1 6.8 %collective-permute-start.57 = (bf16[144,1024]{1,0:T(8,128)(2,1)S(1)}, bf16[144,1024]{1,0:T(8,128)(2,1)S(1)}, u32[]{:S(2)}, u32[]{:S(2)}) collective-permute-start(bf16[144,1024]{1,0:T(8,128)(2,1)S(1)} %shard_map.282.refs_0_), channel_id=1, source_target_pairs={{0,16},{8,24},{16,0},{24,8},{1,17},{9,25},{17,1},{25,9},{2,18},{10... | collective-permute-start | bytes 884744 | tf_op jit(solution)/shard_map/ppermute | solution.py:117
  210.6 5.3 %collective-permute-start.56 = (bf16[144,1024]{1,0:T(8,128)(2,1)S(1)}, bf16[144,1024]{1,0:T(8,128)(2,1)S(1)}, u32[]{:S(2)}, u32[]{:S(2)}) collective-permute-start(bf16[144,1024]{1,0:T(8,128)(2,1)S(1)} %shard_map.282.refs_0_), channel_id=1, source_target_pairs={{0,8},{8,0},{16,24},{24,16},{1,9},{9,1},{17,25},{25,17},{2,10},{10... | collective-permute-start | bytes 884744 | tf_op jit(solution)/shard_map/ppermute | solution.py:117
  215.9 1.6 collective-permute-start.58
  (11 other events, 42.3 us)
where the time goes:
time: 220 us
  Pallas kernels  85.3 us (39%)
  waiting for transfers between devices  74 us (34%)
  starting transfers between devices  51.4 us (23%)
  local copies, waits for them, and re-layouts  6.35 us (3%)
    pallas_call x29, Pallas kernels, run(): pl.pallas_call(kernel, out_shape=[jax.ShapeDtypeStruct(o.shape, o.dtype)...  85.3 us
    ppermute x27, waiting for transfers between devices, swap(): return lax.ppermute(value, axis, [(i, i ^ bit) for i in range(count)])  30.2 us
    ppermute x6, waiting for transfers between devices, ring_gather(): left = lax.ppermute(left, 'fsdp', onward)  17.7 us
    ppermute x27, starting transfers between devices, swap(): return lax.ppermute(value, axis, [(i, i ^ bit) for i in range(count)])  17.1 us
    ppermute x8, waiting for transfers between devices, send(): self.left = lax.ppermute(self.left, 'fsdp', self.onward)  13.7 us
    ppermute x6, starting transfers between devices, ring_gather(): left = lax.ppermute(left, 'fsdp', onward)  11 us
    ppermute x8, starting transfers between devices, send(): self.left = lax.ppermute(self.left, 'fsdp', self.onward)  10.1 us
    ppermute x8, starting transfers between devices, send(): self.right = lax.ppermute(self.right, 'fsdp', self.backward)  6.54 us
  transfers between devices with their start and end apart: 59, of which 30 were waited for; matrix products, arithmetic and copies ran while one was open for 2% of the time, Pallas kernels for 31%

commit v1 on v0

--- a/solution.py
+++ b/solution.py
@@ -491,7 +491,7 @@
 def attend(scalars, query, keys, values, query_mask, key_mask, pair, before=()):
     total, share = query.shape
     wide = head_pairs(share)[1]
-    rows = min(total, 256 * STEP // total)
+    rows = min(total, 512 * STEP // total)
     heads = wide // HEAD_DIM
     scale = HEAD_DIM**-0.5
 
@@ -710,7 +710,7 @@
 def outer(scalars, left, right, count):
     total, height = left.shape
     width = right.shape[1]
-    rows = min(height, 256)
+    rows = min(height, 512)
     piece = height // count
 
     def kernel(places, left_ref, right_ref, out):
@@ -869,7 +869,7 @@
 ):
     total, width = normed.shape
     share = mixed[0].shape[1]
-    rows = max(min(width, 256 * STEP // total), 128)
+    rows = max(min(width, 512 * STEP // total), 128)
     piece = width // count
     units = up_sums.shape[1] // count
     block_rows = branches[0].shape[0]

time: 220 us -> 219 us (level)
  Pallas kernels: 85.3 us -> 82.5 us
    pallas_call x29, Pallas kernels: 85.3 us -> 82.5 us  [run(): pl.pallas_call(kernel, out_shape=[jax.ShapeDtypeStruct(o.shape, o.dtype)...]
  transfers between devices with their start and end apart: 59 -> 59, of which waited for: 30 -> 29; matrix products, arithmetic and copies ran while one was open for 2% -> 2% of each run, Pallas kernels for 31% -> 30%
where the time goes in v1:
time: 219 us
  Pallas kernels  82.5 us (38%)
  waiting for transfers between devices  74.9 us (34%)
  starting transfers between devices  52 us (24%)
  local copies, waits for them, and re-layouts  6.35 us (3%)
    pallas_call x29, Pallas kernels, run(): pl.pallas_call(kernel, out_shape=[jax.ShapeDtypeStruct(o.shape, o.dtype)...  82.5 us
    ppermute x27, waiting for transfers between devices, swap(): return lax.ppermute(value, axis, [(i, i ^ bit) for i in range(count)])  31.8 us
    ppermute x6, waiting for transfers between devices, ring_gather(): left = lax.ppermute(left, 'fsdp', onward)  18.3 us
    ppermute x27, starting transfers between devices, swap(): return lax.ppermute(value, axis, [(i, i ^ bit) for i in range(count)])  17.7 us
    ppermute x8, waiting for transfers between devices, send(): self.left = lax.ppermute(self.left, 'fsdp', self.onward)  12.8 us
    ppermute x6, starting transfers between devices, ring_gather(): left = lax.ppermute(left, 'fsdp', onward)  11 us
    ppermute x8, starting transfers between devices, send(): self.left = lax.ppermute(self.left, 'fsdp', self.onward)  10.4 us
    ppermute x8, starting transfers between devices, send(): self.right = lax.ppermute(self.right, 'fsdp', self.backward)  6.26 us
  transfers between devices with their start and end apart: 59, of which 29 were waited for; matrix products, arithmetic and copies ran while one was open for 2% of the time, Pallas kernels for 30%

profile of v1, /device:TPU:0, one launch (start us, length us, event | category | flops | bytes accessed | tf_op | source)
XLA Modules:
  0.0 218.7 jit_solution(785986729374586245)
XLA Ops:
  0.7 1.9 shard_map.255.refs_0_
  2.6 3.1 %collective-permute-start.3 = (bf16[144,1024]{1,0:T(8,128)(2,1)}, bf16[144,1024]{1,0:T(8,128)(2,1)S(1)}, u32[]{:S(2)}, u32[]{:S(2)}) collective-permute-start(bf16[144,1024]{1,0:T(8,128)(2,1)} %shard_map.255.refs_0_), channel_id=1, source_target_pairs={{0,2},{2,4},{4,6},{6,7},{7,5},{5,3},{3,1},{1,0},{8,10},{10,12},{12... | collective-permute-start | bytes 884744 | tf_op jit(solution)/shard_map/ppermute | solution.py:68
  5.7 2.0 collective-permute-start.1
  7.7 5.2 %collective-permute-done.3.refs_1_ = bf16[144,1024]{1,0:T(8,128)(2,1)S(1)} collective-permute-done((bf16[144,1024]{1,0:T(8,128)(2,1)}, bf16[144,1024]{1,0:T(8,128)(2,1)S(1)}, u32[]{:S(2)}, u32[]{:S(2)}) %collective-permute-start.3) | collective-permute-done | bytes 294944 | tf_op jit(solution)/shard_map/ppermute | solution.py:68
  12.9 1.5 collective-permute-done.4.refs_2_
  14.4 1.6 collective-permute-start.5
  19.9 2.1 collective-permute-done.5.refs_3_
  22.1 2.0 collective-permute-done.6.refs_4_
  24.1 1.6 collective-permute-start.7
  26.1 5.0 %collective-permute-done.7.refs_5_ = bf16[144,1024]{1,0:T(8,128)(2,1)} collective-permute-done((bf16[144,1024]{1,0:T(8,128)(2,1)}, bf16[144,1024]{1,0:T(8,128)(2,1)}, u32[]{:S(2)}, u32[]{:S(2)}) %collective-permute-start.7) | collective-permute-done | bytes 294944 | tf_op jit(solution)/shard_map/ppermute | solution.py:68
  31.1 1.5 collective-permute-done.8.refs_6_
  32.6 1.5 collective-permute-start.13
  36.2 1.6 collective-permute-start.9
  38.6 1.3 shard_map.258
  40.0 2.0 collective-permute-done.9.refs_7_
  41.9 1.6 collective-permute-start.15
  44.5 1.9 shard_map.256
  46.4 4.7 %shard_map.257 = (bf16[1024,1024]{1,0:T(8,128)(2,1)S(1)}, bf16[1024,256]{1,0:T(8,128)(2,1)S(1)}, bf16[1024,256]{1,0:T(8,128)(2,1)S(1)}, bf16[1024,256]{1,0:T(8,1...) custom-call(s32[18]{0:T(128)S(1)} %dynamic-slice_bitcast_fusion._.pl, ...), custom_call_target="tpu_custom_call" | custom-call | bytes 1024 | tf_op jit(solution)/shard_map/pallas_call | solution.py:142
  51.2 5.4 %shard_map.259 = (bf16[1024,256]{1,0:T(8,128)(2,1)S(1)}, bf16[1024,256]{1,0:T(8,128)(2,1)S(1)}) custom-call(s32[18]{0:T(128)S(1)} %dynamic-slice_bitcast_fusion._.places, bf16[1024,256]{1,0:T(8,128)(2,1)S(1)} %get-tuple-element.119.q_ref, bf16[1024,256]{1,0:T(8,128)(2,1)S(1)} %get-tuple-element.108.k_ref, bf16[1024,256]{1,0:T(8,128)(2,1)S(1)} %get-tuple-element.109.v_ref, ...), custom_call_target="tpu_custom_call" | custom-call | bytes 1024 | tf_op jit(solution)/shard_map/pallas_call | solution.py:142
  57.2 1.6 collective-permute-start.22
  60.4 5.4 %shard_map.261 = (bf16[1024,256]{1,0:T(8,128)(2,1)S(1)}, bf16[1024,256]{1,0:T(8,128)(2,1)S(1)}) custom-call(s32[18]{0:T(128)S(1)} %dynamic-slice_bitcast_fusion._.places, bf16[1024,256]{1,0:T(8,128)(2,1)S(1)} %get-tuple-element.119.q_ref, bf16[1024,256]{1,0:T(8,128)(2,1)S(1)} %get-tuple-element.108.k_ref, ...), custom_call_target="tpu_custom_call", output_to_operand_aliasing={{0}: (6, {}), {1}: (7, {})} | custom-call | bytes 1024 | tf_op jit(solution)/shard_map/pallas_call | solution.py:142
  65.8 1.6 collective-permute-start.18
  67.4 3.8 %collective-permute-done.22.refs_6_ = bf16[256,1024]{1,0:T(8,128)(2,1)S(1)} collective-permute-done((bf16[256,1024]{1,0:T(8,128)(2,1)S(1)}, bf16[256,1024]{1,0:T(8,128)(2,1)S(1)}, u32[]{:S(2)}, u32[]{:S(2)}) %collective-permute-start.22) | collective-permute-done | bytes 524320 | tf_op jit(solution)/shard_map/ppermute | solution.py:68
  71.2 1.6 collective-permute-start.24
  73.8 8.5 %collective-permute-done.18.refs_2_ = bf16[1024,256]{1,0:T(8,128)(2,1)S(1)} collective-permute-done((bf16[1024,256]{1,0:T(8,128)(2,1)S(1)}, bf16[1024,256]{1,0:T(8,128)(2,1)S(1)}, u32[]{:S(2)}, u32[]{:S(2)}) %collective-permute-start.18) | collective-permute-done | bytes 524320 | tf_op jit(solution)/shard_map/ppermute | solution.py:117
  82.2 2.2 %collective-permute-done.24.refs_8_ = bf16[256,1024]{1,0:T(8,128)(2,1)S(1)} collective-permute-done((bf16[256,1024]{1,0:T(8,128)(2,1)S(1)}, bf16[256,1024]{1,0:T(8,128)(2,1)S(1)}, u32[]{:S(2)}, u32[]{:S(2)}) %collective-permute-start.24) | collective-permute-done | bytes 524320 | tf_op jit(solution)/shard_map/ppermute | solution.py:68
  84.5 1.6 collective-permute-start.26
  86.8 5.6 %shard_map.262 = (bf16[1024,1024]{1,0:T(8,128)(2,1)S(1)}, bf16[1024,1024]{1,0:T(8,128)(2,1)S(1)}, f32[256,1024]{1,0:T(8,128)S(1)}) custom-call(s32[18]{0:T(128)S(1)} %dynamic-slice_bitcast_fusion._.places, bf16[1024,256]{1,0:T(8,128)(2,1)S(1)} %get-tuple-element.146.refs_0_.refs_8_, bf16[1024,256]{1,0:T(8,128)(2,1)S(1)} %collective-permute-done.17.refs_1_, ...), custom_call_target="tpu_custom_call" | custom-call | bytes 1024 | tf_op jit(solution)/shard_map/pallas_call | solution.py:142
  92.8 8.3 %shard_map.263 = (bf16[1024,1024]{1,0:T(8,128)(2,1)S(1)}, bf16[1024,1024]{1,0:T(8,128)(2,1)S(1)}, bf16[2,256,1024]{2,1,0:T(8,128)(2,1)S(1)}, bf16[2,256,1024]{2,...) custom-call(s32[18]{0:T(128)S(1)} %dynamic-slice_bitcast_fusion._.places, ...), custom_call_target="tpu_custom_call" | custom-call | bytes 1024 | tf_op jit(solution)/shard_map/pallas_call | solution.py:142
  101.2 2.6 %collective-permute-done.28 = bf16[2,256,1024]{2,1,0:T(8,128)(2,1)S(1)} collective-permute-done((bf16[2,256,1024]{2,1,0:T(8,128)(2,1)S(1)}, bf16[2,256,1024]{2,1,0:T(8,128)(2,1)S(1)}, u32[]{:S(2)}, u32[]{:S(2)}) %collective-permute-start.28) | collective-permute-done | bytes 1048608 | tf_op jit(solution)/shard_map/ppermute | solution.py:117
  104.1 1.6 collective-permute-start.30
  105.6 3.1 %shard_map.264.refs_0_.refs_2_ = bf16[8,128,1024]{2,1,0:T(8,128)(2,1)S(1)} custom-call(s32[18]{0:T(128)S(1)} %dynamic-slice_bitcast_fusion._.places, bf16[1024,1024]{1,0:T(8,128)(2,1)S(1)} %get-tuple-element.133.refs_0_.left_ref, bf16[1024,1024]{1,0:T(8,128)(2,1)S(1)} %get-tuple-element.134.right_ref), custom_call_target="tpu_custom_call" | custom-call | bytes 1024 | tf_op jit(solution)/shard_map/pallas_call | solution.py:142
  108.8 1.5 collective-permute-start.29
  110.3 3.1 %shard_map.265.refs_1_.refs_3_ = bf16[8,128,1024]{2,1,0:T(8,128)(2,1)S(1)} custom-call(s32[18]{0:T(128)S(1)} %dynamic-slice_bitcast_fusion._.places, bf16[1024,1024]{1,0:T(8,128)(2,1)S(1)} %get-tuple-element.139.left_ref.active_ref, bf16[1024,1024]{1,0:T(8,128)(2,1)S(1)} %constant_dynamic-update-slice_fusion.refs_1_.right_ref), custom_call_target="tpu_custom_call" | custom-call | bytes 1024 | tf_op jit(solution)/shard_map/pallas_call | solution.py:142
  114.2 3.9 %collective-permute-done.30.refs_2_ = bf16[1,256,1024]{2,1,0:T(8,128)(2,1)S(1)} collective-permute-done((bf16[1,256,1024]{2,1,0:T(8,128)(2,1)S(1)}, bf16[1,256,1024]{2,1,0:T(8,128)(2,1)S(1)}, u32[]{:S(2)}, u32[]{:S(2)}) %collective-permute-start.30) | collective-permute-done | bytes 524320 | tf_op jit(solution)/shard_map/ppermute | solution.py:117
  118.1 1.9 shard_map.266
  120.0 1.6 collective-permute-start.35
  122.4 1.5 collective-permute-start.37
  124.5 3.0 %shard_map.268 = (bf16[2,256,1024]{2,1,0:T(8,128)(2,1)S(1)}, bf16[2,256,1024]{2,1,0:T(8,128)(2,1)S(1)}) custom-call(s32[18]{0:T(128)S(1)} %dynamic-slice_bitcast_fusion._.places, bf16[1024,1024]{1,0:T(8,128)(2,1)S(1)} %get-tuple-element.139.left_ref.active_ref, bf16[1024,1024]{1,0:T(8,128)(2,1)S(1)} %get-tuple-element.140.down_ref), custom_call_target="tpu_custom_call" | custom-call | bytes 1024 | tf_op jit(solution)/shard_map/pallas_call | solution.py:142
  128.1 5.1 %collective-permute-done.35.refs_2_.refs_5_ = bf16[256,1024]{1,0:T(8,128)(2,1)S(1)} collective-permute-done((bf16[256,1024]{1,0:T(8,128)(2,1)S(1)}, bf16[256,1024]{1,0:T(8,128)(2,1)S(1)}, u32[]{:S(2)}, u32[]{:S(2)}) %collective-permute-start.35) | collective-permute-done | bytes 524320 | tf_op jit(solution)/shard_map/ppermute | solution.py:117
  133.2 2.1 collective-permute-done.37.refs_4_
  137.3 1.3 collective-permute-start.39
  139.4 2.9 %shard_map.270 = (bf16[1024,256]{1,0:T(8,128)(2,1)S(1)}, bf16[1024,256]{1,0:T(8,128)(2,1)S(1)}) custom-call(s32[18]{0:T(128)S(1)} %dynamic-slice_bitcast_fusion._.places, bf16[256,1024]{1,0:T(8,128)(2,1)S(1)} %get-tuple-element.135.refs_0_.refs_3_, bf16[256,1024]{1,0:T(8,128)(2,1)S(1)} %collective-permute-done.34.refs_1_.refs_4_, ...), custom_call_target="tpu_custom_call" | custom-call | bytes 1024 | tf_op jit(solution)/shard_map/pallas_call | solution.py:142
  142.3 7.2 %shard_map.271 = (bf16[1024,256]{1,0:T(8,128)(2,1)S(1)}, bf16[1024,256]{1,0:T(8,128)(2,1)S(1)}, bf16[1024,256]{1,0:T(8,128)(2,1)S(1)}) custom-call(s32[18]{0:T(128)S(1)} %dynamic-slice_bitcast_fusion._.places, bf16[1024,256]{1,0:T(8,128)(2,1)S(1)} %get-tuple-element.119.q_ref, bf16[1024,256]{1,0:T(8,128)(2,1)S(1)} %get-tuple-element.143.qx_ref, ...), custom_call_target="tpu_custom_call" | custom-call | bytes 1024 | tf_op jit(solution)/shard_map/pallas_call | solution.py:142
  154.3 7.2 %shard_map.273 = (bf16[1024,256]{1,0:T(8,128)(2,1)S(1)}, bf16[1024,256]{1,0:T(8,128)(2,1)S(1)}, bf16[1024,256]{1,0:T(8,128)(2,1)S(1)}) custom-call(s32[18]{0:T(128)S(1)} %dynamic-slice_bitcast_fusion._.places, bf16[1024,256]{1,0:T(8,128)(2,1)S(1)} %get-tuple-element.119.q_ref, ...), custom_call_target="tpu_custom_call", output_to_operand_aliasing={{0}: (8, {}), {1}: (9, {}), {2}: (10, {})} | custom-call | bytes 1024 | tf_op jit(solution)/shard_map/pallas_call | solution.py:142
  163.2 2.3 %collective-permute-start.44 = (bf16[256,1024]{1,0:T(8,128)(2,1)S(1)}, bf16[256,1024]{1,0:T(8,128)(2,1)S(1)}, u32[]{:S(2)}, u32[]{:S(2)}) collective-permute-start(bf16[256,1024]{1,0:T(8,128)(2,1)S(1)} %shard_map.275.refs_0_), channel_id=1, source_target_pairs={{0,16},{8,24},{16,0},{24,8},{1,17},{9,25},{17,1},{25,9},{2,18},{10... | collective-permute-start | bytes 1572872 | tf_op jit(solution)/shard_map/ppermute | solution.py:117
  165.5 3.9 %shard_map.274.refs_0_.refs_1_ = bf16[8,144,1024]{2,1,0:T(8,128)(2,1)S(1)} custom-call(s32[18]{0:T(128)S(1)} %dynamic-slice_bitcast_fusion._.places, bf16[1024,1024]{1,0:T(8,128)(2,1)S(1)} %get-tuple-element.160.normed_ref, bf16[1024,1024]{1,0:T(8,128)(2,1)S(1)} %get-tuple-element.161.gathered_ref, bf16[1024,768]{1,0:T(8,128)(2,1)S(1)} %get-tuple-element.162.weight_ref, ...), custom_call_target="tpu_custom_call" | custom-call | bytes 1024 | tf_op jit(solution)/shard_map/pallas_call | solution.py:142
  169.7 1.8 collective-permute-start.43
  171.5 3.2 %collective-permute-done.43.refs_2_ = bf16[64,1024]{1,0:T(8,128)(2,1)S(1)} collective-permute-done((bf16[64,1024]{1,0:T(8,128)(2,1)S(1)}, bf16[64,1024]{1,0:T(8,128)(2,1)S(1)}, u32[]{:S(2)}, u32[]{:S(2)}) %collective-permute-start.43) | collective-permute-done | bytes 131104 | tf_op jit(solution)/shard_map/ppermute | solution.py:93
  175.4 2.6 %shard_map.277 = (bf16[2,256,1024]{2,1,0:T(8,128)(2,1)S(1)}, bf16[2,256,1024]{2,1,0:T(8,128)(2,1)S(1)}) custom-call(s32[18]{0:T(128)S(1)} %dynamic-slice_bitcast_fusion._.places, bf16[1024,256]{1,0:T(8,128)(2,1)S(1)} %get-tuple-element.169.refs_0_.q_ref, bf16[1024,256]{1,0:T(8,128)(2,1)S(1)} %get-tuple-element.170.refs_1_.k_ref, ...), custom_call_target="tpu_custom_call" | custom-call | bytes 1024 | tf_op jit(solution)/shard_map/pallas_call | solution.py:142
  178.7 1.7 collective-permute-start.48
  182.2 2.9 %shard_map.279 = (f32[128,4096]{1,0:T(8,128)}, f32[512,1024]{1,0:T(8,128)}) custom-call(s32[18]{0:T(128)S(1)} %dynamic-slice_bitcast_fusion._.places, bf16[256,1024]{1,0:T(8,128)(2,1)S(1)} %shard_map.275.refs_0_, bf16[256,1024]{1,0:T(8,128)(2,1)S(1)} %collective-permute-done.49.refs_1_, bf16[256,1024]{1,0:T(8,128)(2,1)S(1)} %collective-permute-done.44.refs_2_, ...), custom_call_target="tpu_custom_call" | custom-call | bytes 1024 | tf_op jit(solution)/shard_map/pallas_call | solution.py:142
  185.4 2.7 %collective-permute-done.48.refs_2_ = bf16[144,1024]{1,0:T(8,128)(2,1)S(1)} collective-permute-done((bf16[144,1024]{1,0:T(8,128)(2,1)S(1)}, bf16[144,1024]{1,0:T(8,128)(2,1)S(1)}, u32[]{:S(2)}, u32[]{:S(2)}) %collective-permute-start.48) | collective-permute-done | bytes 294944 | tf_op jit(solution)/shard_map/ppermute | solution.py:93
  188.0 1.5 collective-permute-done.51.refs_3_
  191.0 1.3 collective-permute-start.53
  192.2 1.4 collective-permute-start.47
  193.7 4.8 %collective-permute-done.52.refs_2_ = bf16[144,1024]{1,0:T(8,128)(2,1)S(1)} collective-permute-done((bf16[144,1024]{1,0:T(8,128)(2,1)S(1)}, bf16[144,1024]{1,0:T(8,128)(2,1)S(1)}, u32[]{:S(2)}, u32[]{:S(2)}) %collective-permute-start.52) | collective-permute-done | bytes 294944 | tf_op jit(solution)/shard_map/ppermute | solution.py:93
  200.4 1.3 collective-permute-start.55
  201.8 3.1 %collective-permute-done.47.refs_2_ = bf16[1,256,1024]{2,1,0:T(8,128)(2,1)S(1)} collective-permute-done((bf16[1,256,1024]{2,1,0:T(8,128)(2,1)S(1)}, bf16[1,256,1024]{2,1,0:T(8,128)(2,1)S(1)}, u32[]{:S(2)}, u32[]{:S(2)}) %collective-permute-start.47) | collective-permute-done | bytes 524320 | tf_op jit(solution)/shard_map/ppermute | solution.py:117
  204.9 2.2 %shard_map.278 = bf16[256,1024]{1,0:T(8,128)(2,1)} custom-call(s32[18]{0:T(128)S(1)} %dynamic-slice_bitcast_fusion._.places, bf16[1,256,1024]{2,1,0:T(8,128)(2,1)S(1)} %slice.121.refs_0_, bf16[1,256,1024]{2,1,0:T(8,128)(2,1)S(1)} %slice.141.refs_1_, bf16[1,256,1024]{2,1,0:T(8,128)(2,1)S(1)} %collective-permute-done.47.refs_2_, ...), custom_call_target="tpu_custom_call" | custom-call | bytes 1024 | tf_op jit(solution)/shard_map/pallas_call | solution.py:142
  207.8 1.5 collective-permute-start.57
  209.3 5.3 %collective-permute-done.57.refs_2_ = bf16[144,1024]{1,0:T(8,128)(2,1)S(1)} collective-permute-done((bf16[144,1024]{1,0:T(8,128)(2,1)S(1)}, bf16[144,1024]{1,0:T(8,128)(2,1)S(1)}, u32[]{:S(2)}, u32[]{:S(2)}) %collective-permute-start.57) | collective-permute-done | bytes 294944 | tf_op jit(solution)/shard_map/ppermute | solution.py:117
  214.6 1.6 collective-permute-done.58.refs_3_
  216.2 2.0 shard_map.283
  (140 shorter events, 33.0 us)
Async XLA Ops:
  0.6 37.2 %copy-start = (bf16[512,1024]{1,0:T(8,128)(2,1)S(1)}, bf16[512,1024]{1,0:T(8,128)(2,1)}, u32[]{:S(2)}) copy-start(bf16[512,1024]{1,0:T(8,128)(2,1)} %param.23) | copy-start | bytes 3145732
  0.7 31.9 %copy-start.4 = (bf16[1,256,1024]{2,1,0:T(8,128)(2,1)S(1)}, bf16[1,256,1024]{2,1,0:T(8,128)(2,1)}, u32[]{:S(2)}) copy-start(bf16[1,256,1024]{2,1,0:T(8,128)(2,1)} %param.17) | copy-start | bytes 1572868
  0.7 37.2 %copy-start.2 = (bf16[128,4096]{1,0:T(8,128)(2,1)S(1)}, bf16[128,4096]{1,0:T(8,128)(2,1)}, u32[]{:S(2)}) copy-start(bf16[128,4096]{1,0:T(8,128)(2,1)} %refs_7_) | copy-start | bytes 3145732
  2.6 10.2 %collective-permute-start.3 = (bf16[144,1024]{1,0:T(8,128)(2,1)}, bf16[144,1024]{1,0:T(8,128)(2,1)S(1)}, u32[]{:S(2)}, u32[]{:S(2)}) collective-permute-start(bf16[144,1024]{1,0:T(8,128)(2,1)} %shard_map.255.refs_0_), channel_id=1, source_target_pairs={{0,2},{2,4},{4,6},{6,7},{7,5},{5,3},{3,1},{1,0},{8,10},{10,12},{12... | collective-permute-start | bytes 884744 | tf_op jit(solution)/shard_map/ppermute | solution.py:68
  5.7 8.7 %collective-permute-start.4 = (bf16[144,1024]{1,0:T(8,128)(2,1)}, bf16[144,1024]{1,0:T(8,128)(2,1)S(1)}, u32[]{:S(2)}, u32[]{:S(2)}) collective-permute-start(bf16[144,1024]{1,0:T(8,128)(2,1)} %shard_map.255.refs_0_), channel_id=1, source_target_pairs={{2,0},{4,2},{6,4},{7,6},{5,7},{3,5},{1,3},{0,1},{10,8},{12,10},{14... | collective-permute-start | bytes 884744 | tf_op jit(solution)/shard_map/ppermute | solution.py:69
  5.7 13.4 %collective-permute-start.1 = (bf16[256,1024]{1,0:T(8,128)(2,1)S(1)}, bf16[256,1024]{1,0:T(8,128)(2,1)S(1)}, u32[]{:S(2)}, u32[]{:S(2)}) collective-permute-start(bf16[256,1024]{1,0:T(8,128)(2,1)S(1)} %bitcast.39), channel_id=1, source_target_pairs={{0,16},{8,24},{16,0},{24,8},{1,17},{9,25},{17,1},{25,9},{2,18},{10... | collective-permute-start | bytes 1572872 | tf_op jit(solution)/shard_map/ppermute | solution.py:117
  7.7 11.4 %collective-permute-start = (bf16[256,1024]{1,0:T(8,128)(2,1)S(1)}, bf16[256,1024]{1,0:T(8,128)(2,1)S(1)}, u32[]{:S(2)}, u32[]{:S(2)}) collective-permute-start(bf16[256,1024]{1,0:T(8,128)(2,1)S(1)} %bitcast.40), channel_id=1, source_target_pairs={{0,8},{8,0},{16,24},{24,16},{1,9},{9,1},{17,25},{25,17},{2,10},{10... | collective-permute-start | bytes 1572872 | tf_op jit(solution)/shard_map/ppermute | solution.py:117
  14.4 7.7 %collective-permute-start.5 = (bf16[144,1024]{1,0:T(8,128)(2,1)S(1)}, bf16[144,1024]{1,0:T(8,128)(2,1)}, u32[]{:S(2)}, u32[]{:S(2)}) collective-permute-start(bf16[144,1024]{1,0:T(8,128)(2,1)S(1)} %collective-permute-done.3.refs_1_), channel_id=1, source_target_pairs={{0,2},{2,4},{4,6},{6,7},{7,5},{5,3},{3,1},{1,0},{8,10},{10,12},{12... | collective-permute-start | bytes 884744 | tf_op jit(solution)/shard_map/ppermute | solution.py:68
  16.7 7.4 %collective-permute-start.6 = (bf16[144,1024]{1,0:T(8,128)(2,1)S(1)}, bf16[144,1024]{1,0:T(8,128)(2,1)}, u32[]{:S(2)}, u32[]{:S(2)}) collective-permute-start(bf16[144,1024]{1,0:T(8,128)(2,1)S(1)} %collective-permute-done.4.refs_2_), channel_id=1, source_target_pairs={{2,0},{4,2},{6,4},{7,6},{5,7},{3,5},{1,3},{0,1},{10,8},{12,10},{14... | collective-permute-start | bytes 884744 | tf_op jit(solution)/shard_map/ppermute | solution.py:69
  24.1 7.0 %collective-permute-start.7 = (bf16[144,1024]{1,0:T(8,128)(2,1)}, bf16[144,1024]{1,0:T(8,128)(2,1)}, u32[]{:S(2)}, u32[]{:S(2)}) collective-permute-start(bf16[144,1024]{1,0:T(8,128)(2,1)} %collective-permute-done.5.refs_3_), channel_id=1, source_target_pairs={{0,2},{2,4},{4,6},{6,7},{7,5},{5,3},{3,1},{1,0},{8,10},{10,12},{12... | collective-permute-start | bytes 884744 | tf_op jit(solution)/shard_map/ppermute | solution.py:68
  25.7 6.9 %collective-permute-start.8 = (bf16[144,1024]{1,0:T(8,128)(2,1)}, bf16[144,1024]{1,0:T(8,128)(2,1)S(1)}, u32[]{:S(2)}, u32[]{:S(2)}) collective-permute-start(bf16[144,1024]{1,0:T(8,128)(2,1)} %collective-permute-done.6.refs_4_), channel_id=1, source_target_pairs={{2,0},{4,2},{6,4},{7,6},{5,7},{3,5},{1,3},{0,1},{10,8},{12,10},{14... | collective-permute-start | bytes 884744 | tf_op jit(solution)/shard_map/ppermute | solution.py:69
  32.6 11.4 %collective-permute-start.13 = (bf16[256,1024]{1,0:T(8,128)(2,1)S(1)}, bf16[256,1024]{1,0:T(8,128)(2,1)}, u32[]{:S(2)}, u32[]{:S(2)}) collective-permute-start(bf16[256,1024]{1,0:T(8,128)(2,1)S(1)} %bitcast.43), channel_id=1, source_target_pairs={{0,16},{8,24},{16,0},{24,8},{1,17},{9,25},{17,1},{25,9},{2,18},{10... | collective-permute-start | bytes 1572872 | tf_op jit(solution)/shard_map/ppermute | solution.py:117
  34.8 9.7 %collective-permute-start.2 = (bf16[256,1024]{1,0:T(8,128)(2,1)}, bf16[256,1024]{1,0:T(8,128)(2,1)S(1)}, u32[]{:S(2)}, u32[]{:S(2)}) collective-permute-start(bf16[256,1024]{1,0:T(8,128)(2,1)} %copy-done.6), channel_id=1, source_target_pairs={{0,8},{8,0},{16,24},{24,16},{1,9},{9,1},{17,25},{25,17},{2,10},{10... | collective-permute-start | bytes 1572872 | tf_op jit(solution)/shard_map/ppermute | solution.py:117
  34.8 7.1 %collective-permute-start.10 = (bf16[80,1024]{1,0:T(8,128)(2,1)S(1)}, bf16[80,1024]{1,0:T(8,128)(2,1)S(1)}, u32[]{:S(2)}, u32[]{:S(2)}) collective-permute-start(bf16[80,1024]{1,0:T(8,128)(2,1)S(1)} %slice.132), channel_id=1, source_target_pairs={{2,0},{4,2},{6,4},{7,6},{5,7},{3,5},{1,3},{0,1},{10,8},{12,10},{14... | collective-permute-start | bytes 491528 | tf_op jit(solution)/shard_map/ppermute | solution.py:75
  36.2 5.7 %collective-permute-start.9 = (bf16[64,1024]{1,0:T(8,128)(2,1)S(1)}, bf16[64,1024]{1,0:T(8,128)(2,1)S(1)}, u32[]{:S(2)}, u32[]{:S(2)}) collective-permute-start(bf16[64,1024]{1,0:T(8,128)(2,1)S(1)} %slice.131), channel_id=1, source_target_pairs={{0,2},{2,4},{4,6},{6,7},{7,5},{5,3},{3,1},{1,0},{8,10},{10,12},{12... | collective-permute-start | bytes 393224 | tf_op jit(solution)/shard_map/ppermute | solution.py:73
  38.6 7.8 %copy-start.13 = (bf16[144,1024]{1,0:T(8,128)(2,1)S(1)}, bf16[144,1024]{1,0:T(8,128)(2,1)}, u32[]{:S(2)}) copy-start(bf16[144,1024]{1,0:T(8,128)(2,1)} %copy-done.12) | copy-start | bytes 884740
  41.9 14.7 %collective-permute-start.15 = (bf16[256,1024]{1,0:T(8,128)(2,1)S(1)}, bf16[256,1024]{1,0:T(8,128)(2,1)S(1)}, u32[]{:S(2)}, u32[]{:S(2)}) collective-permute-start(bf16[256,1024]{1,0:T(8,128)(2,1)S(1)} %pad_maximum_fusion.refs_3_), channel_id=1, source_target_pairs={{0,2},{2,4},{4,6},{6,7},{7,5},{5,3},{3,1},{1,0},{8,10},{10,12},{12... | collective-permute-start | bytes 1572872 | tf_op jit(solution)/shard_map/ppermute | solution.py:68
  43.5 13.7 %collective-permute-start.16 = (bf16[256,1024]{1,0:T(8,128)(2,1)S(1)}, bf16[256,1024]{1,0:T(8,128)(2,1)S(1)}, u32[]{:S(2)}, u32[]{:S(2)}) collective-permute-start(bf16[256,1024]{1,0:T(8,128)(2,1)S(1)} %pad_maximum_fusion.refs_3_), channel_id=1, source_target_pairs={{2,0},{4,2},{6,4},{7,6},{5,7},{3,5},{1,3},{0,1},{10,8},{12,10},{14... | collective-permute-start | bytes 1572872 | tf_op jit(solution)/shard_map/ppermute | solution.py:69
  44.0 14.8 %collective-permute-start.12 = (bf16[256,1024]{1,0:T(8,128)(2,1)S(1)}, bf16[256,1024]{1,0:T(8,128)(2,1)S(1)}, u32[]{:S(2)}, u32[]{:S(2)}) collective-permute-start(bf16[256,1024]{1,0:T(8,128)(2,1)S(1)} %bitcast.44), channel_id=1, source_target_pairs={{0,8},{8,0},{16,24},{24,16},{1,9},{9,1},{17,25},{25,17},{2,10},{10... | collective-permute-start | bytes 1572872 | tf_op jit(solution)/shard_map/ppermute | solution.py:117
  44.0 16.4 %collective-permute-start.14 = (bf16[256,1024]{1,0:T(8,128)(2,1)}, bf16[256,1024]{1,0:T(8,128)(2,1)S(1)}, u32[]{:S(2)}, u32[]{:S(2)}) collective-permute-start(bf16[256,1024]{1,0:T(8,128)(2,1)} %collective-permute-done.13), channel_id=1, source_target_pairs={{0,8},{8,0},{16,24},{24,16},{1,9},{9,1},{17,25},{25,17},{2,10},{10... | collective-permute-start | bytes 1572872 | tf_op jit(solution)/shard_map/ppermute | solution.py:117
  51.1 9.3 %collective-permute-start.11 = (bf16[1024,256]{1,0:T(8,128)(2,1)S(1)}, bf16[1024,256]{1,0:T(8,128)(2,1)S(1)}, u32[]{:S(2)}, u32[]{:S(2)}) collective-permute-start(bf16[1024,256]{1,0:T(8,128)(2,1)S(1)} %get-tuple-element.107.refs_6_.refs_4_), channel_id=1, source_target_pairs={{0,8},{8,0},{16,24},{24,16},{1,9},{9,1},{17,25},{25,17},{2,10},{10... | collective-permute-start | bytes 1572872 | tf_op jit(solution)/shard_map/ppermute | solution.py:117
  56.6 16.6 %collective-permute-start.20 = (bf16[1024,256]{1,0:T(8,128)(2,1)S(1)}, bf16[1024,256]{1,0:T(8,128)(2,1)S(1)}, u32[]{:S(2)}, u32[]{:S(2)}) collective-permute-start(bf16[1024,256]{1,0:T(8,128)(2,1)S(1)} %get-tuple-element.107.refs_6_.refs_4_), channel_id=1, source_target_pairs={{0,16},{8,24},{16,0},{24,8},{1,17},{9,25},{17,1},{25,9},{2,18},{10... | collective-permute-start | bytes 1572872 | tf_op jit(solution)/shard_map/ppermute | solution.py:117
  57.2 14.0 %collective-permute-start.22 = (bf16[256,1024]{1,0:T(8,128)(2,1)S(1)}, bf16[256,1024]{1,0:T(8,128)(2,1)S(1)}, u32[]{:S(2)}, u32[]{:S(2)}) collective-permute-start(bf16[256,1024]{1,0:T(8,128)(2,1)S(1)} %collective-permute-done.15.refs_4_), channel_id=1, source_target_pairs={{0,2},{2,4},{4,6},{6,7},{7,5},{5,3},{3,1},{1,0},{8,10},{10,12},{12... | collective-permute-start | bytes 1572872 | tf_op jit(solution)/shard_map/ppermute | solution.py:68
  58.8 14.0 %collective-permute-start.23 = (bf16[256,1024]{1,0:T(8,128)(2,1)S(1)}, bf16[256,1024]{1,0:T(8,128)(2,1)S(1)}, u32[]{:S(2)}, u32[]{:S(2)}) collective-permute-start(bf16[256,1024]{1,0:T(8,128)(2,1)S(1)} %collective-permute-done.16.refs_5_), channel_id=1, source_target_pairs={{2,0},{4,2},{6,4},{7,6},{5,7},{3,5},{1,3},{0,1},{10,8},{12,10},{14... | collective-permute-start | bytes 1572872 | tf_op jit(solution)/shard_map/ppermute | solution.py:69
  65.8 16.4 %collective-permute-start.18 = (bf16[1024,256]{1,0:T(8,128)(2,1)S(1)}, bf16[1024,256]{1,0:T(8,128)(2,1)S(1)}, u32[]{:S(2)}, u32[]{:S(2)}) collective-permute-start(bf16[1024,256]{1,0:T(8,128)(2,1)S(1)} %get-tuple-element.146.refs_0_.refs_8_), channel_id=1, source_target_pairs={{0,16},{8,24},{16,0},{24,8},{1,17},{9,25},{17,1},{25,9},{2,18},{10... | collective-permute-start | bytes 1572872 | tf_op jit(solution)/shard_map/ppermute | solution.py:117
  71.2 13.2 %collective-permute-start.24 = (bf16[256,1024]{1,0:T(8,128)(2,1)S(1)}, bf16[256,1024]{1,0:T(8,128)(2,1)S(1)}, u32[]{:S(2)}, u32[]{:S(2)}) collective-permute-start(bf16[256,1024]{1,0:T(8,128)(2,1)S(1)} %collective-permute-done.22.refs_6_), channel_id=1, source_target_pairs={{0,2},{2,4},{4,6},{6,7},{7,5},{5,3},{3,1},{1,0},{8,10},{10,12},{12... | collective-permute-start | bytes 1572872 | tf_op jit(solution)/shard_map/ppermute | solution.py:68
  72.8 13.3 %collective-permute-start.25 = (bf16[256,1024]{1,0:T(8,128)(2,1)S(1)}, bf16[256,1024]{1,0:T(8,128)(2,1)S(1)}, u32[]{:S(2)}, u32[]{:S(2)}) collective-permute-start(bf16[256,1024]{1,0:T(8,128)(2,1)S(1)} %collective-permute-done.23.refs_7_), channel_id=1, source_target_pairs={{2,0},{4,2},{6,4},{7,6},{5,7},{3,5},{1,3},{0,1},{10,8},{12,10},{14... | collective-permute-start | bytes 1572872 | tf_op jit(solution)/shard_map/ppermute | solution.py:69
  73.3 13.5 %collective-permute-start.21 = (bf16[1024,256]{1,0:T(8,128)(2,1)S(1)}, bf16[1024,256]{1,0:T(8,128)(2,1)S(1)}, u32[]{:S(2)}, u32[]{:S(2)}) collective-permute-start(bf16[1024,256]{1,0:T(8,128)(2,1)S(1)} %collective-permute-done.20.refs_8_.refs_6_), channel_id=1, source_target_pairs={{0,8},{8,0},{16,24},{24,16},{1,9},{9,1},{17,25},{25,17},{2,10},{10... | collective-permute-start | bytes 1572872 | tf_op jit(solution)/shard_map/ppermute | solution.py:117
  73.3 13.5 %collective-permute-start.17 = (bf16[1024,256]{1,0:T(8,128)(2,1)S(1)}, bf16[1024,256]{1,0:T(8,128)(2,1)S(1)}, u32[]{:S(2)}, u32[]{:S(2)}) collective-permute-start(bf16[1024,256]{1,0:T(8,128)(2,1)S(1)} %get-tuple-element.146.refs_0_.refs_8_), channel_id=1, source_target_pairs={{0,8},{8,0},{16,24},{24,16},{1,9},{9,1},{17,25},{25,17},{2,10},{10... | collective-permute-start | bytes 1572872 | tf_op jit(solution)/shard_map/ppermute | solution.py:117
  82.2 4.6 %collective-permute-start.19 = (bf16[1024,256]{1,0:T(8,128)(2,1)S(1)}, bf16[1024,256]{1,0:T(8,128)(2,1)S(1)}, u32[]{:S(2)}, u32[]{:S(2)}) collective-permute-start(bf16[1024,256]{1,0:T(8,128)(2,1)S(1)} %collective-permute-done.18.refs_2_), channel_id=1, source_target_pairs={{0,8},{8,0},{16,24},{24,16},{1,9},{9,1},{17,25},{25,17},{2,10},{10... | collective-permute-start | bytes 1572872 | tf_op jit(solution)/shard_map/ppermute | solution.py:117
  84.5 7.9 %collective-permute-start.26 = (bf16[128,1024]{1,0:T(8,128)(2,1)S(1)}, bf16[128,1024]{1,0:T(8,128)(2,1)S(1)}, u32[]{:S(2)}, u32[]{:S(2)}) collective-permute-start(bf16[128,1024]{1,0:T(8,128)(2,1)S(1)} %slice.133), channel_id=1, source_target_pairs={{0,2},{2,4},{4,6},{6,7},{7,5},{5,3},{3,1},{1,0},{8,10},{10,12},{12... | collective-permute-start | bytes 786440 | tf_op jit(solution)/shard_map/ppermute | solution.py:73
  86.1 6.6 %collective-permute-start.27 = (bf16[128,1024]{1,0:T(8,128)(2,1)S(1)}, bf16[128,1024]{1,0:T(8,128)(2,1)S(1)}, u32[]{:S(2)}, u32[]{:S(2)}) collective-permute-start(bf16[128,1024]{1,0:T(8,128)(2,1)S(1)} %slice.134), channel_id=1, source_target_pairs={{2,0},{4,2},{6,4},{7,6},{5,7},{3,5},{1,3},{0,1},{10,8},{12,10},{14... | collective-permute-start | bytes 786440 | tf_op jit(solution)/shard_map/ppermute | solution.py:75
  101.1 2.7 %collective-permute-start.28 = (bf16[2,256,1024]{2,1,0:T(8,128)(2,1)S(1)}, bf16[2,256,1024]{2,1,0:T(8,128)(2,1)S(1)}, u32[]{:S(2)}, u32[]{:S(2)}) collective-permute-start(bf16[2,256,1024]{2,1,0:T(8,128)(2,1)S(1)} %get-tuple-element.131), channel_id=1, source_target_pairs={{0,8},{8,0},{16,24},{24,16},{1,9},{9,1},{17,25},{25,17},{2,10},{10... | collective-permute-start | bytes 3145736 | tf_op jit(solution)/shard_map/ppermute | solution.py:117
  104.1 14.0 %collective-permute-start.30 = (bf16[1,256,1024]{2,1,0:T(8,128)(2,1)S(1)}, bf16[1,256,1024]{2,1,0:T(8,128)(2,1)S(1)}, u32[]{:S(2)}, u32[]{:S(2)}) collective-permute-start(bf16[1,256,1024]{2,1,0:T(8,128)(2,1)S(1)} %add_convert_fusion.2), channel_id=1, source_target_pairs={{0,16},{8,24},{16,0},{24,8},{1,17},{9,25},{17,1},{25,9},{2,18},{10... | collective-permute-start | bytes 1572872 | tf_op jit(solution)/shard_map/ppermute | solution.py:117
  108.8 12.8 %collective-permute-start.29 = (bf16[128,1024]{1,0:T(8,128)(2,1)S(1)}, bf16[128,1024]{1,0:T(8,128)(2,1)S(1)}, u32[]{:S(2)}, u32[]{:S(2)}) collective-permute-start(bf16[128,1024]{1,0:T(8,128)(2,1)S(1)} %slice_bitcast_fusion.1), channel_id=1, source_target_pairs={{0,2},{2,4},{4,6},{6,7},{7,5},{5,3},{3,1},{1,0},{8,10},{10,12},{12... | collective-permute-start | bytes 786440 | tf_op jit(solution)/shard_map/ppermute | solution.py:93
  113.5 8.1 %collective-permute-start.31 = (bf16[128,1024]{1,0:T(8,128)(2,1)S(1)}, bf16[128,1024]{1,0:T(8,128)(2,1)S(1)}, u32[]{:S(2)}, u32[]{:S(2)}) collective-permute-start(bf16[128,1024]{1,0:T(8,128)(2,1)S(1)} %slice_bitcast_fusion), channel_id=1, source_target_pairs={{2,0},{4,2},{6,4},{7,6},{5,7},{3,5},{1,3},{0,1},{10,8},{12,10},{14... | collective-permute-start | bytes 786440 | tf_op jit(solution)/shard_map/ppermute | solution.py:95
  120.0 13.2 %collective-permute-start.35 = (bf16[256,1024]{1,0:T(8,128)(2,1)S(1)}, bf16[256,1024]{1,0:T(8,128)(2,1)S(1)}, u32[]{:S(2)}, u32[]{:S(2)}) collective-permute-start(bf16[256,1024]{1,0:T(8,128)(2,1)S(1)} %get-tuple-element.135.refs_0_.refs_3_), channel_id=1, source_target_pairs={{0,16},{8,24},{16,0},{24,8},{1,17},{9,25},{17,1},{25,9},{2,18},{10... | collective-permute-start | bytes 1572872 | tf_op jit(solution)/shard_map/ppermute | solution.py:117
  122.4 12.9 %collective-permute-start.37 = (bf16[256,1024]{1,0:T(8,128)(2,1)S(1)}, bf16[256,1024]{1,0:T(8,128)(2,1)S(1)}, u32[]{:S(2)}, u32[]{:S(2)}) collective-permute-start(bf16[256,1024]{1,0:T(8,128)(2,1)S(1)} %get-tuple-element.137), channel_id=1, source_target_pairs={{0,2},{2,4},{4,6},{6,7},{7,5},{5,3},{3,1},{1,0},{8,10},{10,12},{12... | collective-permute-start | bytes 1572872 | tf_op jit(solution)/shard_map/ppermute | solution.py:93
  124.0 12.6 %collective-permute-start.38 = (bf16[256,1024]{1,0:T(8,128)(2,1)S(1)}, bf16[256,1024]{1,0:T(8,128)(2,1)S(1)}, u32[]{:S(2)}, u32[]{:S(2)}) collective-permute-start(bf16[256,1024]{1,0:T(8,128)(2,1)S(1)} %get-tuple-element.138), channel_id=1, source_target_pairs={{2,0},{4,2},{6,4},{7,6},{5,7},{3,5},{1,3},{0,1},{10,8},{12,10},{14... | collective-permute-start | bytes 1572872 | tf_op jit(solution)/shard_map/ppermute | solution.py:95
  127.5 25.3 %collective-permute-start.32 = (bf16[2,256,1024]{2,1,0:T(8,128)(2,1)S(1)}, bf16[2,256,1024]{2,1,0:T(8,128)(2,1)S(1)}, u32[]{:S(2)}, u32[]{:S(2)}) collective-permute-start(bf16[2,256,1024]{2,1,0:T(8,128)(2,1)S(1)} %get-tuple-element.142), channel_id=1, source_target_pairs={{0,8},{8,0},{16,24},{24,16},{1,9},{9,1},{17,25},{25,17},{2,10},{10... | collective-permute-start | bytes 3145736 | tf_op jit(solution)/shard_map/ppermute | solution.py:117
  127.6 11.8 %collective-permute-start.34 = (bf16[256,1024]{1,0:T(8,128)(2,1)S(1)}, bf16[256,1024]{1,0:T(8,128)(2,1)S(1)}, u32[]{:S(2)}, u32[]{:S(2)}) collective-permute-start(bf16[256,1024]{1,0:T(8,128)(2,1)S(1)} %get-tuple-element.135.refs_0_.refs_3_), channel_id=1, source_target_pairs={{0,8},{8,0},{16,24},{24,16},{1,9},{9,1},{17,25},{25,17},{2,10},{10... | collective-permute-start | bytes 1572872 | tf_op jit(solution)/shard_map/ppermute | solution.py:117
  133.2 6.2 %collective-permute-start.36 = (bf16[256,1024]{1,0:T(8,128)(2,1)S(1)}, bf16[256,1024]{1,0:T(8,128)(2,1)S(1)}, u32[]{:S(2)}, u32[]{:S(2)}) collective-permute-start(bf16[256,1024]{1,0:T(8,128)(2,1)S(1)} %collective-permute-done.35.refs_2_.refs_5_), channel_id=1, source_target_pairs={{0,8},{8,0},{16,24},{24,16},{1,9},{9,1},{17,25},{25,17},{2,10},{10... | collective-permute-start | bytes 1572872 | tf_op jit(solution)/shard_map/ppermute | solution.py:117
  137.3 12.2 %collective-permute-start.39 = (bf16[256,1024]{1,0:T(8,128)(2,1)S(1)}, bf16[256,1024]{1,0:T(8,128)(2,1)S(1)}, u32[]{:S(2)}, u32[]{:S(2)}) collective-permute-start(bf16[256,1024]{1,0:T(8,128)(2,1)S(1)} %get-tuple-element.144), channel_id=1, source_target_pairs={{0,2},{2,4},{4,6},{6,7},{7,5},{5,3},{3,1},{1,0},{8,10},{10,12},{12... | collective-permute-start | bytes 1572872 | tf_op jit(solution)/shard_map/ppermute | solution.py:93
  138.6 11.4 %collective-permute-start.40 = (bf16[256,1024]{1,0:T(8,128)(2,1)S(1)}, bf16[256,1024]{1,0:T(8,128)(2,1)S(1)}, u32[]{:S(2)}, u32[]{:S(2)}) collective-permute-start(bf16[256,1024]{1,0:T(8,128)(2,1)S(1)} %get-tuple-element.145), channel_id=1, source_target_pairs={{2,0},{4,2},{6,4},{7,6},{5,7},{3,5},{1,3},{0,1},{10,8},{12,10},{14... | collective-permute-start | bytes 1572872 | tf_op jit(solution)/shard_map/ppermute | solution.py:95
  150.8 10.7 %collective-permute-start.41 = (bf16[256,1024]{1,0:T(8,128)(2,1)S(1)}, bf16[256,1024]{1,0:T(8,128)(2,1)S(1)}, u32[]{:S(2)}, u32[]{:S(2)}) collective-permute-start(bf16[256,1024]{1,0:T(8,128)(2,1)S(1)} %get-tuple-element.151), channel_id=1, source_target_pairs={{0,2},{2,4},{4,6},{6,7},{7,5},{5,3},{3,1},{1,0},{8,10},{10,12},{12... | collective-permute-start | bytes 1572872 | tf_op jit(solution)/shard_map/ppermute | solution.py:93
  151.7 10.7 %collective-permute-start.42 = (bf16[256,1024]{1,0:T(8,128)(2,1)S(1)}, bf16[256,1024]{1,0:T(8,128)(2,1)S(1)}, u32[]{:S(2)}, u32[]{:S(2)}) collective-permute-start(bf16[256,1024]{1,0:T(8,128)(2,1)S(1)} %get-tuple-element.152), channel_id=1, source_target_pairs={{2,0},{4,2},{6,4},{7,6},{5,7},{3,5},{1,3},{0,1},{10,8},{12,10},{14... | collective-permute-start | bytes 1572872 | tf_op jit(solution)/shard_map/ppermute | solution.py:95
  153.1 12.4 %collective-permute-start.33 = (bf16[1,256,1024]{2,1,0:T(8,128)(2,1)S(1)}, bf16[1,256,1024]{2,1,0:T(8,128)(2,1)S(1)}, u32[]{:S(2)}, u32[]{:S(2)}) collective-permute-start(bf16[1,256,1024]{2,1,0:T(8,128)(2,1)S(1)} %add_convert_fusion.1), channel_id=1, source_target_pairs={{0,16},{8,24},{16,0},{24,8},{1,17},{9,25},{17,1},{25,9},{2,18},{10... | collective-permute-start | bytes 1572872 | tf_op jit(solution)/shard_map/ppermute | solution.py:117
  163.2 11.6 %collective-permute-start.44 = (bf16[256,1024]{1,0:T(8,128)(2,1)S(1)}, bf16[256,1024]{1,0:T(8,128)(2,1)S(1)}, u32[]{:S(2)}, u32[]{:S(2)}) collective-permute-start(bf16[256,1024]{1,0:T(8,128)(2,1)S(1)} %shard_map.275.refs_0_), channel_id=1, source_target_pairs={{0,16},{8,24},{16,0},{24,8},{1,17},{9,25},{17,1},{25,9},{2,18},{10... | collective-permute-start | bytes 1572872 | tf_op jit(solution)/shard_map/ppermute | solution.py:117
  169.4 5.4 %collective-permute-start.45 = (bf16[80,1024]{1,0:T(8,128)(2,1)S(1)}, bf16[80,1024]{1,0:T(8,128)(2,1)S(1)}, u32[]{:S(2)}, u32[]{:S(2)}) collective-permute-start(bf16[80,1024]{1,0:T(8,128)(2,1)S(1)} %slice_bitcast_fusion.2), channel_id=1, source_target_pairs={{2,0},{4,2},{6,4},{7,6},{5,7},{3,5},{1,3},{0,1},{10,8},{12,10},{14... | collective-permute-start | bytes 491528 | tf_op jit(solution)/shard_map/ppermute | solution.py:95
  169.7 5.0 %collective-permute-start.43 = (bf16[64,1024]{1,0:T(8,128)(2,1)S(1)}, bf16[64,1024]{1,0:T(8,128)(2,1)S(1)}, u32[]{:S(2)}, u32[]{:S(2)}) collective-permute-start(bf16[64,1024]{1,0:T(8,128)(2,1)S(1)} %slice_bitcast_fusion.3), channel_id=1, source_target_pairs={{0,2},{2,4},{4,6},{6,7},{7,5},{5,3},{3,1},{1,0},{8,10},{10,12},{12... | collective-permute-start | bytes 393224 | tf_op jit(solution)/shard_map/ppermute | solution.py:93
  178.0 7.2 %collective-permute-start.46 = (bf16[2,256,1024]{2,1,0:T(8,128)(2,1)S(1)}, bf16[2,256,1024]{2,1,0:T(8,128)(2,1)S(1)}, u32[]{:S(2)}, u32[]{:S(2)}) collective-permute-start(bf16[2,256,1024]{2,1,0:T(8,128)(2,1)S(1)} %get-tuple-element.173), channel_id=1, source_target_pairs={{0,8},{8,0},{16,24},{24,16},{1,9},{9,1},{17,25},{25,17},{2,10},{10... | collective-permute-start | bytes 3145736 | tf_op jit(solution)/shard_map/ppermute | solution.py:117
  178.1 3.7 %collective-permute-start.49 = (bf16[256,1024]{1,0:T(8,128)(2,1)S(1)}, bf16[256,1024]{1,0:T(8,128)(2,1)S(1)}, u32[]{:S(2)}, u32[]{:S(2)}) collective-permute-start(bf16[256,1024]{1,0:T(8,128)(2,1)S(1)} %shard_map.275.refs_0_), channel_id=1, source_target_pairs={{0,8},{8,0},{16,24},{24,16},{1,9},{9,1},{17,25},{25,17},{2,10},{10... | collective-permute-start | bytes 1572872 | tf_op jit(solution)/shard_map/ppermute | solution.py:117
  178.6 3.6 %collective-permute-start.50 = (bf16[256,1024]{1,0:T(8,128)(2,1)S(1)}, bf16[256,1024]{1,0:T(8,128)(2,1)S(1)}, u32[]{:S(2)}, u32[]{:S(2)}) collective-permute-start(bf16[256,1024]{1,0:T(8,128)(2,1)S(1)} %collective-permute-done.44.refs_2_), channel_id=1, source_target_pairs={{0,8},{8,0},{16,24},{24,16},{1,9},{9,1},{17,25},{25,17},{2,10},{10... | collective-permute-start | bytes 1572872 | tf_op jit(solution)/shard_map/ppermute | solution.py:117
  178.7 9.4 %collective-permute-start.48 = (bf16[144,1024]{1,0:T(8,128)(2,1)S(1)}, bf16[144,1024]{1,0:T(8,128)(2,1)S(1)}, u32[]{:S(2)}, u32[]{:S(2)}) collective-permute-start(bf16[144,1024]{1,0:T(8,128)(2,1)S(1)} %get-tuple-element.167), channel_id=1, source_target_pairs={{0,2},{2,4},{4,6},{6,7},{7,5},{5,3},{3,1},{1,0},{8,10},{10,12},{12... | collective-permute-start | bytes 884744 | tf_op jit(solution)/shard_map/ppermute | solution.py:93
  180.4 9.1 %collective-permute-start.51 = (bf16[144,1024]{1,0:T(8,128)(2,1)S(1)}, bf16[144,1024]{1,0:T(8,128)(2,1)S(1)}, u32[]{:S(2)}, u32[]{:S(2)}) collective-permute-start(bf16[144,1024]{1,0:T(8,128)(2,1)S(1)} %get-tuple-element.168), channel_id=1, source_target_pairs={{2,0},{4,2},{6,4},{7,6},{5,7},{3,5},{1,3},{0,1},{10,8},{12,10},{14... | collective-permute-start | bytes 884744 | tf_op jit(solution)/shard_map/ppermute | solution.py:95
  190.2 8.3 %collective-permute-start.52 = (bf16[144,1024]{1,0:T(8,128)(2,1)S(1)}, bf16[144,1024]{1,0:T(8,128)(2,1)S(1)}, u32[]{:S(2)}, u32[]{:S(2)}) collective-permute-start(bf16[144,1024]{1,0:T(8,128)(2,1)S(1)} %get-tuple-element.178), channel_id=1, source_target_pairs={{0,2},{2,4},{4,6},{6,7},{7,5},{5,3},{3,1},{1,0},{8,10},{10,12},{12... | collective-permute-start | bytes 884744 | tf_op jit(solution)/shard_map/ppermute | solution.py:93
  191.0 8.0 %collective-permute-start.53 = (bf16[144,1024]{1,0:T(8,128)(2,1)S(1)}, bf16[144,1024]{1,0:T(8,128)(2,1)S(1)}, u32[]{:S(2)}, u32[]{:S(2)}) collective-permute-start(bf16[144,1024]{1,0:T(8,128)(2,1)S(1)} %get-tuple-element.179), channel_id=1, source_target_pairs={{2,0},{4,2},{6,4},{7,6},{5,7},{3,5},{1,3},{0,1},{10,8},{12,10},{14... | collective-permute-start | bytes 884744 | tf_op jit(solution)/shard_map/ppermute | solution.py:95
  192.2 12.6 %collective-permute-start.47 = (bf16[1,256,1024]{2,1,0:T(8,128)(2,1)S(1)}, bf16[1,256,1024]{2,1,0:T(8,128)(2,1)S(1)}, u32[]{:S(2)}, u32[]{:S(2)}) collective-permute-start(bf16[1,256,1024]{2,1,0:T(8,128)(2,1)S(1)} %add_convert_fusion), channel_id=1, source_target_pairs={{0,16},{8,24},{16,0},{24,8},{1,17},{9,25},{17,1},{25,9},{2,18},{10... | collective-permute-start | bytes 1572872 | tf_op jit(solution)/shard_map/ppermute | solution.py:117
  199.6 7.4 %collective-permute-start.54 = (bf16[144,1024]{1,0:T(8,128)(2,1)S(1)}, bf16[144,1024]{1,0:T(8,128)(2,1)S(1)}, u32[]{:S(2)}, u32[]{:S(2)}) collective-permute-start(bf16[144,1024]{1,0:T(8,128)(2,1)S(1)} %get-tuple-element.180), channel_id=1, source_target_pairs={{0,2},{2,4},{4,6},{6,7},{7,5},{5,3},{3,1},{1,0},{8,10},{10,12},{12... | collective-permute-start | bytes 884744 | tf_op jit(solution)/shard_map/ppermute | solution.py:93
  200.4 6.8 %collective-permute-start.55 = (bf16[144,1024]{1,0:T(8,128)(2,1)S(1)}, bf16[144,1024]{1,0:T(8,128)(2,1)S(1)}, u32[]{:S(2)}, u32[]{:S(2)}) collective-permute-start(bf16[144,1024]{1,0:T(8,128)(2,1)S(1)} %get-tuple-element.181), channel_id=1, source_target_pairs={{2,0},{4,2},{6,4},{7,6},{5,7},{3,5},{1,3},{0,1},{10,8},{12,10},{14... | collective-permute-start | bytes 884744 | tf_op jit(solution)/shard_map/ppermute | solution.py:95
  204.9 13.8 %copy-start.1 = (bf16[512,1024]{1,0:T(8,128)(2,1)S(1)}, bf16[512,1024]{1,0:T(8,128)(2,1)}, u32[]{:S(2)}) copy-start(bf16[512,1024]{1,0:T(8,128)(2,1)} %param.23) | copy-start | bytes 3145732
  207.8 6.8 %collective-permute-start.57 = (bf16[144,1024]{1,0:T(8,128)(2,1)S(1)}, bf16[144,1024]{1,0:T(8,128)(2,1)S(1)}, u32[]{:S(2)}, u32[]{:S(2)}) collective-permute-start(bf16[144,1024]{1,0:T(8,128)(2,1)S(1)} %shard_map.282.refs_0_), channel_id=1, source_target_pairs={{0,16},{8,24},{16,0},{24,8},{1,17},{9,25},{17,1},{25,9},{2,18},{10... | collective-permute-start | bytes 884744 | tf_op jit(solution)/shard_map/ppermute | solution.py:117
  209.3 5.3 %collective-permute-start.56 = (bf16[144,1024]{1,0:T(8,128)(2,1)S(1)}, bf16[144,1024]{1,0:T(8,128)(2,1)S(1)}, u32[]{:S(2)}, u32[]{:S(2)}) collective-permute-start(bf16[144,1024]{1,0:T(8,128)(2,1)S(1)} %shard_map.282.refs_0_), channel_id=1, source_target_pairs={{0,8},{8,0},{16,24},{24,16},{1,9},{9,1},{17,25},{25,17},{2,10},{10... | collective-permute-start | bytes 884744 | tf_op jit(solution)/shard_map/ppermute | solution.py:117
  214.6 1.6 collective-permute-start.58
  (11 other events, 42.3 us)

commit v2 on v1

--- a/solution.py
+++ b/solution.py
@@ -1219,7 +1219,8 @@
     if fits:
         grad_up, grad_down = place_feed(scalars, feed_parts, strip, unit_strip, groups)
         done += [grad_up, grad_down]
-    attention_sum.advance(sends[-1], *done)
+    attention_sum.advance(sends[-1], *done[:1])
+    attention_sum.advance(*done[1:])
     grad_tokens = tokens_back(scalars, addends, own_tokens, grad_middle, vectors)
     attention_grads = after(attention_sum.finish(), grad_tokens)
 

time: 219 us -> 218 us (level)
  transfers between devices with their start and end apart: 59 -> 59, of which waited for: 29 -> 27; matrix products, arithmetic and copies ran while one was open for 2% -> 2% of each run, Pallas kernels for 30% -> 30%
where the time goes in v2:
time: 218 us
  Pallas kernels  82.5 us (38%)
  waiting for transfers between devices  74.1 us (34%)
  starting transfers between devices  51.9 us (24%)
  local copies, waits for them, and re-layouts  6.35 us (3%)
    pallas_call x29, Pallas kernels, run(): pl.pallas_call(kernel, out_shape=[jax.ShapeDtypeStruct(o.shape, o.dtype)...  82.5 us
    ppermute x27, waiting for transfers between devices, swap(): return lax.ppermute(value, axis, [(i, i ^ bit) for i in range(count)])  31.4 us
    ppermute x6, waiting for transfers between devices, ring_gather(): left = lax.ppermute(left, 'fsdp', onward)  18.3 us
    ppermute x27, starting transfers between devices, swap(): return lax.ppermute(value, axis, [(i, i ^ bit) for i in range(count)])  17.6 us
    ppermute x8, waiting for transfers between devices, send(): self.left = lax.ppermute(self.left, 'fsdp', self.onward)  12.4 us
    ppermute x6, starting transfers between devices, ring_gather(): left = lax.ppermute(left, 'fsdp', onward)  11 us
    ppermute x8, starting transfers between devices, send(): self.left = lax.ppermute(self.left, 'fsdp', self.onward)  10.4 us
    ppermute x8, starting transfers between devices, send(): self.right = lax.ppermute(self.right, 'fsdp', self.backward)  6.26 us
  transfers between devices with their start and end apart: 59, of which 27 were waited for; matrix products, arithmetic and copies ran while one was open for 2% of the time, Pallas kernels for 30%

profile of v2, /device:TPU:0, one launch (start us, length us, event | category | flops | bytes accessed | tf_op | source)
XLA Modules:
  0.0 217.8 jit_solution(6175284277225973371)
XLA Ops:
  0.7 1.9 shard_map.255.refs_0_
  2.6 3.1 %collective-permute-start.3 = (bf16[144,1024]{1,0:T(8,128)(2,1)}, bf16[144,1024]{1,0:T(8,128)(2,1)S(1)}, u32[]{:S(2)}, u32[]{:S(2)}) collective-permute-start(bf16[144,1024]{1,0:T(8,128)(2,1)} %shard_map.255.refs_0_), channel_id=1, source_target_pairs={{0,2},{2,4},{4,6},{6,7},{7,5},{5,3},{3,1},{1,0},{8,10},{10,12},{12... | collective-permute-start | bytes 884744 | tf_op jit(solution)/shard_map/ppermute | solution.py:68
  5.7 2.0 collective-permute-start.1
  7.7 5.2 %collective-permute-done.3.refs_1_ = bf16[144,1024]{1,0:T(8,128)(2,1)S(1)} collective-permute-done((bf16[144,1024]{1,0:T(8,128)(2,1)}, bf16[144,1024]{1,0:T(8,128)(2,1)S(1)}, u32[]{:S(2)}, u32[]{:S(2)}) %collective-permute-start.3) | collective-permute-done | bytes 294944 | tf_op jit(solution)/shard_map/ppermute | solution.py:68
  12.9 1.5 collective-permute-done.4.refs_2_
  14.4 1.6 collective-permute-start.5
  19.9 2.1 collective-permute-done.5.refs_3_
  22.1 2.0 collective-permute-done.6.refs_4_
  24.1 1.6 collective-permute-start.7
  26.1 5.0 %collective-permute-done.7.refs_5_ = bf16[144,1024]{1,0:T(8,128)(2,1)} collective-permute-done((bf16[144,1024]{1,0:T(8,128)(2,1)}, bf16[144,1024]{1,0:T(8,128)(2,1)}, u32[]{:S(2)}, u32[]{:S(2)}) %collective-permute-start.7) | collective-permute-done | bytes 294944 | tf_op jit(solution)/shard_map/ppermute | solution.py:68
  31.1 1.5 collective-permute-done.8.refs_6_
  32.6 1.5 collective-permute-start.13
  36.2 1.6 collective-permute-start.9
  38.6 1.3 shard_map.258
  40.0 2.0 collective-permute-done.9.refs_7_
  41.9 1.6 collective-permute-start.15
  44.5 1.9 shard_map.256
  46.4 4.7 %shard_map.257 = (bf16[1024,1024]{1,0:T(8,128)(2,1)S(1)}, bf16[1024,256]{1,0:T(8,128)(2,1)S(1)}, bf16[1024,256]{1,0:T(8,128)(2,1)S(1)}, bf16[1024,256]{1,0:T(8,1...) custom-call(s32[18]{0:T(128)S(1)} %dynamic-slice_bitcast_fusion._.pl, ...), custom_call_target="tpu_custom_call" | custom-call | bytes 1024 | tf_op jit(solution)/shard_map/pallas_call | solution.py:142
  51.2 5.4 %shard_map.259 = (bf16[1024,256]{1,0:T(8,128)(2,1)S(1)}, bf16[1024,256]{1,0:T(8,128)(2,1)S(1)}) custom-call(s32[18]{0:T(128)S(1)} %dynamic-slice_bitcast_fusion._.places, bf16[1024,256]{1,0:T(8,128)(2,1)S(1)} %get-tuple-element.120.q_ref, bf16[1024,256]{1,0:T(8,128)(2,1)S(1)} %get-tuple-element.109.k_ref, bf16[1024,256]{1,0:T(8,128)(2,1)S(1)} %get-tuple-element.110.v_ref, ...), custom_call_target="tpu_custom_call" | custom-call | bytes 1024 | tf_op jit(solution)/shard_map/pallas_call | solution.py:142
  57.2 1.6 collective-permute-start.22
  60.4 5.4 %shard_map.261 = (bf16[1024,256]{1,0:T(8,128)(2,1)S(1)}, bf16[1024,256]{1,0:T(8,128)(2,1)S(1)}) custom-call(s32[18]{0:T(128)S(1)} %dynamic-slice_bitcast_fusion._.places, bf16[1024,256]{1,0:T(8,128)(2,1)S(1)} %get-tuple-element.120.q_ref, bf16[1024,256]{1,0:T(8,128)(2,1)S(1)} %get-tuple-element.109.k_ref, ...), custom_call_target="tpu_custom_call", output_to_operand_aliasing={{0}: (6, {}), {1}: (7, {})} | custom-call | bytes 1024 | tf_op jit(solution)/shard_map/pallas_call | solution.py:142
  65.8 1.6 collective-permute-start.18
  67.4 3.8 %collective-permute-done.22.refs_6_ = bf16[256,1024]{1,0:T(8,128)(2,1)S(1)} collective-permute-done((bf16[256,1024]{1,0:T(8,128)(2,1)S(1)}, bf16[256,1024]{1,0:T(8,128)(2,1)S(1)}, u32[]{:S(2)}, u32[]{:S(2)}) %collective-permute-start.22) | collective-permute-done | bytes 524320 | tf_op jit(solution)/shard_map/ppermute | solution.py:68
  71.2 1.6 collective-permute-start.24
  73.8 8.5 %collective-permute-done.18.refs_2_ = bf16[1024,256]{1,0:T(8,128)(2,1)S(1)} collective-permute-done((bf16[1024,256]{1,0:T(8,128)(2,1)S(1)}, bf16[1024,256]{1,0:T(8,128)(2,1)S(1)}, u32[]{:S(2)}, u32[]{:S(2)}) %collective-permute-start.18) | collective-permute-done | bytes 524320 | tf_op jit(solution)/shard_map/ppermute | solution.py:117
  82.2 2.2 %collective-permute-done.24.refs_8_ = bf16[256,1024]{1,0:T(8,128)(2,1)S(1)} collective-permute-done((bf16[256,1024]{1,0:T(8,128)(2,1)S(1)}, bf16[256,1024]{1,0:T(8,128)(2,1)S(1)}, u32[]{:S(2)}, u32[]{:S(2)}) %collective-permute-start.24) | collective-permute-done | bytes 524320 | tf_op jit(solution)/shard_map/ppermute | solution.py:68
  84.5 1.6 collective-permute-start.26
  86.8 5.6 %shard_map.262 = (bf16[1024,1024]{1,0:T(8,128)(2,1)S(1)}, bf16[1024,1024]{1,0:T(8,128)(2,1)S(1)}, f32[256,1024]{1,0:T(8,128)S(1)}) custom-call(s32[18]{0:T(128)S(1)} %dynamic-slice_bitcast_fusion._.places, bf16[1024,256]{1,0:T(8,128)(2,1)S(1)} %get-tuple-element.147.refs_0_.refs_8_, bf16[1024,256]{1,0:T(8,128)(2,1)S(1)} %collective-permute-done.17.refs_1_, ...), custom_call_target="tpu_custom_call" | custom-call | bytes 1024 | tf_op jit(solution)/shard_map/pallas_call | solution.py:142
  92.8 8.3 %shard_map.263 = (bf16[1024,1024]{1,0:T(8,128)(2,1)S(1)}, bf16[1024,1024]{1,0:T(8,128)(2,1)S(1)}, bf16[2,256,1024]{2,1,0:T(8,128)(2,1)S(1)}, bf16[2,256,1024]{2,...) custom-call(s32[18]{0:T(128)S(1)} %dynamic-slice_bitcast_fusion._.places, ...), custom_call_target="tpu_custom_call" | custom-call | bytes 1024 | tf_op jit(solution)/shard_map/pallas_call | solution.py:142
  101.2 2.6 %collective-permute-done.28 = bf16[2,256,1024]{2,1,0:T(8,128)(2,1)S(1)} collective-permute-done((bf16[2,256,1024]{2,1,0:T(8,128)(2,1)S(1)}, bf16[2,256,1024]{2,1,0:T(8,128)(2,1)S(1)}, u32[]{:S(2)}, u32[]{:S(2)}) %collective-permute-start.28) | collective-permute-done | bytes 1048608 | tf_op jit(solution)/shard_map/ppermute | solution.py:117
  104.1 1.6 collective-permute-start.30
  105.6 3.1 %shard_map.264.refs_0_.refs_2_ = bf16[8,128,1024]{2,1,0:T(8,128)(2,1)S(1)} custom-call(s32[18]{0:T(128)S(1)} %dynamic-slice_bitcast_fusion._.places, bf16[1024,1024]{1,0:T(8,128)(2,1)S(1)} %get-tuple-element.134.refs_0_.left_ref, bf16[1024,1024]{1,0:T(8,128)(2,1)S(1)} %get-tuple-element.135.right_ref), custom_call_target="tpu_custom_call" | custom-call | bytes 1024 | tf_op jit(solution)/shard_map/pallas_call | solution.py:142
  108.8 1.5 collective-permute-start.29
  110.3 3.1 %shard_map.265.refs_1_.refs_3_ = bf16[8,128,1024]{2,1,0:T(8,128)(2,1)S(1)} custom-call(s32[18]{0:T(128)S(1)} %dynamic-slice_bitcast_fusion._.places, bf16[1024,1024]{1,0:T(8,128)(2,1)S(1)} %get-tuple-element.140.left_ref.active_ref, bf16[1024,1024]{1,0:T(8,128)(2,1)S(1)} %constant_dynamic-update-slice_fusion.refs_1_.right_ref), custom_call_target="tpu_custom_call" | custom-call | bytes 1024 | tf_op jit(solution)/shard_map/pallas_call | solution.py:142
  114.2 3.9 %collective-permute-done.30.refs_2_ = bf16[1,256,1024]{2,1,0:T(8,128)(2,1)S(1)} collective-permute-done((bf16[1,256,1024]{2,1,0:T(8,128)(2,1)S(1)}, bf16[1,256,1024]{2,1,0:T(8,128)(2,1)S(1)}, u32[]{:S(2)}, u32[]{:S(2)}) %collective-permute-start.30) | collective-permute-done | bytes 524320 | tf_op jit(solution)/shard_map/ppermute | solution.py:117
  118.1 1.9 shard_map.266
  120.0 1.6 collective-permute-start.35
  122.4 1.5 collective-permute-start.37
  124.5 3.0 %shard_map.268 = (bf16[2,256,1024]{2,1,0:T(8,128)(2,1)S(1)}, bf16[2,256,1024]{2,1,0:T(8,128)(2,1)S(1)}) custom-call(s32[18]{0:T(128)S(1)} %dynamic-slice_bitcast_fusion._.places, bf16[1024,1024]{1,0:T(8,128)(2,1)S(1)} %get-tuple-element.140.left_ref.active_ref, bf16[1024,1024]{1,0:T(8,128)(2,1)S(1)} %get-tuple-element.141.down_ref), custom_call_target="tpu_custom_call" | custom-call | bytes 1024 | tf_op jit(solution)/shard_map/pallas_call | solution.py:142
  128.1 5.1 %collective-permute-done.35.refs_2_.refs_5_ = bf16[256,1024]{1,0:T(8,128)(2,1)S(1)} collective-permute-done((bf16[256,1024]{1,0:T(8,128)(2,1)S(1)}, bf16[256,1024]{1,0:T(8,128)(2,1)S(1)}, u32[]{:S(2)}, u32[]{:S(2)}) %collective-permute-start.35) | collective-permute-done | bytes 524320 | tf_op jit(solution)/shard_map/ppermute | solution.py:117
  133.2 2.1 collective-permute-done.37.refs_4_
  137.3 1.3 collective-permute-start.39
  139.4 2.9 %shard_map.270 = (bf16[1024,256]{1,0:T(8,128)(2,1)S(1)}, bf16[1024,256]{1,0:T(8,128)(2,1)S(1)}) custom-call(s32[18]{0:T(128)S(1)} %dynamic-slice_bitcast_fusion._.places, bf16[256,1024]{1,0:T(8,128)(2,1)S(1)} %get-tuple-element.136.refs_0_.refs_3_, bf16[256,1024]{1,0:T(8,128)(2,1)S(1)} %collective-permute-done.34.refs_1_.refs_4_, ...), custom_call_target="tpu_custom_call" | custom-call | bytes 1024 | tf_op jit(solution)/shard_map/pallas_call | solution.py:142
  142.3 7.2 %shard_map.271 = (bf16[1024,256]{1,0:T(8,128)(2,1)S(1)}, bf16[1024,256]{1,0:T(8,128)(2,1)S(1)}, bf16[1024,256]{1,0:T(8,128)(2,1)S(1)}) custom-call(s32[18]{0:T(128)S(1)} %dynamic-slice_bitcast_fusion._.places, bf16[1024,256]{1,0:T(8,128)(2,1)S(1)} %get-tuple-element.120.q_ref, bf16[1024,256]{1,0:T(8,128)(2,1)S(1)} %get-tuple-element.144.qx_ref, ...), custom_call_target="tpu_custom_call" | custom-call | bytes 1024 | tf_op jit(solution)/shard_map/pallas_call | solution.py:142
  154.3 7.2 %shard_map.273 = (bf16[1024,256]{1,0:T(8,128)(2,1)S(1)}, bf16[1024,256]{1,0:T(8,128)(2,1)S(1)}, bf16[1024,256]{1,0:T(8,128)(2,1)S(1)}) custom-call(s32[18]{0:T(128)S(1)} %dynamic-slice_bitcast_fusion._.places, bf16[1024,256]{1,0:T(8,128)(2,1)S(1)} %get-tuple-element.120.q_ref, ...), custom_call_target="tpu_custom_call", output_to_operand_aliasing={{0}: (8, {}), {1}: (9, {}), {2}: (10, {})} | custom-call | bytes 1024 | tf_op jit(solution)/shard_map/pallas_call | solution.py:142
  163.2 2.3 %collective-permute-start.44 = (bf16[256,1024]{1,0:T(8,128)(2,1)S(1)}, bf16[256,1024]{1,0:T(8,128)(2,1)S(1)}, u32[]{:S(2)}, u32[]{:S(2)}) collective-permute-start(bf16[256,1024]{1,0:T(8,128)(2,1)S(1)} %shard_map.275.refs_0_), channel_id=1, source_target_pairs={{0,16},{8,24},{16,0},{24,8},{1,17},{9,25},{17,1},{25,9},{2,18},{10... | collective-permute-start | bytes 1572872 | tf_op jit(solution)/shard_map/ppermute | solution.py:117
  165.5 3.9 %shard_map.274.refs_0_.refs_1_ = bf16[8,144,1024]{2,1,0:T(8,128)(2,1)S(1)} custom-call(s32[18]{0:T(128)S(1)} %dynamic-slice_bitcast_fusion._.places, bf16[1024,1024]{1,0:T(8,128)(2,1)S(1)} %get-tuple-element.161.normed_ref, bf16[1024,1024]{1,0:T(8,128)(2,1)S(1)} %get-tuple-element.162.gathered_ref, bf16[1024,768]{1,0:T(8,128)(2,1)S(1)} %get-tuple-element.163.weight_ref, ...), custom_call_target="tpu_custom_call" | custom-call | bytes 1024 | tf_op jit(solution)/shard_map/pallas_call | solution.py:142
  169.7 1.8 collective-permute-start.43
  171.5 3.2 %collective-permute-done.43.refs_2_ = bf16[64,1024]{1,0:T(8,128)(2,1)S(1)} collective-permute-done((bf16[64,1024]{1,0:T(8,128)(2,1)S(1)}, bf16[64,1024]{1,0:T(8,128)(2,1)S(1)}, u32[]{:S(2)}, u32[]{:S(2)}) %collective-permute-start.43) | collective-permute-done | bytes 131104 | tf_op jit(solution)/shard_map/ppermute | solution.py:93
  175.4 2.6 %shard_map.277 = (bf16[2,256,1024]{2,1,0:T(8,128)(2,1)S(1)}, bf16[2,256,1024]{2,1,0:T(8,128)(2,1)S(1)}) custom-call(s32[18]{0:T(128)S(1)} %dynamic-slice_bitcast_fusion._.places, bf16[1024,256]{1,0:T(8,128)(2,1)S(1)} %get-tuple-element.170.refs_0_.q_ref, bf16[1024,256]{1,0:T(8,128)(2,1)S(1)} %get-tuple-element.171.refs_1_.k_ref, ...), custom_call_target="tpu_custom_call" | custom-call | bytes 1024 | tf_op jit(solution)/shard_map/pallas_call | solution.py:142
  178.6 1.7 collective-permute-start.48
  181.9 5.7 %collective-permute-done.48.refs_2_ = bf16[144,1024]{1,0:T(8,128)(2,1)S(1)} collective-permute-done((bf16[144,1024]{1,0:T(8,128)(2,1)S(1)}, bf16[144,1024]{1,0:T(8,128)(2,1)S(1)}, u32[]{:S(2)}, u32[]{:S(2)}) %collective-permute-start.48) | collective-permute-done | bytes 294944 | tf_op jit(solution)/shard_map/ppermute | solution.py:93
  187.6 1.5 collective-permute-done.49.refs_3_
  190.5 1.3 collective-permute-start.53
  191.8 1.4 collective-permute-start.47
  193.3 2.9 %shard_map.280 = (f32[128,4096]{1,0:T(8,128)}, f32[512,1024]{1,0:T(8,128)}) custom-call(s32[18]{0:T(128)S(1)} %dynamic-slice_bitcast_fusion._.places, bf16[256,1024]{1,0:T(8,128)(2,1)S(1)} %shard_map.275.refs_0_, bf16[256,1024]{1,0:T(8,128)(2,1)S(1)} %collective-permute-done.51.refs_1_, bf16[256,1024]{1,0:T(8,128)(2,1)S(1)} %collective-permute-done.44.refs_2_, ...), custom_call_target="tpu_custom_call" | custom-call | bytes 1024 | tf_op jit(solution)/shard_map/pallas_call | solution.py:142
  196.2 1.4 collective-permute-done.50.refs_2_
  199.5 1.3 collective-permute-start.55
  200.9 3.1 %collective-permute-done.47.refs_2_ = bf16[1,256,1024]{2,1,0:T(8,128)(2,1)S(1)} collective-permute-done((bf16[1,256,1024]{2,1,0:T(8,128)(2,1)S(1)}, bf16[1,256,1024]{2,1,0:T(8,128)(2,1)S(1)}, u32[]{:S(2)}, u32[]{:S(2)}) %collective-permute-start.47) | collective-permute-done | bytes 524320 | tf_op jit(solution)/shard_map/ppermute | solution.py:117
  204.0 2.2 %shard_map.278 = bf16[256,1024]{1,0:T(8,128)(2,1)} custom-call(s32[18]{0:T(128)S(1)} %dynamic-slice_bitcast_fusion._.places, bf16[1,256,1024]{2,1,0:T(8,128)(2,1)S(1)} %slice.121.refs_0_, bf16[1,256,1024]{2,1,0:T(8,128)(2,1)S(1)} %slice.141.refs_1_, bf16[1,256,1024]{2,1,0:T(8,128)(2,1)S(1)} %collective-permute-done.47.refs_2_, ...), custom_call_target="tpu_custom_call" | custom-call | bytes 1024 | tf_op jit(solution)/shard_map/pallas_call | solution.py:142
  206.9 1.5 collective-permute-start.57
  208.4 5.3 %collective-permute-done.57.refs_2_ = bf16[144,1024]{1,0:T(8,128)(2,1)S(1)} collective-permute-done((bf16[144,1024]{1,0:T(8,128)(2,1)S(1)}, bf16[144,1024]{1,0:T(8,128)(2,1)S(1)}, u32[]{:S(2)}, u32[]{:S(2)}) %collective-permute-start.57) | collective-permute-done | bytes 294944 | tf_op jit(solution)/shard_map/ppermute | solution.py:117
  213.7 1.6 collective-permute-done.58.refs_3_
  215.3 2.0 shard_map.283
  (140 shorter events, 32.5 us)
Async XLA Ops:
  0.6 37.2 %copy-start = (bf16[512,1024]{1,0:T(8,128)(2,1)S(1)}, bf16[512,1024]{1,0:T(8,128)(2,1)}, u32[]{:S(2)}) copy-start(bf16[512,1024]{1,0:T(8,128)(2,1)} %param.23) | copy-start | bytes 3145732
  0.7 31.9 %copy-start.4 = (bf16[1,256,1024]{2,1,0:T(8,128)(2,1)S(1)}, bf16[1,256,1024]{2,1,0:T(8,128)(2,1)}, u32[]{:S(2)}) copy-start(bf16[1,256,1024]{2,1,0:T(8,128)(2,1)} %param.17) | copy-start | bytes 1572868
  0.7 37.2 %copy-start.2 = (bf16[128,4096]{1,0:T(8,128)(2,1)S(1)}, bf16[128,4096]{1,0:T(8,128)(2,1)}, u32[]{:S(2)}) copy-start(bf16[128,4096]{1,0:T(8,128)(2,1)} %refs_7_) | copy-start | bytes 3145732
  2.6 10.2 %collective-permute-start.3 = (bf16[144,1024]{1,0:T(8,128)(2,1)}, bf16[144,1024]{1,0:T(8,128)(2,1)S(1)}, u32[]{:S(2)}, u32[]{:S(2)}) collective-permute-start(bf16[144,1024]{1,0:T(8,128)(2,1)} %shard_map.255.refs_0_), channel_id=1, source_target_pairs={{0,2},{2,4},{4,6},{6,7},{7,5},{5,3},{3,1},{1,0},{8,10},{10,12},{12... | collective-permute-start | bytes 884744 | tf_op jit(solution)/shard_map/ppermute | solution.py:68
  5.7 8.7 %collective-permute-start.4 = (bf16[144,1024]{1,0:T(8,128)(2,1)}, bf16[144,1024]{1,0:T(8,128)(2,1)S(1)}, u32[]{:S(2)}, u32[]{:S(2)}) collective-permute-start(bf16[144,1024]{1,0:T(8,128)(2,1)} %shard_map.255.refs_0_), channel_id=1, source_target_pairs={{2,0},{4,2},{6,4},{7,6},{5,7},{3,5},{1,3},{0,1},{10,8},{12,10},{14... | collective-permute-start | bytes 884744 | tf_op jit(solution)/shard_map/ppermute | solution.py:69
  5.7 13.4 %collective-permute-start.1 = (bf16[256,1024]{1,0:T(8,128)(2,1)S(1)}, bf16[256,1024]{1,0:T(8,128)(2,1)S(1)}, u32[]{:S(2)}, u32[]{:S(2)}) collective-permute-start(bf16[256,1024]{1,0:T(8,128)(2,1)S(1)} %bitcast.39), channel_id=1, source_target_pairs={{0,16},{8,24},{16,0},{24,8},{1,17},{9,25},{17,1},{25,9},{2,18},{10... | collective-permute-start | bytes 1572872 | tf_op jit(solution)/shard_map/ppermute | solution.py:117
  7.7 11.4 %collective-permute-start = (bf16[256,1024]{1,0:T(8,128)(2,1)S(1)}, bf16[256,1024]{1,0:T(8,128)(2,1)S(1)}, u32[]{:S(2)}, u32[]{:S(2)}) collective-permute-start(bf16[256,1024]{1,0:T(8,128)(2,1)S(1)} %bitcast.40), channel_id=1, source_target_pairs={{0,8},{8,0},{16,24},{24,16},{1,9},{9,1},{17,25},{25,17},{2,10},{10... | collective-permute-start | bytes 1572872 | tf_op jit(solution)/shard_map/ppermute | solution.py:117
  14.4 7.7 %collective-permute-start.5 = (bf16[144,1024]{1,0:T(8,128)(2,1)S(1)}, bf16[144,1024]{1,0:T(8,128)(2,1)}, u32[]{:S(2)}, u32[]{:S(2)}) collective-permute-start(bf16[144,1024]{1,0:T(8,128)(2,1)S(1)} %collective-permute-done.3.refs_1_), channel_id=1, source_target_pairs={{0,2},{2,4},{4,6},{6,7},{7,5},{5,3},{3,1},{1,0},{8,10},{10,12},{12... | collective-permute-start | bytes 884744 | tf_op jit(solution)/shard_map/ppermute | solution.py:68
  16.7 7.4 %collective-permute-start.6 = (bf16[144,1024]{1,0:T(8,128)(2,1)S(1)}, bf16[144,1024]{1,0:T(8,128)(2,1)}, u32[]{:S(2)}, u32[]{:S(2)}) collective-permute-start(bf16[144,1024]{1,0:T(8,128)(2,1)S(1)} %collective-permute-done.4.refs_2_), channel_id=1, source_target_pairs={{2,0},{4,2},{6,4},{7,6},{5,7},{3,5},{1,3},{0,1},{10,8},{12,10},{14... | collective-permute-start | bytes 884744 | tf_op jit(solution)/shard_map/ppermute | solution.py:69
  24.1 7.0 %collective-permute-start.7 = (bf16[144,1024]{1,0:T(8,128)(2,1)}, bf16[144,1024]{1,0:T(8,128)(2,1)}, u32[]{:S(2)}, u32[]{:S(2)}) collective-permute-start(bf16[144,1024]{1,0:T(8,128)(2,1)} %collective-permute-done.5.refs_3_), channel_id=1, source_target_pairs={{0,2},{2,4},{4,6},{6,7},{7,5},{5,3},{3,1},{1,0},{8,10},{10,12},{12... | collective-permute-start | bytes 884744 | tf_op jit(solution)/shard_map/ppermute | solution.py:68
  25.7 6.9 %collective-permute-start.8 = (bf16[144,1024]{1,0:T(8,128)(2,1)}, bf16[144,1024]{1,0:T(8,128)(2,1)S(1)}, u32[]{:S(2)}, u32[]{:S(2)}) collective-permute-start(bf16[144,1024]{1,0:T(8,128)(2,1)} %collective-permute-done.6.refs_4_), channel_id=1, source_target_pairs={{2,0},{4,2},{6,4},{7,6},{5,7},{3,5},{1,3},{0,1},{10,8},{12,10},{14... | collective-permute-start | bytes 884744 | tf_op jit(solution)/shard_map/ppermute | solution.py:69
  32.6 11.4 %collective-permute-start.13 = (bf16[256,1024]{1,0:T(8,128)(2,1)S(1)}, bf16[256,1024]{1,0:T(8,128)(2,1)}, u32[]{:S(2)}, u32[]{:S(2)}) collective-permute-start(bf16[256,1024]{1,0:T(8,128)(2,1)S(1)} %bitcast.43), channel_id=1, source_target_pairs={{0,16},{8,24},{16,0},{24,8},{1,17},{9,25},{17,1},{25,9},{2,18},{10... | collective-permute-start | bytes 1572872 | tf_op jit(solution)/shard_map/ppermute | solution.py:117
  34.8 9.7 %collective-permute-start.2 = (bf16[256,1024]{1,0:T(8,128)(2,1)}, bf16[256,1024]{1,0:T(8,128)(2,1)S(1)}, u32[]{:S(2)}, u32[]{:S(2)}) collective-permute-start(bf16[256,1024]{1,0:T(8,128)(2,1)} %copy-done.6), channel_id=1, source_target_pairs={{0,8},{8,0},{16,24},{24,16},{1,9},{9,1},{17,25},{25,17},{2,10},{10... | collective-permute-start | bytes 1572872 | tf_op jit(solution)/shard_map/ppermute | solution.py:117
  34.8 7.1 %collective-permute-start.10 = (bf16[80,1024]{1,0:T(8,128)(2,1)S(1)}, bf16[80,1024]{1,0:T(8,128)(2,1)S(1)}, u32[]{:S(2)}, u32[]{:S(2)}) collective-permute-start(bf16[80,1024]{1,0:T(8,128)(2,1)S(1)} %slice.132), channel_id=1, source_target_pairs={{2,0},{4,2},{6,4},{7,6},{5,7},{3,5},{1,3},{0,1},{10,8},{12,10},{14... | collective-permute-start | bytes 491528 | tf_op jit(solution)/shard_map/ppermute | solution.py:75
  36.2 5.7 %collective-permute-start.9 = (bf16[64,1024]{1,0:T(8,128)(2,1)S(1)}, bf16[64,1024]{1,0:T(8,128)(2,1)S(1)}, u32[]{:S(2)}, u32[]{:S(2)}) collective-permute-start(bf16[64,1024]{1,0:T(8,128)(2,1)S(1)} %slice.131), channel_id=1, source_target_pairs={{0,2},{2,4},{4,6},{6,7},{7,5},{5,3},{3,1},{1,0},{8,10},{10,12},{12... | collective-permute-start | bytes 393224 | tf_op jit(solution)/shard_map/ppermute | solution.py:73
  38.6 7.8 %copy-start.13 = (bf16[144,1024]{1,0:T(8,128)(2,1)S(1)}, bf16[144,1024]{1,0:T(8,128)(2,1)}, u32[]{:S(2)}) copy-start(bf16[144,1024]{1,0:T(8,128)(2,1)} %copy-done.12) | copy-start | bytes 884740
  41.9 14.7 %collective-permute-start.15 = (bf16[256,1024]{1,0:T(8,128)(2,1)S(1)}, bf16[256,1024]{1,0:T(8,128)(2,1)S(1)}, u32[]{:S(2)}, u32[]{:S(2)}) collective-permute-start(bf16[256,1024]{1,0:T(8,128)(2,1)S(1)} %pad_maximum_fusion.refs_3_), channel_id=1, source_target_pairs={{0,2},{2,4},{4,6},{6,7},{7,5},{5,3},{3,1},{1,0},{8,10},{10,12},{12... | collective-permute-start | bytes 1572872 | tf_op jit(solution)/shard_map/ppermute | solution.py:68
  43.5 13.7 %collective-permute-start.16 = (bf16[256,1024]{1,0:T(8,128)(2,1)S(1)}, bf16[256,1024]{1,0:T(8,128)(2,1)S(1)}, u32[]{:S(2)}, u32[]{:S(2)}) collective-permute-start(bf16[256,1024]{1,0:T(8,128)(2,1)S(1)} %pad_maximum_fusion.refs_3_), channel_id=1, source_target_pairs={{2,0},{4,2},{6,4},{7,6},{5,7},{3,5},{1,3},{0,1},{10,8},{12,10},{14... | collective-permute-start | bytes 1572872 | tf_op jit(solution)/shard_map/ppermute | solution.py:69
  44.0 14.8 %collective-permute-start.12 = (bf16[256,1024]{1,0:T(8,128)(2,1)S(1)}, bf16[256,1024]{1,0:T(8,128)(2,1)S(1)}, u32[]{:S(2)}, u32[]{:S(2)}) collective-permute-start(bf16[256,1024]{1,0:T(8,128)(2,1)S(1)} %bitcast.44), channel_id=1, source_target_pairs={{0,8},{8,0},{16,24},{24,16},{1,9},{9,1},{17,25},{25,17},{2,10},{10... | collective-permute-start | bytes 1572872 | tf_op jit(solution)/shard_map/ppermute | solution.py:117
  44.0 16.4 %collective-permute-start.14 = (bf16[256,1024]{1,0:T(8,128)(2,1)}, bf16[256,1024]{1,0:T(8,128)(2,1)S(1)}, u32[]{:S(2)}, u32[]{:S(2)}) collective-permute-start(bf16[256,1024]{1,0:T(8,128)(2,1)} %collective-permute-done.13), channel_id=1, source_target_pairs={{0,8},{8,0},{16,24},{24,16},{1,9},{9,1},{17,25},{25,17},{2,10},{10... | collective-permute-start | bytes 1572872 | tf_op jit(solution)/shard_map/ppermute | solution.py:117
  51.1 9.3 %collective-permute-start.11 = (bf16[1024,256]{1,0:T(8,128)(2,1)S(1)}, bf16[1024,256]{1,0:T(8,128)(2,1)S(1)}, u32[]{:S(2)}, u32[]{:S(2)}) collective-permute-start(bf16[1024,256]{1,0:T(8,128)(2,1)S(1)} %get-tuple-element.108.refs_6_.refs_4_), channel_id=1, source_target_pairs={{0,8},{8,0},{16,24},{24,16},{1,9},{9,1},{17,25},{25,17},{2,10},{10... | collective-permute-start | bytes 1572872 | tf_op jit(solution)/shard_map/ppermute | solution.py:117
  56.6 16.6 %collective-permute-start.20 = (bf16[1024,256]{1,0:T(8,128)(2,1)S(1)}, bf16[1024,256]{1,0:T(8,128)(2,1)S(1)}, u32[]{:S(2)}, u32[]{:S(2)}) collective-permute-start(bf16[1024,256]{1,0:T(8,128)(2,1)S(1)} %get-tuple-element.108.refs_6_.refs_4_), channel_id=1, source_target_pairs={{0,16},{8,24},{16,0},{24,8},{1,17},{9,25},{17,1},{25,9},{2,18},{10... | collective-permute-start | bytes 1572872 | tf_op jit(solution)/shard_map/ppermute | solution.py:117
  57.2 14.0 %collective-permute-start.22 = (bf16[256,1024]{1,0:T(8,128)(2,1)S(1)}, bf16[256,1024]{1,0:T(8,128)(2,1)S(1)}, u32[]{:S(2)}, u32[]{:S(2)}) collective-permute-start(bf16[256,1024]{1,0:T(8,128)(2,1)S(1)} %collective-permute-done.15.refs_4_), channel_id=1, source_target_pairs={{0,2},{2,4},{4,6},{6,7},{7,5},{5,3},{3,1},{1,0},{8,10},{10,12},{12... | collective-permute-start | bytes 1572872 | tf_op jit(solution)/shard_map/ppermute | solution.py:68
  58.8 14.0 %collective-permute-start.23 = (bf16[256,1024]{1,0:T(8,128)(2,1)S(1)}, bf16[256,1024]{1,0:T(8,128)(2,1)S(1)}, u32[]{:S(2)}, u32[]{:S(2)}) collective-permute-start(bf16[256,1024]{1,0:T(8,128)(2,1)S(1)} %collective-permute-done.16.refs_5_), channel_id=1, source_target_pairs={{2,0},{4,2},{6,4},{7,6},{5,7},{3,5},{1,3},{0,1},{10,8},{12,10},{14... | collective-permute-start | bytes 1572872 | tf_op jit(solution)/shard_map/ppermute | solution.py:69
  65.8 16.4 %collective-permute-start.18 = (bf16[1024,256]{1,0:T(8,128)(2,1)S(1)}, bf16[1024,256]{1,0:T(8,128)(2,1)S(1)}, u32[]{:S(2)}, u32[]{:S(2)}) collective-permute-start(bf16[1024,256]{1,0:T(8,128)(2,1)S(1)} %get-tuple-element.147.refs_0_.refs_8_), channel_id=1, source_target_pairs={{0,16},{8,24},{16,0},{24,8},{1,17},{9,25},{17,1},{25,9},{2,18},{10... | collective-permute-start | bytes 1572872 | tf_op jit(solution)/shard_map/ppermute | solution.py:117
  71.2 13.2 %collective-permute-start.24 = (bf16[256,1024]{1,0:T(8,128)(2,1)S(1)}, bf16[256,1024]{1,0:T(8,128)(2,1)S(1)}, u32[]{:S(2)}, u32[]{:S(2)}) collective-permute-start(bf16[256,1024]{1,0:T(8,128)(2,1)S(1)} %collective-permute-done.22.refs_6_), channel_id=1, source_target_pairs={{0,2},{2,4},{4,6},{6,7},{7,5},{5,3},{3,1},{1,0},{8,10},{10,12},{12... | collective-permute-start | bytes 1572872 | tf_op jit(solution)/shard_map/ppermute | solution.py:68
  72.8 13.3 %collective-permute-start.25 = (bf16[256,1024]{1,0:T(8,128)(2,1)S(1)}, bf16[256,1024]{1,0:T(8,128)(2,1)S(1)}, u32[]{:S(2)}, u32[]{:S(2)}) collective-permute-start(bf16[256,1024]{1,0:T(8,128)(2,1)S(1)} %collective-permute-done.23.refs_7_), channel_id=1, source_target_pairs={{2,0},{4,2},{6,4},{7,6},{5,7},{3,5},{1,3},{0,1},{10,8},{12,10},{14... | collective-permute-start | bytes 1572872 | tf_op jit(solution)/shard_map/ppermute | solution.py:69
  73.3 13.5 %collective-permute-start.21 = (bf16[1024,256]{1,0:T(8,128)(2,1)S(1)}, bf16[1024,256]{1,0:T(8,128)(2,1)S(1)}, u32[]{:S(2)}, u32[]{:S(2)}) collective-permute-start(bf16[1024,256]{1,0:T(8,128)(2,1)S(1)} %collective-permute-done.20.refs_8_.refs_6_), channel_id=1, source_target_pairs={{0,8},{8,0},{16,24},{24,16},{1,9},{9,1},{17,25},{25,17},{2,10},{10... | collective-permute-start | bytes 1572872 | tf_op jit(solution)/shard_map/ppermute | solution.py:117
  73.3 13.5 %collective-permute-start.17 = (bf16[1024,256]{1,0:T(8,128)(2,1)S(1)}, bf16[1024,256]{1,0:T(8,128)(2,1)S(1)}, u32[]{:S(2)}, u32[]{:S(2)}) collective-permute-start(bf16[1024,256]{1,0:T(8,128)(2,1)S(1)} %get-tuple-element.147.refs_0_.refs_8_), channel_id=1, source_target_pairs={{0,8},{8,0},{16,24},{24,16},{1,9},{9,1},{17,25},{25,17},{2,10},{10... | collective-permute-start | bytes 1572872 | tf_op jit(solution)/shard_map/ppermute | solution.py:117
  82.2 4.6 %collective-permute-start.19 = (bf16[1024,256]{1,0:T(8,128)(2,1)S(1)}, bf16[1024,256]{1,0:T(8,128)(2,1)S(1)}, u32[]{:S(2)}, u32[]{:S(2)}) collective-permute-start(bf16[1024,256]{1,0:T(8,128)(2,1)S(1)} %collective-permute-done.18.refs_2_), channel_id=1, source_target_pairs={{0,8},{8,0},{16,24},{24,16},{1,9},{9,1},{17,25},{25,17},{2,10},{10... | collective-permute-start | bytes 1572872 | tf_op jit(solution)/shard_map/ppermute | solution.py:117
  84.5 7.9 %collective-permute-start.26 = (bf16[128,1024]{1,0:T(8,128)(2,1)S(1)}, bf16[128,1024]{1,0:T(8,128)(2,1)S(1)}, u32[]{:S(2)}, u32[]{:S(2)}) collective-permute-start(bf16[128,1024]{1,0:T(8,128)(2,1)S(1)} %slice.133), channel_id=1, source_target_pairs={{0,2},{2,4},{4,6},{6,7},{7,5},{5,3},{3,1},{1,0},{8,10},{10,12},{12... | collective-permute-start | bytes 786440 | tf_op jit(solution)/shard_map/ppermute | solution.py:73
  86.1 6.6 %collective-permute-start.27 = (bf16[128,1024]{1,0:T(8,128)(2,1)S(1)}, bf16[128,1024]{1,0:T(8,128)(2,1)S(1)}, u32[]{:S(2)}, u32[]{:S(2)}) collective-permute-start(bf16[128,1024]{1,0:T(8,128)(2,1)S(1)} %slice.134), channel_id=1, source_target_pairs={{2,0},{4,2},{6,4},{7,6},{5,7},{3,5},{1,3},{0,1},{10,8},{12,10},{14... | collective-permute-start | bytes 786440 | tf_op jit(solution)/shard_map/ppermute | solution.py:75
  101.1 2.7 %collective-permute-start.28 = (bf16[2,256,1024]{2,1,0:T(8,128)(2,1)S(1)}, bf16[2,256,1024]{2,1,0:T(8,128)(2,1)S(1)}, u32[]{:S(2)}, u32[]{:S(2)}) collective-permute-start(bf16[2,256,1024]{2,1,0:T(8,128)(2,1)S(1)} %get-tuple-element.132), channel_id=1, source_target_pairs={{0,8},{8,0},{16,24},{24,16},{1,9},{9,1},{17,25},{25,17},{2,10},{10... | collective-permute-start | bytes 3145736 | tf_op jit(solution)/shard_map/ppermute | solution.py:117
  104.1 14.0 %collective-permute-start.30 = (bf16[1,256,1024]{2,1,0:T(8,128)(2,1)S(1)}, bf16[1,256,1024]{2,1,0:T(8,128)(2,1)S(1)}, u32[]{:S(2)}, u32[]{:S(2)}) collective-permute-start(bf16[1,256,1024]{2,1,0:T(8,128)(2,1)S(1)} %add_convert_fusion.2), channel_id=1, source_target_pairs={{0,16},{8,24},{16,0},{24,8},{1,17},{9,25},{17,1},{25,9},{2,18},{10... | collective-permute-start | bytes 1572872 | tf_op jit(solution)/shard_map/ppermute | solution.py:117
  108.8 12.8 %collective-permute-start.29 = (bf16[128,1024]{1,0:T(8,128)(2,1)S(1)}, bf16[128,1024]{1,0:T(8,128)(2,1)S(1)}, u32[]{:S(2)}, u32[]{:S(2)}) collective-permute-start(bf16[128,1024]{1,0:T(8,128)(2,1)S(1)} %slice_bitcast_fusion.1), channel_id=1, source_target_pairs={{0,2},{2,4},{4,6},{6,7},{7,5},{5,3},{3,1},{1,0},{8,10},{10,12},{12... | collective-permute-start | bytes 786440 | tf_op jit(solution)/shard_map/ppermute | solution.py:93
  113.5 8.1 %collective-permute-start.31 = (bf16[128,1024]{1,0:T(8,128)(2,1)S(1)}, bf16[128,1024]{1,0:T(8,128)(2,1)S(1)}, u32[]{:S(2)}, u32[]{:S(2)}) collective-permute-start(bf16[128,1024]{1,0:T(8,128)(2,1)S(1)} %slice_bitcast_fusion), channel_id=1, source_target_pairs={{2,0},{4,2},{6,4},{7,6},{5,7},{3,5},{1,3},{0,1},{10,8},{12,10},{14... | collective-permute-start | bytes 786440 | tf_op jit(solution)/shard_map/ppermute | solution.py:95
  120.0 13.2 %collective-permute-start.35 = (bf16[256,1024]{1,0:T(8,128)(2,1)S(1)}, bf16[256,1024]{1,0:T(8,128)(2,1)S(1)}, u32[]{:S(2)}, u32[]{:S(2)}) collective-permute-start(bf16[256,1024]{1,0:T(8,128)(2,1)S(1)} %get-tuple-element.136.refs_0_.refs_3_), channel_id=1, source_target_pairs={{0,16},{8,24},{16,0},{24,8},{1,17},{9,25},{17,1},{25,9},{2,18},{10... | collective-permute-start | bytes 1572872 | tf_op jit(solution)/shard_map/ppermute | solution.py:117
  122.4 12.9 %collective-permute-start.37 = (bf16[256,1024]{1,0:T(8,128)(2,1)S(1)}, bf16[256,1024]{1,0:T(8,128)(2,1)S(1)}, u32[]{:S(2)}, u32[]{:S(2)}) collective-permute-start(bf16[256,1024]{1,0:T(8,128)(2,1)S(1)} %get-tuple-element.138), channel_id=1, source_target_pairs={{0,2},{2,4},{4,6},{6,7},{7,5},{5,3},{3,1},{1,0},{8,10},{10,12},{12... | collective-permute-start | bytes 1572872 | tf_op jit(solution)/shard_map/ppermute | solution.py:93
  124.0 12.6 %collective-permute-start.38 = (bf16[256,1024]{1,0:T(8,128)(2,1)S(1)}, bf16[256,1024]{1,0:T(8,128)(2,1)S(1)}, u32[]{:S(2)}, u32[]{:S(2)}) collective-permute-start(bf16[256,1024]{1,0:T(8,128)(2,1)S(1)} %get-tuple-element.139), channel_id=1, source_target_pairs={{2,0},{4,2},{6,4},{7,6},{5,7},{3,5},{1,3},{0,1},{10,8},{12,10},{14... | collective-permute-start | bytes 1572872 | tf_op jit(solution)/shard_map/ppermute | solution.py:95
  127.5 25.3 %collective-permute-start.32 = (bf16[2,256,1024]{2,1,0:T(8,128)(2,1)S(1)}, bf16[2,256,1024]{2,1,0:T(8,128)(2,1)S(1)}, u32[]{:S(2)}, u32[]{:S(2)}) collective-permute-start(bf16[2,256,1024]{2,1,0:T(8,128)(2,1)S(1)} %get-tuple-element.143), channel_id=1, source_target_pairs={{0,8},{8,0},{16,24},{24,16},{1,9},{9,1},{17,25},{25,17},{2,10},{10... | collective-permute-start | bytes 3145736 | tf_op jit(solution)/shard_map/ppermute | solution.py:117
  127.6 11.8 %collective-permute-start.34 = (bf16[256,1024]{1,0:T(8,128)(2,1)S(1)}, bf16[256,1024]{1,0:T(8,128)(2,1)S(1)}, u32[]{:S(2)}, u32[]{:S(2)}) collective-permute-start(bf16[256,1024]{1,0:T(8,128)(2,1)S(1)} %get-tuple-element.136.refs_0_.refs_3_), channel_id=1, source_target_pairs={{0,8},{8,0},{16,24},{24,16},{1,9},{9,1},{17,25},{25,17},{2,10},{10... | collective-permute-start | bytes 1572872 | tf_op jit(solution)/shard_map/ppermute | solution.py:117
  133.2 6.2 %collective-permute-start.36 = (bf16[256,1024]{1,0:T(8,128)(2,1)S(1)}, bf16[256,1024]{1,0:T(8,128)(2,1)S(1)}, u32[]{:S(2)}, u32[]{:S(2)}) collective-permute-start(bf16[256,1024]{1,0:T(8,128)(2,1)S(1)} %collective-permute-done.35.refs_2_.refs_5_), channel_id=1, source_target_pairs={{0,8},{8,0},{16,24},{24,16},{1,9},{9,1},{17,25},{25,17},{2,10},{10... | collective-permute-start | bytes 1572872 | tf_op jit(solution)/shard_map/ppermute | solution.py:117
  137.3 12.2 %collective-permute-start.39 = (bf16[256,1024]{1,0:T(8,128)(2,1)S(1)}, bf16[256,1024]{1,0:T(8,128)(2,1)S(1)}, u32[]{:S(2)}, u32[]{:S(2)}) collective-permute-start(bf16[256,1024]{1,0:T(8,128)(2,1)S(1)} %get-tuple-element.145), channel_id=1, source_target_pairs={{0,2},{2,4},{4,6},{6,7},{7,5},{5,3},{3,1},{1,0},{8,10},{10,12},{12... | collective-permute-start | bytes 1572872 | tf_op jit(solution)/shard_map/ppermute | solution.py:93
  138.6 11.4 %collective-permute-start.40 = (bf16[256,1024]{1,0:T(8,128)(2,1)S(1)}, bf16[256,1024]{1,0:T(8,128)(2,1)S(1)}, u32[]{:S(2)}, u32[]{:S(2)}) collective-permute-start(bf16[256,1024]{1,0:T(8,128)(2,1)S(1)} %get-tuple-element.146), channel_id=1, source_target_pairs={{2,0},{4,2},{6,4},{7,6},{5,7},{3,5},{1,3},{0,1},{10,8},{12,10},{14... | collective-permute-start | bytes 1572872 | tf_op jit(solution)/shard_map/ppermute | solution.py:95
  150.8 10.7 %collective-permute-start.41 = (bf16[256,1024]{1,0:T(8,128)(2,1)S(1)}, bf16[256,1024]{1,0:T(8,128)(2,1)S(1)}, u32[]{:S(2)}, u32[]{:S(2)}) collective-permute-start(bf16[256,1024]{1,0:T(8,128)(2,1)S(1)} %get-tuple-element.152), channel_id=1, source_target_pairs={{0,2},{2,4},{4,6},{6,7},{7,5},{5,3},{3,1},{1,0},{8,10},{10,12},{12... | collective-permute-start | bytes 1572872 | tf_op jit(solution)/shard_map/ppermute | solution.py:93
  151.7 10.7 %collective-permute-start.42 = (bf16[256,1024]{1,0:T(8,128)(2,1)S(1)}, bf16[256,1024]{1,0:T(8,128)(2,1)S(1)}, u32[]{:S(2)}, u32[]{:S(2)}) collective-permute-start(bf16[256,1024]{1,0:T(8,128)(2,1)S(1)} %get-tuple-element.153), channel_id=1, source_target_pairs={{2,0},{4,2},{6,4},{7,6},{5,7},{3,5},{1,3},{0,1},{10,8},{12,10},{14... | collective-permute-start | bytes 1572872 | tf_op jit(solution)/shard_map/ppermute | solution.py:95
  153.1 12.4 %collective-permute-start.33 = (bf16[1,256,1024]{2,1,0:T(8,128)(2,1)S(1)}, bf16[1,256,1024]{2,1,0:T(8,128)(2,1)S(1)}, u32[]{:S(2)}, u32[]{:S(2)}) collective-permute-start(bf16[1,256,1024]{2,1,0:T(8,128)(2,1)S(1)} %add_convert_fusion.1), channel_id=1, source_target_pairs={{0,16},{8,24},{16,0},{24,8},{1,17},{9,25},{17,1},{25,9},{2,18},{10... | collective-permute-start | bytes 1572872 | tf_op jit(solution)/shard_map/ppermute | solution.py:117
  163.2 11.6 %collective-permute-start.44 = (bf16[256,1024]{1,0:T(8,128)(2,1)S(1)}, bf16[256,1024]{1,0:T(8,128)(2,1)S(1)}, u32[]{:S(2)}, u32[]{:S(2)}) collective-permute-start(bf16[256,1024]{1,0:T(8,128)(2,1)S(1)} %shard_map.275.refs_0_), channel_id=1, source_target_pairs={{0,16},{8,24},{16,0},{24,8},{1,17},{9,25},{17,1},{25,9},{2,18},{10... | collective-permute-start | bytes 1572872 | tf_op jit(solution)/shard_map/ppermute | solution.py:117
  169.4 5.4 %collective-permute-start.45 = (bf16[80,1024]{1,0:T(8,128)(2,1)S(1)}, bf16[80,1024]{1,0:T(8,128)(2,1)S(1)}, u32[]{:S(2)}, u32[]{:S(2)}) collective-permute-start(bf16[80,1024]{1,0:T(8,128)(2,1)S(1)} %slice_bitcast_fusion.2), channel_id=1, source_target_pairs={{2,0},{4,2},{6,4},{7,6},{5,7},{3,5},{1,3},{0,1},{10,8},{12,10},{14... | collective-permute-start | bytes 491528 | tf_op jit(solution)/shard_map/ppermute | solution.py:95
  169.7 5.0 %collective-permute-start.43 = (bf16[64,1024]{1,0:T(8,128)(2,1)S(1)}, bf16[64,1024]{1,0:T(8,128)(2,1)S(1)}, u32[]{:S(2)}, u32[]{:S(2)}) collective-permute-start(bf16[64,1024]{1,0:T(8,128)(2,1)S(1)} %slice_bitcast_fusion.3), channel_id=1, source_target_pairs={{0,2},{2,4},{4,6},{6,7},{7,5},{5,3},{3,1},{1,0},{8,10},{10,12},{12... | collective-permute-start | bytes 393224 | tf_op jit(solution)/shard_map/ppermute | solution.py:93
  178.0 3.7 %collective-permute-start.46 = (bf16[2,256,1024]{2,1,0:T(8,128)(2,1)S(1)}, bf16[2,256,1024]{2,1,0:T(8,128)(2,1)S(1)}, u32[]{:S(2)}, u32[]{:S(2)}) collective-permute-start(bf16[2,256,1024]{2,1,0:T(8,128)(2,1)S(1)} %get-tuple-element.174), channel_id=1, source_target_pairs={{0,8},{8,0},{16,24},{24,16},{1,9},{9,1},{17,25},{25,17},{2,10},{10... | collective-permute-start | bytes 3145736 | tf_op jit(solution)/shard_map/ppermute | solution.py:117
  178.1 15.2 %collective-permute-start.51 = (bf16[256,1024]{1,0:T(8,128)(2,1)S(1)}, bf16[256,1024]{1,0:T(8,128)(2,1)S(1)}, u32[]{:S(2)}, u32[]{:S(2)}) collective-permute-start(bf16[256,1024]{1,0:T(8,128)(2,1)S(1)} %shard_map.275.refs_0_), channel_id=1, source_target_pairs={{0,8},{8,0},{16,24},{24,16},{1,9},{9,1},{17,25},{25,17},{2,10},{10... | collective-permute-start | bytes 1572872 | tf_op jit(solution)/shard_map/ppermute | solution.py:117
  178.6 9.0 %collective-permute-start.48 = (bf16[144,1024]{1,0:T(8,128)(2,1)S(1)}, bf16[144,1024]{1,0:T(8,128)(2,1)S(1)}, u32[]{:S(2)}, u32[]{:S(2)}) collective-permute-start(bf16[144,1024]{1,0:T(8,128)(2,1)S(1)} %get-tuple-element.168), channel_id=1, source_target_pairs={{0,2},{2,4},{4,6},{6,7},{7,5},{5,3},{3,1},{1,0},{8,10},{10,12},{12... | collective-permute-start | bytes 884744 | tf_op jit(solution)/shard_map/ppermute | solution.py:93
  180.3 8.7 %collective-permute-start.49 = (bf16[144,1024]{1,0:T(8,128)(2,1)S(1)}, bf16[144,1024]{1,0:T(8,128)(2,1)S(1)}, u32[]{:S(2)}, u32[]{:S(2)}) collective-permute-start(bf16[144,1024]{1,0:T(8,128)(2,1)S(1)} %get-tuple-element.169), channel_id=1, source_target_pairs={{2,0},{4,2},{6,4},{7,6},{5,7},{3,5},{1,3},{0,1},{10,8},{12,10},{14... | collective-permute-start | bytes 884744 | tf_op jit(solution)/shard_map/ppermute | solution.py:95
  181.7 11.5 %collective-permute-start.52 = (bf16[256,1024]{1,0:T(8,128)(2,1)S(1)}, bf16[256,1024]{1,0:T(8,128)(2,1)S(1)}, u32[]{:S(2)}, u32[]{:S(2)}) collective-permute-start(bf16[256,1024]{1,0:T(8,128)(2,1)S(1)} %collective-permute-done.44.refs_2_), channel_id=1, source_target_pairs={{0,8},{8,0},{16,24},{24,16},{1,9},{9,1},{17,25},{25,17},{2,10},{10... | collective-permute-start | bytes 1572872 | tf_op jit(solution)/shard_map/ppermute | solution.py:117
  189.7 7.9 %collective-permute-start.50 = (bf16[144,1024]{1,0:T(8,128)(2,1)S(1)}, bf16[144,1024]{1,0:T(8,128)(2,1)S(1)}, u32[]{:S(2)}, u32[]{:S(2)}) collective-permute-start(bf16[144,1024]{1,0:T(8,128)(2,1)S(1)} %get-tuple-element.177), channel_id=1, source_target_pairs={{0,2},{2,4},{4,6},{6,7},{7,5},{5,3},{3,1},{1,0},{8,10},{10,12},{12... | collective-permute-start | bytes 884744 | tf_op jit(solution)/shard_map/ppermute | solution.py:93
  190.5 7.6 %collective-permute-start.53 = (bf16[144,1024]{1,0:T(8,128)(2,1)S(1)}, bf16[144,1024]{1,0:T(8,128)(2,1)S(1)}, u32[]{:S(2)}, u32[]{:S(2)}) collective-permute-start(bf16[144,1024]{1,0:T(8,128)(2,1)S(1)} %get-tuple-element.181), channel_id=1, source_target_pairs={{2,0},{4,2},{6,4},{7,6},{5,7},{3,5},{1,3},{0,1},{10,8},{12,10},{14... | collective-permute-start | bytes 884744 | tf_op jit(solution)/shard_map/ppermute | solution.py:95
  191.8 12.2 %collective-permute-start.47 = (bf16[1,256,1024]{2,1,0:T(8,128)(2,1)S(1)}, bf16[1,256,1024]{2,1,0:T(8,128)(2,1)S(1)}, u32[]{:S(2)}, u32[]{:S(2)}) collective-permute-start(bf16[1,256,1024]{2,1,0:T(8,128)(2,1)S(1)} %add_convert_fusion), channel_id=1, source_target_pairs={{0,16},{8,24},{16,0},{24,8},{1,17},{9,25},{17,1},{25,9},{2,18},{10... | collective-permute-start | bytes 1572872 | tf_op jit(solution)/shard_map/ppermute | solution.py:117
  198.8 7.4 %collective-permute-start.54 = (bf16[144,1024]{1,0:T(8,128)(2,1)S(1)}, bf16[144,1024]{1,0:T(8,128)(2,1)S(1)}, u32[]{:S(2)}, u32[]{:S(2)}) collective-permute-start(bf16[144,1024]{1,0:T(8,128)(2,1)S(1)} %get-tuple-element.182), channel_id=1, source_target_pairs={{0,2},{2,4},{4,6},{6,7},{7,5},{5,3},{3,1},{1,0},{8,10},{10,12},{12... | collective-permute-start | bytes 884744 | tf_op jit(solution)/shard_map/ppermute | solution.py:93
  199.5 6.7 %collective-permute-start.55 = (bf16[144,1024]{1,0:T(8,128)(2,1)S(1)}, bf16[144,1024]{1,0:T(8,128)(2,1)S(1)}, u32[]{:S(2)}, u32[]{:S(2)}) collective-permute-start(bf16[144,1024]{1,0:T(8,128)(2,1)S(1)} %get-tuple-element.183), channel_id=1, source_target_pairs={{2,0},{4,2},{6,4},{7,6},{5,7},{3,5},{1,3},{0,1},{10,8},{12,10},{14... | collective-permute-start | bytes 884744 | tf_op jit(solution)/shard_map/ppermute | solution.py:95
  204.0 13.8 %copy-start.1 = (bf16[512,1024]{1,0:T(8,128)(2,1)S(1)}, bf16[512,1024]{1,0:T(8,128)(2,1)}, u32[]{:S(2)}) copy-start(bf16[512,1024]{1,0:T(8,128)(2,1)} %param.23) | copy-start | bytes 3145732
  206.9 6.8 %collective-permute-start.57 = (bf16[144,1024]{1,0:T(8,128)(2,1)S(1)}, bf16[144,1024]{1,0:T(8,128)(2,1)S(1)}, u32[]{:S(2)}, u32[]{:S(2)}) collective-permute-start(bf16[144,1024]{1,0:T(8,128)(2,1)S(1)} %shard_map.282.refs_0_), channel_id=1, source_target_pairs={{0,16},{8,24},{16,0},{24,8},{1,17},{9,25},{17,1},{25,9},{2,18},{10... | collective-permute-start | bytes 884744 | tf_op jit(solution)/shard_map/ppermute | solution.py:117
  208.4 5.3 %collective-permute-start.56 = (bf16[144,1024]{1,0:T(8,128)(2,1)S(1)}, bf16[144,1024]{1,0:T(8,128)(2,1)S(1)}, u32[]{:S(2)}, u32[]{:S(2)}) collective-permute-start(bf16[144,1024]{1,0:T(8,128)(2,1)S(1)} %shard_map.282.refs_0_), channel_id=1, source_target_pairs={{0,8},{8,0},{16,24},{24,16},{1,9},{9,1},{17,25},{25,17},{2,10},{10... | collective-permute-start | bytes 884744 | tf_op jit(solution)/shard_map/ppermute | solution.py:117
  213.7 1.6 collective-permute-start.58
  (11 other events, 42.3 us)
